TPU v7x, 32 devices: a whole 2x2x4 slice. The times are simulated.
32 devices in a mesh: dp: 16 (over z, y, x), tensor: 2 (over core).
Axes of the slice: x: 2, y: 2, z: 4, core: 2. Of those that a mesh axis runs over, the one named last changes fastest.
Arguments:
- layer_input: bfloat16 [8192, 2048], P(('dp', 'tensor')), may hold values from -6 to 6
- ln1_gain: bfloat16 [2048], replicated, may hold values from 0.5 to 1.5
- ln1_bias: bfloat16 [2048], replicated, may hold values from -1.1953125 to 1.1953125
- ln2_gain: bfloat16 [2048], replicated, may hold values from 0.5 to 1.5
- ln2_bias: bfloat16 [2048], replicated, may hold values from -1.1953125 to 1.1953125
- qkv_weight: bfloat16 [2048, 6144], P('dp', 'tensor'), may hold values from -0.125 to 0.125
- qkv_bias: bfloat16 [6144], P('tensor'), may hold values from -1.1953125 to 1.1953125
- dense_weight: bfloat16 [2048, 2048], P('tensor', 'dp'), may hold values from -1 to 1
- dense_bias: bfloat16 [2048], replicated, may hold values from -1.1953125 to 1.1953125
- fc1_weight: bfloat16 [2048, 8192], P('dp', 'tensor'), may hold values from -0.125 to 0.125
- fc1_bias: bfloat16 [8192], P('tensor'), may hold values from -1.1953125 to 1.1953125
- fc2_weight: bfloat16 [8192, 2048], P('tensor', 'dp'), may hold values from -0.0625 to 0.0625
- fc2_bias: bfloat16 [2048], replicated, may hold values from -1.1953125 to 1.1953125
- seq_ids: int32 [8192], P('dp'), may hold values from 0 to 2, as said below
- cotangent: bfloat16 [8192, 2048], P(('dp', 'tensor')), may hold values from -6 to 6
Outputs:
- layer_output: bfloat16 [8192, 2048], P(('dp', 'tensor'))
- input_grad: float32 [8192, 2048], P(('dp', 'tensor'))
- ln1_gain_grad: float32 [2048], replicated
- ln1_bias_grad: float32 [2048], replicated
- ln2_gain_grad: float32 [2048], replicated
- ln2_bias_grad: float32 [2048], replicated
- qkv_weight_grad: float32 [2048, 6144], P('dp', 'tensor')
- qkv_bias_grad: float32 [6144], P('tensor')
- dense_weight_grad: float32 [2048, 2048], P('tensor', 'dp')
- dense_bias_grad: float32 [2048], replicated
- fc1_weight_grad: float32 [2048, 8192], P('dp', 'tensor')
- fc1_bias_grad: float32 [8192], P('tensor')
- fc2_weight_grad: float32 [8192, 2048], P('tensor', 'dp')
- fc2_bias_grad: float32 [2048], replicated
Inputs may be any that keep to these rules, and one draw needn't show every extreme that they name: `seq_ids`: within each group of 512 tokens the numbers start at 0 and never fall. A group is either one sequence (all 0) or three sequences of 128, 256 and 128 tokens (0, 1, 2); at least one group has three.
All inputs are finite; a program needn't handle non-finite values.
Results may differ from a plain program's by a relative error of at most 0.0089.
Values may be sent and summed in bfloat16 or wider, within the bound.
A program may use at most 256 MiB of HBM per device.

v0:
```python
import math

import jax
import jax.numpy as jnp
from jax import lax
from jax.sharding import PartitionSpec as P

HEAD_DIM = 256
ROT = 64


def layer_norm(values, gain, shift):
    center = values - jnp.mean(values, axis=-1, keepdims=True)
    spread = jnp.mean(center * center, axis=-1, keepdims=True)
    return center * lax.rsqrt(spread + 1e-05) * gain + shift


def turn_angles(group_ids):
    places = jnp.arange(group_ids.shape[-1], dtype=jnp.int32)
    starts_flag = jnp.concatenate(
        [jnp.ones_like(group_ids[..., :1], dtype=bool), group_ids[..., 1:] != group_ids[..., :-1]],
        axis=-1,
    )
    starts = lax.cummax(jnp.where(starts_flag, places, 0), axis=group_ids.ndim - 1)
    position = (places - starts).astype(jnp.float32)
    steps_rot = jnp.arange(ROT // 2, dtype=jnp.float32)
    inverse = jnp.exp(steps_rot * (-2.0 * math.log(10000.0) / ROT))
    angles = position[..., None] * inverse
    angles = jnp.concatenate([angles, angles], axis=-1)
    return (jnp.cos(angles), jnp.sin(angles))


def rotary(vectors, cosine_table, sine_table):
    half_rot = ROT // 2
    rot_part = vectors[..., :ROT]
    rot_rest = vectors[..., ROT:]
    turned = jnp.concatenate([-rot_part[..., half_rot:], rot_part[..., :half_rot]], axis=-1)
    rotated = rot_part * cosine_table[:, None, :] + turned * sine_table[:, None, :]
    return jnp.concatenate([rotated, rot_rest], axis=-1)


def gelu_exact(values):
    return jax.nn.gelu(values, approximate=False)


def both_norms(values, gain_attn, shift_attn, gain_ffn, shift_ffn):
    return (layer_norm(values, gain_attn, shift_attn), layer_norm(values, gain_ffn, shift_ffn))


def local(
    layer_input,
    ln1_gain,
    ln1_bias,
    ln2_gain,
    ln2_bias,
    qkv_weight,
    qkv_bias,
    dense_weight,
    dense_bias,
    fc1_weight,
    fc1_bias,
    fc2_weight,
    fc2_bias,
    seq_ids,
    cotangent,
):
    group_len = seq_ids.shape[0]
    norm_params = (
        ln1_gain.astype(jnp.float32),
        ln1_bias.astype(jnp.float32),
        ln2_gain.astype(jnp.float32),
        ln2_bias.astype(jnp.float32),
    )
    input_rows = layer_input.astype(jnp.float32)
    own_attn, own_ffn = both_norms(input_rows, *norm_params)
    normed_attn, normed_ffn = (
        lax.all_gather(own_attn.astype(jnp.bfloat16), "tensor", axis=0, tiled=True),
        lax.all_gather(own_ffn.astype(jnp.bfloat16), "tensor", axis=0, tiled=True),
    )
    width_qkv = qkv_weight.shape[1]
    heads_here = width_qkv // (3 * HEAD_DIM)
    contract_last = (((1,), (1,)), ((), ()))
    contract_first = (((0,), (0,)), ((), ()))
    pieces = (
        lax.all_gather(qkv_weight, "dp", axis=0, tiled=True),
        lax.all_gather(fc1_weight, "dp", axis=0, tiled=True),
    )
    qkv_pre = jnp.dot(normed_attn, pieces[0], preferred_element_type=jnp.float32)
    ffn_pre = jnp.dot(normed_ffn, pieces[1], preferred_element_type=jnp.float32)
    qkv_full = (qkv_pre + qkv_bias.astype(jnp.float32)).reshape(group_len, heads_here, 3, HEAD_DIM)
    cosine_table, sine_table = turn_angles(seq_ids)
    query_pre = qkv_full[:, :, 0]
    keys_pre = qkv_full[:, :, 1]
    query = rotary(query_pre, cosine_table, sine_table).astype(jnp.bfloat16)
    keys = rotary(keys_pre, cosine_table, sine_table).astype(jnp.bfloat16)
    values = qkv_full[:, :, 2].astype(jnp.bfloat16)
    ffn_input = ffn_pre + fc1_bias.astype(jnp.float32)
    hidden = gelu_exact(ffn_input).astype(jnp.bfloat16)
    block_len = min(group_len, 512)
    block_count = group_len // block_len
    places = jnp.arange(group_len, dtype=jnp.int32)

    def block_scores(offset):
        row_places = offset + jnp.arange(block_len, dtype=jnp.int32)
        allowed = (seq_ids[:, None] == seq_ids[None, :]) & (places[None, :] <= row_places[:, None])
        raw_scores = (
            jnp.einsum("qhd,khd->hqk", query, keys, preferred_element_type=jnp.float32) * 0.0625
        )
        return (query, jnp.where(allowed[None], raw_scores, -1e30))

    def attend(number):
        query_rows, scores = block_scores(number * block_len)
        highest = jnp.max(scores, axis=-1, keepdims=True)
        weights = jnp.exp(scores - highest)
        denominator = jnp.sum(weights, axis=-1, keepdims=True)
        probability = (weights / denominator).astype(jnp.bfloat16)
        block_out = jnp.einsum(
            "hqk,khd->qhd", probability, values, preferred_element_type=jnp.float32
        )
        return (block_out.astype(jnp.bfloat16), highest + jnp.log(denominator))

    attended_blocks, log_total = lax.map(attend, jnp.arange(block_count, dtype=jnp.int32))
    attended = attended_blocks.reshape(group_len, heads_here * HEAD_DIM)
    pieces = lax.all_gather((dense_weight, fc2_weight), "dp", axis=1, tiled=True)
    partial_branch = jnp.dot(attended, pieces[0], preferred_element_type=jnp.float32) + jnp.dot(
        hidden, pieces[1], preferred_element_type=jnp.float32
    )
    branch = lax.psum_scatter(partial_branch, "tensor", scatter_dimension=0, tiled=True)
    layer_output = (
        input_rows + branch + dense_bias.astype(jnp.float32) + fc2_bias.astype(jnp.float32)
    ).astype(jnp.bfloat16)
    cot_rows = cotangent.astype(jnp.float32)
    cot_group = lax.all_gather(cotangent, "tensor", axis=0, tiled=True)
    pieces = (
        lax.all_gather(dense_weight, "dp", axis=1, tiled=True),
        lax.all_gather(fc2_weight, "dp", axis=1, tiled=True),
    )
    grad_attended_sum = lax.dot_general(
        cot_group, pieces[0], contract_last, preferred_element_type=jnp.float32
    )
    grad_hidden = lax.dot_general(
        cot_group, pieces[1], contract_last, preferred_element_type=jnp.float32
    )
    grad_dense = lax.dot_general(
        attended, cot_group, contract_first, preferred_element_type=jnp.float32
    )
    grad_fc2 = lax.dot_general(
        hidden, cot_group, contract_first, preferred_element_type=jnp.float32
    )
    grad_ffn = jax.vjp(gelu_exact, ffn_input)[1](grad_hidden)[0].astype(jnp.bfloat16)
    grad_attended = grad_attended_sum.astype(jnp.bfloat16).reshape(group_len, heads_here, HEAD_DIM)

    def back_block(carry, packed):
        number, log_rows = packed
        offset = number * block_len
        query_rows, scores = block_scores(offset)
        probability = jnp.exp(scores - log_rows)
        grad_prob = jnp.einsum(
            "qhd,khd->hqk", grad_attended, values, preferred_element_type=jnp.float32
        )
        row_dot = jnp.sum(probability * grad_prob, axis=-1, keepdims=True)
        grad_scores = (probability * (grad_prob - row_dot)).astype(jnp.bfloat16)
        grad_query_rows = (
            jnp.einsum("hqk,khd->qhd", grad_scores, keys, preferred_element_type=jnp.float32)
            * 0.0625
        )
        grad_keys = (
            carry[0]
            + jnp.einsum(
                "hqk,qhd->khd", grad_scores, query_rows, preferred_element_type=jnp.float32
            )
            * 0.0625
        )
        grad_values = carry[1] + jnp.einsum(
            "hqk,qhd->khd",
            probability.astype(jnp.bfloat16),
            grad_attended,
            preferred_element_type=jnp.float32,
        )
        return ((grad_keys, grad_values), grad_query_rows)

    empty_heads = jnp.zeros((group_len, heads_here, HEAD_DIM), jnp.float32)
    (grad_keys, grad_values), grad_query_blocks = lax.scan(
        back_block,
        (empty_heads, empty_heads),
        (jnp.arange(block_count, dtype=jnp.int32), log_total),
    )
    grad_query = grad_query_blocks.reshape(group_len, heads_here, HEAD_DIM)
    turn_back = jax.vjp(
        lambda former, latter: (
            rotary(former, cosine_table, sine_table),
            rotary(latter, cosine_table, sine_table),
        ),
        query_pre,
        keys_pre,
    )[1]
    grad_query_pre, grad_keys_pre = turn_back((grad_query, grad_keys))
    qkv_grad = (
        jnp.stack([grad_query_pre, grad_keys_pre, grad_values], axis=2)
        .reshape(group_len, width_qkv)
        .astype(jnp.bfloat16)
    )
    pieces = lax.all_gather((qkv_weight, fc1_weight), "dp", axis=0, tiled=True)
    attn_part = lax.dot_general(
        qkv_grad, pieces[0], contract_last, preferred_element_type=jnp.float32
    )
    ffn_part = lax.dot_general(
        grad_ffn, pieces[1], contract_last, preferred_element_type=jnp.float32
    )
    grad_normed = jnp.stack([attn_part, ffn_part], axis=0)
    grad_norm_attn, grad_norm_ffn = (
        lax.psum_scatter(grad_normed[0], "tensor", scatter_dimension=0, tiled=True),
        lax.psum_scatter(grad_normed[1], "tensor", scatter_dimension=0, tiled=True),
    )
    norm_pullback = jax.vjp(both_norms, input_rows, *norm_params)[1]
    grad_rows_in, grad_gain_attn, grad_shift_attn, grad_gain_ffn, grad_shift_ffn = norm_pullback(
        (grad_norm_attn, grad_norm_ffn)
    )
    input_grad = cot_rows + grad_rows_in
    small_sums = lax.psum(
        (grad_gain_attn, grad_shift_attn, grad_gain_ffn, grad_shift_ffn, jnp.sum(cot_rows, axis=0)),
        ("dp", "tensor"),
    )
    column_sums = lax.psum(
        (
            jnp.sum(qkv_grad.astype(jnp.float32), axis=0),
            jnp.sum(grad_ffn.astype(jnp.float32), axis=0),
        ),
        "dp",
    )
    grad_qkv = lax.dot_general(
        normed_attn, qkv_grad, contract_first, preferred_element_type=jnp.float32
    )
    grad_fc1 = lax.dot_general(
        normed_ffn, grad_ffn, contract_first, preferred_element_type=jnp.float32
    )
    grad_qkv, grad_fc1, grad_dense, grad_fc2 = (
        lax.psum_scatter(grad_qkv, "dp", scatter_dimension=0, tiled=True),
        lax.psum_scatter(grad_fc1, "dp", scatter_dimension=0, tiled=True),
        lax.psum_scatter(grad_dense, "dp", scatter_dimension=1, tiled=True),
        lax.psum_scatter(grad_fc2, "dp", scatter_dimension=1, tiled=True),
    )
    return (
        layer_output,
        input_grad,
        small_sums[0],
        small_sums[1],
        small_sums[2],
        small_sums[3],
        grad_qkv,
        column_sums[0],
        grad_dense,
        small_sums[4],
        grad_fc1,
        column_sums[1],
        grad_fc2,
        small_sums[4],
    )


def solution(mesh):
    in_specs = (
        P(("dp", "tensor"), None),
        P(),
        P(),
        P(),
        P(),
        P("dp", "tensor"),
        P("tensor"),
        P("tensor", "dp"),
        P(),
        P("dp", "tensor"),
        P("tensor"),
        P("tensor", "dp"),
        P(),
        P("dp"),
        P(("dp", "tensor"), None),
    )
    out_specs = (
        P(("dp", "tensor"), None),
        P(("dp", "tensor"), None),
        P(),
        P(),
        P(),
        P(),
        P("dp", "tensor"),
        P("tensor"),
        P("tensor", "dp"),
        P(),
        P("dp", "tensor"),
        P("tensor"),
        P("tensor", "dp"),
        P(),
    )
    return jax.shard_map(local, mesh=mesh, in_specs=in_specs, out_specs=out_specs, check_vma=False)
```

profile of v0, /device:TPU:0, one launch (start us, length us, event | category | flops | bytes accessed | tf_op | source)
XLA Modules:
  0.0 2774.3 jit_solution(17852173725813281113)
XLA Ops:
  7.2 0.7 all-gather.20.cloned.1.call-update
  8.0 0.7 all-gather.12.cloned.1.call-update
  8.7 0.7 convert_element_type.95
  9.4 0.7 convert_element_type.104
  10.1 0.7 convert_element_type.96
  10.8 0.7 convert_element_type.105
  11.5 1.4 convert_reduce_fusion.2
  13.0 1.6 fusion.24
  15.2 2.1 fusion.21
  19.1 0.7 all-gather.18.cloned.1.call-update
  20.8 1.8 fusion.48
  22.6 0.9 fusion.43
  23.5 92.5 %all-gather.12.cloned.1.call-done = bf16[1024,2048]{1,0:T(8,128)(2,1)} async-done(((bf16[1024,128]{1,0:T(8,128)(2,1)}), bf16[1024,2048]{1,0:T(8,128)(2,1)}) %all-gather.12.cloned.1.call-update) | async-done | bytes 4194320 | tf_op jit(solution)/shard_map/all_gather | solution.py:124
  116.0 5.2 convolution_convert_fusion
  121.7 5.2 all-gather.8.cloned.1.call-done
  126.9 155.8 %all-gather.10.cloned.1.call-done = bf16[2048,3072]{1,0:T(8,128)(2,1)} async-done(((bf16[128,3072]{1,0:T(8,128)(2,1)}), bf16[2048,3072]{1,0:T(8,128)(2,1)}) %all-gather.10.cloned.1.call-update) | async-done | bytes 12582928 | tf_op jit(solution)/shard_map/all_gather | solution.py:85
  282.7 11.9 convolution_add_fusion
  294.7 6.5 copy.61
  301.2 4.7 fusion.59
  305.9 2.1 copy.89
  308.0 1.3 slice.97
  309.3 3.4 copy.90
  312.7 2.0 slice.96
  314.7 2.4 slice_negate_fusion.2
  317.2 0.8 fusion.42
  318.4 1.6 fusion.62
  320.7 1.0 copy-done.20
  321.7 2.6 multiply_reduce_fusion
  324.3 1.2 multiply_convert_fusion.1
  325.5 1.2 multiply_bitcast_fusion.1
  327.4 0.8 multiply_bitcast_fusion
  329.7 0.7 pad_add_fusion.1
  331.4 0.9 fusion.34
  332.4 1.3 convert_reduce_fusion.1
  333.7 2.8 copy.77
  336.5 12.9 fusion.66
  349.5 139.5 %all-gather.16.cloned.1.call-done = bf16[2048,4096]{1,0:T(8,128)(2,1)} async-done(((bf16[128,4096]{1,0:T(8,128)(2,1)}), bf16[2048,4096]{1,0:T(8,128)(2,1)}) %all-gather.16.cloned.1.call-update) | async-done | bytes 16777232 | tf_op jit(solution)/shard_map/all_gather | solution.py:86
  489.0 14.9 fusion.64
  503.9 235.7 %all-gather.18.cloned.1.call-done = bf16[4096,2048]{1,0:T(8,128)(2,1)} async-done(((bf16[4096,128]{1,0:T(8,128)(2,1)}), bf16[4096,2048]{1,0:T(8,128)(2,1)}) %all-gather.18.cloned.1.call-update) | async-done | bytes 16777232 | tf_op jit(solution)/shard_map/all_gather | solution.py:124
  739.5 32.3 %convert_reduce_fusion = (f32[4096]{0:T(1024)S(1)}, bf16[512,4096]{1,0:T(8,128)(2,1)S(1)}, f32[512,4096]{1,0:T(8,128)}) fusion(f32[512,4096]{1,0:T(8,128)} %fusion.64, f32[4096]{0:T(1024)S(1)} %convert_element_type.107, bf16[512,2048]{1,0:T(8,128)(2,1)S(1)} %copy-done.32, bf16[4096,2048]{1,0:T(8,128)(2,1)} %all-gather.18.cloned.1.call-done), kind=kOutput, calls=%fused_computation.2 | convolution fusion | flops 8747216896 | bytes 39878656 | tf_op jit(solution)/shard_map/dot_general | solution.py:141
  771.8 1.9 copy-done.35
  773.8 13.9 fusion.65
  787.8 0.6 copy-done.19
  788.4 3.9 fusion.37
  792.9 2.5 fusion.63
  795.4 10.3 multiply_convert_fusion
  805.8 15.3 convolution_add_fusion.1
  821.1 8.3 fusion.68
  829.5 2.0 copy-done.8
  831.5 13.8 fusion.67
  845.4 1.5 copy-done.33
  846.9 17.7 fusion.70
  864.7 1.5 copy-done.34
  866.3 17.7 fusion.69
  884.0 0.6 copy-done.30
  884.7 75.1 %all-reduce.9 = (f32[3072]{0:T(1024)}, f32[4096]{0:T(1024)}) all-reduce(f32[3072]{0:T(1024)S(1)} %reduce_sum.163, f32[4096]{0:T(1024)S(1)} %get-tuple-element.88), channel_id=1, replica_groups=mesh['dp'=16,'tensor'=2] {'dp'}, use_global_device_ids=true, to_apply=%region_24.25 | all-reduce | flops 7168 | bytes 57344 | tf_op jit(solution)/shard_map/psum | solution.py:224
  959.9 3.2 fusion.57
  963.3 1.7 fusion.23
  965.1 5.1 convert_reduce_fusion.3
  970.2 42.3 %all-reduce.8 = (f32[2048]{0:T(1024)}, f32[2048]{0:T(1024)}, f32[2048]{0:T(1024)}, f32[2048]{0:T(1024)}, f32[2048]{0:T(1024)S(1)}) all-reduce(f32[2048]{0:T(1024)S(1)} %get-tuple-element.80, f32[2048]{0:T(1024)S(1)} %get-tuple-element.77, f32[2048]{0:T(1024)S(1)} %get-tuple-element.60, ...), channel_id=1, replica_groups=mesh['dp'=16,'tensor'=2] {'dp','tensor'}, use_global_device_ids=true, to_apply=%region_15.16 | all-reduce | flops 10240 | bytes 81920 | tf_op jit(solution)/shard_map/psum | solution.py:220
  1012.4 5.8 reduce-scatter.16.cloned.1.call-done
  1018.3 371.2 %reduce-scatter.14.cloned.1.call-done = f32[128,3072]{1,0:T(8,128)} async-done(((f32[2048,3072]{1,0:T(8,128)}), f32[128,3072]{1,0:T(8,128)}) %reduce-scatter.14.cloned.1.call-update) | async-done | bytes 1572880 | tf_op jit(solution)/shard_map/reduce_scatter | solution.py:238
  1389.4 685.5 %reduce-scatter.20.cloned.1.call-done = f32[4096,128]{1,0:T(8,128)} async-done(((f32[4096,2048]{1,0:T(8,128)}), f32[4096,128]{1,0:T(8,128)}) %reduce-scatter.20.cloned.1.call-update) | async-done | bytes 2097168 | tf_op jit(solution)/shard_map/reduce_scatter | solution.py:241
  2074.9 692.0 %reduce-scatter.18.cloned.1.call-done = f32[128,4096]{1,0:T(8,128)} async-done(((f32[2048,4096]{1,0:T(8,128)}), f32[128,4096]{1,0:T(8,128)}) %reduce-scatter.18.cloned.1.call-update) | async-done | bytes 2097168 | tf_op jit(solution)/shard_map/reduce_scatter | solution.py:239
  (127 shorter events, 10.1 us)
Async XLA Ops:
  7.2 8.0 copy-start.1
  7.2 16.3 all-gather.20.cloned.1.call-start
  7.9 108.0 %all-gather.12.cloned.1.call-start = ((), (), s32[]{:S(2)}) async-start(), calls=%async_computation.9 | async-start | bytes 4456448 | tf_op jit(solution)/shard_map/all_gather | solution.py:124
  8.7 118.2 %all-gather.8.cloned.1.call-start = ((), (), s32[]{:S(2)}) async-start(), calls=%async_computation.7 | async-start | bytes 3145728 | tf_op jit(solution)/shard_map/all_gather | solution.py:77
  9.4 7.9 copy-start.11
  10.1 7.2 copy-start.13
  12.9 4.3 copy-start.16
  14.6 0.6 copy-start.25
  15.2 4.7 copy-start.22
  15.2 5.3 copy-start.29
  15.2 5.3 copy-start.27
  15.2 2.1 copy-start.23
  17.3 265.4 %all-gather.10.cloned.1.call-start = ((), (), s32[]{:S(2)}) async-start(), calls=%async_computation.8 | async-start | bytes 13369344 | tf_op jit(solution)/shard_map/all_gather | solution.py:85
  17.9 331.6 %all-gather.14.cloned.1.call-start = ((), (), s32[]{:S(2)}) async-start(), calls=%async_computation.10 | async-start | bytes 3145728 | tf_op jit(solution)/shard_map/all_gather | solution.py:78
  18.5 470.5 %all-gather.16.cloned.1.call-start = ((), (), s32[]{:S(2)}) async-start(), calls=%async_computation.11 | async-start | bytes 17825792 | tf_op jit(solution)/shard_map/all_gather | solution.py:86
  19.1 720.4 %all-gather.18.cloned.1.call-start = ((), (), s32[]{:S(2)}) async-start(), calls=%async_computation.12 | async-start | bytes 17825792 | tf_op jit(solution)/shard_map/all_gather | solution.py:124
  19.8 940.0 %reduce-scatter.12.cloned.1.call-start = ((), (), s32[]{:S(2)}) async-start(), calls=%async_computation.16 | async-start | bytes 6291456 | tf_op jit(solution)/shard_map/reduce_scatter | solution.py:212
  314.7 2.5 copy-start.5
  314.7 2.5 copy-start.9
  317.1 1.2 copy-start.7
  317.2 1.3 copy-start.10
  320.0 4.3 copy-start.18
  320.0 11.4 copy-start
  320.6 1.1 copy-start.20
  349.4 390.1 %copy-start.32 = (bf16[512,2048]{1,0:T(8,128)(2,1)S(1)}, bf16[512,2048]{1,0:T(8,128)(2,1)}, u32[]{:S(2)}) copy-start(bf16[512,2048]{1,0:T(8,128)(2,1)} %all-gather.20.cloned.1.call-done) | copy-start | bytes 6291460
  349.4 610.4 %reduce-scatter.10.cloned.1.call-start = ((), (), s32[]{:S(2)}) async-start(), calls=%async_computation.15 | async-start | bytes 6291456 | tf_op jit(solution)/shard_map/reduce_scatter | solution.py:213
  771.8 1.9 copy-start.35
  787.7 0.7 copy-start.19
  787.7 0.7 copy-start.21
  787.7 177.3 %reduce-scatter.8.cloned.1.call-start = ((), (), s32[]{:S(2)}) async-start(), calls=%async_computation.13 | async-start | bytes 6291456 | tf_op jit(solution)/shard_map/reduce_scatter | solution.py:128
  788.4 4.5 copy-start.6
  821.1 197.2 %reduce-scatter.16.cloned.1.call-start = ((), (), s32[]{:S(2)}) async-start(), calls=%async_computation.18 | async-start | bytes 8912896 | tf_op jit(solution)/shard_map/reduce_scatter | solution.py:240
  829.4 2.1 copy-start.8
  829.4 560.0 %reduce-scatter.14.cloned.1.call-start = ((), (), s32[]{:S(2)}) async-start(), calls=%async_computation.17 | async-start | bytes 26738688 | tf_op jit(solution)/shard_map/reduce_scatter | solution.py:238
  845.3 1.6 copy-start.33
  845.4 1229.6 %reduce-scatter.20.cloned.1.call-start = ((), (), s32[]{:S(2)}) async-start(), calls=%async_computation.20 | async-start | bytes 35651584 | tf_op jit(solution)/shard_map/reduce_scatter | solution.py:241
  864.7 1.6 copy-start.34
  864.7 1902.2 %reduce-scatter.18.cloned.1.call-start = ((), (), s32[]{:S(2)}) async-start(), calls=%async_computation.19 | async-start | bytes 35651584 | tf_op jit(solution)/shard_map/reduce_scatter | solution.py:239
  883.9 0.7 copy-start.30
  883.9 0.7 copy-start.31
  883.9 0.7 copy-start.15
  883.9 75.9 %copy-start.2 = (bf16[256,2048]{1,0:T(8,128)(2,1)S(1)}, bf16[256,2048]{1,0:T(8,128)(2,1)}, u32[]{:S(2)}) copy-start(bf16[256,2048]{1,0:T(8,128)(2,1)} %param.15) | copy-start | bytes 3145732
  883.9 75.9 %copy-start.12 = (f32[2048]{0:T(1024)S(1)}, f32[2048]{0:T(1024)}, u32[]{:S(2)}) copy-start(f32[2048]{0:T(1024)} %copy-done.11) | copy-start | bytes 24580
  883.9 75.9 %copy-start.14 = (f32[2048]{0:T(1024)S(1)}, f32[2048]{0:T(1024)}, u32[]{:S(2)}) copy-start(f32[2048]{0:T(1024)} %copy-done.13) | copy-start | bytes 24580
  884.0 75.9 %copy-start.17 = (f32[256]{0:T(256)S(1)}, f32[256]{0:T(256)}, u32[]{:S(2)}) copy-start(f32[256]{0:T(256)} %copy-done.16) | copy-start | bytes 3076
  884.6 78.5 %copy-start.26 = (f32[256]{0:T(256)S(1)}, f32[256]{0:T(256)}, u32[]{:S(2)}) copy-start(f32[256]{0:T(256)} %copy-done.25) | copy-start | bytes 3076
  884.6 78.5 %copy-start.24 = (f32[256]{0:T(256)S(1)}, f32[256]{0:T(256)}, u32[]{:S(2)}) copy-start(f32[256]{0:T(256)} %copy-done.23) | copy-start | bytes 3076
  959.8 3.3 copy-start.3
  959.8 3.5 copy-start.4
  1012.4 1755.1 %copy-start.28 = (f32[2048]{0:T(1024)}, f32[2048]{0:T(1024)S(1)}, u32[]{:S(2)}) copy-start(f32[2048]{0:T(1024)S(1)} %get-tuple-element.153) | copy-start | bytes 24580
Sparse Core Ops, SparseCore 0:
  9.6 13.2 all-gather.19
  25.6 90.3 all-gather.11
  118.1 8.7 all-gather.7
  129.5 153.1 all-gather.9
  284.7 8.7 all-gather.13
  296.1 192.7 all-gather.15
  491.7 247.8 all-gather.17
  741.8 10.2 reduce-scatter.11
  787.9 10.2 reduce-scatter.9
  821.2 10.7 reduce-scatter.7
  834.9 183.2 reduce-scatter.15
  1025.4 363.9 reduce-scatter.13
  1392.5 682.3 reduce-scatter.19
  2077.8 689.0 reduce-scatter.17
where the time goes:
time: 2790 us; the launch traced here: 2770 us
  waiting for transfers between devices  2390 us (86%)
  matrix products  178 us (6%)
  blocking collectives  117 us (4%)
  other arithmetic  40.6 us (1%)
  local copies, waits for them, and re-layouts  36.6 us (1%)
    reduce_scatter x1, waiting for transfers between devices, local(): lax.psum_scatter(grad_fc1, 'dp', scatter_dimension=0, tiled=True)  692 us
    reduce_scatter x1, waiting for transfers between devices, local(): lax.psum_scatter(grad_fc2, 'dp', scatter_dimension=1, tiled=True)  685 us
    reduce_scatter x1, waiting for transfers between devices, local(): lax.psum_scatter(grad_qkv, 'dp', scatter_dimension=0, tiled=True)  371 us
    all_gather x2, waiting for transfers between devices, local(): lax.all_gather((dense_weight, fc2_weight), 'dp', axis=1, tiled=True)  328 us
    all_gather x1, waiting for transfers between devices, local(): lax.all_gather(qkv_weight, 'dp', axis=0, tiled=True)  156 us
    all_gather x1, waiting for transfers between devices, local(): lax.all_gather(fc1_weight, 'dp', axis=0, tiled=True)  139 us
    psum x1, blocking collectives, local(): lax.psum((jnp.sum(qkv_grad.astype(jnp.float32), axis=0), jnp.sum(grad_ffn...  75.1 us
  transfers between devices with their start and end apart: 14, of which 9 were waited for; matrix products, arithmetic and copies ran while one was open for 9% of the time, Pallas kernels for 0%

commit v1 on v0

v1 whole, which is shorter than its diff:
```python
import math

import jax
import jax.numpy as jnp
from jax import lax
from jax.sharding import PartitionSpec as P

HEAD_DIM = 256
ROT = 64
BIT_X, BIT_Y, BIT_ZL, FIRST_ZH = 0, 1, 2, 3
F32, BF16 = jnp.float32, jnp.bfloat16
NN = (((1,), (0,)), ((), ()))
NT = (((1,), (1,)), ((), ()))
TN = (((0,), (0,)), ((), ()))


def mm(a, b, dims):
    return lax.dot_general(a, b, dims, preferred_element_type=F32)


def turn_angles(group_ids):
    places = jnp.arange(group_ids.shape[-1], dtype=jnp.int32)
    starts_flag = jnp.concatenate(
        [jnp.ones_like(group_ids[..., :1], dtype=bool), group_ids[..., 1:] != group_ids[..., :-1]],
        axis=-1,
    )
    starts = lax.cummax(jnp.where(starts_flag, places, 0), axis=group_ids.ndim - 1)
    position = (places - starts).astype(F32)
    steps_rot = jnp.arange(ROT // 2, dtype=F32)
    inverse = jnp.exp(steps_rot * (-2.0 * math.log(10000.0) / ROT))
    angles = position[..., None] * inverse
    angles = jnp.concatenate([angles, angles], axis=-1)
    return (jnp.cos(angles), jnp.sin(angles))


def rotary(vectors, cosine_table, sine_table):
    half_rot = ROT // 2
    rot_part = vectors[..., :ROT]
    rot_rest = vectors[..., ROT:]
    turned = jnp.concatenate([-rot_part[..., half_rot:], rot_part[..., :half_rot]], axis=-1)
    rotated = rot_part * cosine_table + turned * sine_table
    return jnp.concatenate([rotated, rot_rest], axis=-1)


def rotary_back(vectors, cosine_table, sine_table):
    half_rot = ROT // 2
    rot_part = vectors[..., :ROT]
    rot_rest = vectors[..., ROT:]
    turned = jnp.concatenate([rot_part[..., half_rot:], -rot_part[..., :half_rot]], axis=-1)
    rotated = rot_part * cosine_table + turned * sine_table
    return jnp.concatenate([rotated, rot_rest], axis=-1)


def local(
    layer_input,
    ln1_gain,
    ln1_bias,
    ln2_gain,
    ln2_bias,
    qkv_weight,
    qkv_bias,
    dense_weight,
    dense_bias,
    fc1_weight,
    fc1_bias,
    fc2_weight,
    fc2_bias,
    seq_ids,
    cotangent,
):
    n = lax.axis_size("dp")
    bits = n.bit_length() - 1
    me = lax.axis_index("dp")
    core = lax.axis_index("tensor")
    bit = [(me >> k) & 1 for k in range(bits)]
    zh_bits = tuple(range(FIRST_ZH, bits))
    rows_here, d_model = layer_input.shape
    feature = 2 * bit[BIT_ZL] + bit[BIT_X]

    def swap(v, k):
        return lax.ppermute(v, "dp", [(i, i ^ (1 << k)) for i in range(n)])

    def swap_core(v):
        return lax.ppermute(v, "tensor", [(0, 1), (1, 0)])

    def pick(v, b, axis):
        return lax.dynamic_index_in_dim(v, b, axis, keepdims=False)

    def ordered(b, own, other, axis):
        return jnp.stack(
            [jnp.where(b == 0, own, other), jnp.where(b == 0, other, own)], axis=axis
        )

    def gather_rows(v):
        v = jnp.stack([v, swap(v, BIT_ZL)], axis=0)
        v = jnp.concatenate([v, swap(v, BIT_X)], axis=0)
        return v

    def gather_tokens(v):
        v = gather_rows(v)
        return ordered(core, v, swap_core(v), 1).reshape(4 * 2 * rows_here, d_model)

    def scatter_tokens(v):
        v = v.reshape(4, 2, rows_here, d_model)
        keep = pick(v, core, 1)
        v = keep + swap_core(pick(v, 1 - core, 1).astype(BF16))
        v = v[:2] + swap(v[2:].astype(BF16), BIT_X)
        return v[0] + swap(v[1].astype(BF16), BIT_ZL)

    def gather_weight(w):
        rows, width = w.shape
        w = w.reshape(rows, 2, 2, width // 4)
        w = ordered(bit[BIT_X], pick(w, bit[BIT_X], 2), swap(pick(w, 1 - bit[BIT_X], 2), BIT_X), 0)
        w = ordered(bit[BIT_ZL], pick(w, bit[BIT_ZL], 2), swap(pick(w, 1 - bit[BIT_ZL], 2), BIT_ZL), 0)
        for k in zh_bits:
            w = ordered(bit[k], w, swap(w, k), 0)
        w = ordered(bit[BIT_Y], w, swap(w, BIT_Y), w.ndim - 3)
        return w.reshape(rows * n, width // 4)

    def scatter_grad(g):
        rows, width = g.shape[0] // n, g.shape[1]
        g = g.reshape((2,) * bits + (rows, width))
        axis = bits - 1 - BIT_Y
        g = pick(g, bit[BIT_Y], axis) + swap(pick(g, 1 - bit[BIT_Y], axis).astype(BF16), BIT_Y)
        for k in reversed(zh_bits):
            g = pick(g, bit[k], 0) + swap(pick(g, 1 - bit[k], 0).astype(BF16), k)
        g = g.astype(BF16)
        g = ordered(bit[BIT_ZL], pick(g, bit[BIT_ZL], 0), swap(pick(g, 1 - bit[BIT_ZL], 0), BIT_ZL), 2)
        g = ordered(bit[BIT_X], pick(g, bit[BIT_X], 0), swap(pick(g, 1 - bit[BIT_X], 0), BIT_X), 2)
        return g.reshape(rows, 4 * width).astype(F32)

    def take_block(v, parts):
        return lax.dynamic_slice_in_dim(v, feature * (v.shape[0] // parts), v.shape[0] // parts, 0)

    gains = [v.astype(F32) for v in (ln1_gain, ln1_bias, ln2_gain, ln2_bias)]

    rows_in = gather_tokens(layer_input)
    w_fc1 = gather_weight(fc1_weight)
    cot = gather_tokens(cotangent)
    w_fc2 = gather_weight(fc2_weight.T)
    w_qkv = gather_weight(qkv_weight)
    w_dense = gather_weight(dense_weight.T)
    ids = gather_rows(seq_ids)
    group_len = seq_ids.shape[0]

    def normalize(v):
        v = v.astype(F32)
        center = v - jnp.mean(v, axis=-1, keepdims=True)
        spread = jnp.mean(center * center, axis=-1, keepdims=True)
        scale = lax.rsqrt(spread + 1e-05)
        return center * scale, scale

    xhat, _ = normalize(rows_in)
    normed_attn = (xhat * gains[0] + gains[1]).astype(BF16)
    normed_ffn = (xhat * gains[2] + gains[3]).astype(BF16)

    ffn_input = mm(normed_ffn, w_fc1, NN) + take_block(fc1_bias, 4).astype(F32)
    cdf = 0.5 * (1.0 + lax.erf(ffn_input * (1.0 / math.sqrt(2.0))))
    density = jnp.exp(-0.5 * ffn_input * ffn_input) * (1.0 / math.sqrt(2.0 * math.pi))
    hidden = (ffn_input * cdf).astype(BF16)
    slope = cdf + ffn_input * density
    grad_fc2 = mm(cot, hidden, TN)
    out_fc2 = scatter_grad(grad_fc2).T

    grad_ffn = (mm(cot, w_fc2, NN) * slope).astype(BF16)
    grad_fc1 = mm(normed_ffn, grad_ffn, TN)
    out_fc1 = scatter_grad(grad_fc1)

    qkv = mm(normed_attn, w_qkv, NN) + take_block(qkv_bias, 4).astype(F32)
    qkv = qkv.reshape(4, group_len, 3, HEAD_DIM)
    cosines, sines = turn_angles(ids)
    query = rotary(qkv[:, :, 0], cosines, sines).astype(BF16)
    keys = rotary(qkv[:, :, 1], cosines, sines).astype(BF16)
    values = qkv[:, :, 2].astype(BF16)
    places = jnp.arange(group_len, dtype=jnp.int32)
    allowed = (ids[:, :, None] == ids[:, None, :]) & (places[None, None, :] <= places[None, :, None])
    scores = jnp.einsum("gqd,gkd->gqk", query, keys, preferred_element_type=F32) * 0.0625
    scores = jnp.where(allowed, scores, -1e30)
    weights = jnp.exp(scores - jnp.max(scores, axis=-1, keepdims=True))
    probability = weights / jnp.sum(weights, axis=-1, keepdims=True)
    prob_low = probability.astype(BF16)
    attended = jnp.einsum("gqk,gkd->gqd", prob_low, values, preferred_element_type=F32)
    attended = attended.astype(BF16).reshape(-1, HEAD_DIM)

    partial = mm(attended, w_dense, NT) + mm(hidden, w_fc2, NT)
    branch = scatter_tokens(partial)
    layer_output = (
        layer_input.astype(F32) + branch + dense_bias.astype(F32) + fc2_bias.astype(F32)
    ).astype(BF16)

    grad_dense = mm(cot, attended, TN)
    grad_attended = mm(cot, w_dense, NN).astype(BF16).reshape(4, group_len, HEAD_DIM)
    grad_prob = jnp.einsum("gqd,gkd->gqk", grad_attended, values, preferred_element_type=F32)
    row_dot = jnp.sum(probability * grad_prob, axis=-1, keepdims=True)
    grad_scores = (probability * (grad_prob - row_dot)).astype(BF16)
    grad_query = jnp.einsum("gqk,gkd->gqd", grad_scores, keys, preferred_element_type=F32) * 0.0625
    grad_keys = jnp.einsum("gqk,gqd->gkd", grad_scores, query, preferred_element_type=F32) * 0.0625
    grad_values = jnp.einsum("gqk,gqd->gkd", prob_low, grad_attended, preferred_element_type=F32)
    qkv_grad = jnp.concatenate(
        [
            rotary_back(grad_query, cosines, sines).astype(BF16),
            rotary_back(grad_keys, cosines, sines).astype(BF16),
            grad_values.astype(BF16),
        ],
        axis=-1,
    ).reshape(-1, 3 * HEAD_DIM)
    out_qkv = scatter_grad(mm(normed_attn, qkv_grad, TN))
    out_dense = scatter_grad(grad_dense).T

    attn_part = mm(qkv_grad, w_qkv, NT)
    ffn_part = mm(grad_ffn, w_fc1, NT)
    e_rows = scatter_tokens(attn_part * gains[0] + ffn_part * gains[2])
    own_hat, own_scale = normalize(layer_input)
    cot_rows = cotangent.astype(F32)
    input_grad = cot_rows + own_scale * (
        e_rows
        - jnp.mean(e_rows, axis=-1, keepdims=True)
        - own_hat * jnp.mean(e_rows * own_hat, axis=-1, keepdims=True)
    )

    small = jnp.stack(
        [
            jnp.sum(attn_part * xhat, axis=0),
            jnp.sum(attn_part, axis=0),
            jnp.sum(ffn_part * xhat, axis=0),
            jnp.sum(ffn_part, axis=0),
            jnp.sum(cot_rows, axis=0),
        ]
    )
    small = small + swap_core(small)
    for k in range(bits):
        small = small + swap(small, k)
    columns = jnp.concatenate(
        [jnp.sum(qkv_grad.astype(F32), axis=0), jnp.sum(grad_ffn.astype(F32), axis=0)]
    )
    for k in (BIT_Y,) + zh_bits:
        columns = columns + swap(columns, k)
    columns = ordered(bit[BIT_X], columns, swap(columns, BIT_X), 0)
    columns = ordered(bit[BIT_ZL], columns, swap(columns, BIT_ZL), 0).reshape(4, -1)
    out_qkv_bias = columns[:, : 3 * HEAD_DIM].reshape(-1)
    out_fc1_bias = columns[:, 3 * HEAD_DIM :].reshape(-1)

    return (
        layer_output,
        input_grad,
        small[0],
        small[1],
        small[2],
        small[3],
        out_qkv,
        out_qkv_bias,
        out_dense,
        small[4],
        out_fc1,
        out_fc1_bias,
        out_fc2,
        small[4],
    )


def solution(mesh):
    in_specs = (
        P(("dp", "tensor"), None),
        P(),
        P(),
        P(),
        P(),
        P("dp", "tensor"),
        P("tensor"),
        P("tensor", "dp"),
        P(),
        P("dp", "tensor"),
        P("tensor"),
        P("tensor", "dp"),
        P(),
        P("dp"),
        P(("dp", "tensor"), None),
    )
    out_specs = (
        P(("dp", "tensor"), None),
        P(("dp", "tensor"), None),
        P(),
        P(),
        P(),
        P(),
        P("dp", "tensor"),
        P("tensor"),
        P("tensor", "dp"),
        P(),
        P("dp", "tensor"),
        P("tensor"),
        P("tensor", "dp"),
        P(),
    )
    return jax.shard_map(local, mesh=mesh, in_specs=in_specs, out_specs=out_specs, check_vma=False)
```

time: 2790 us -> 965 us (0.35)
  waiting for transfers between devices: 2390 us -> 418 us
  local copies, waits for them, and re-layouts: 36.6 us -> 168 us
  blocking collectives: 117 us -> 0 us
  other arithmetic: 40.6 us -> 135 us
  starting transfers between devices: 0.56 us -> 55.3 us
    reduce_scatter x7 -> x0, waiting for transfers between devices: 1750 us -> none  [the longest x1 692 us: local(): lax.psum_scatter(grad_fc1, 'dp', scatter_dimension=0, tiled=True)]
    all_gather x7 -> x0, waiting for transfers between devices: 629 us -> none  [the longest x2 328 us: local(): lax.all_gather((dense_weight, fc2_weight), 'dp', axis=1, tiled=True)]
    ppermute x0 -> x55, waiting for transfers between devices: none -> 418 us  [the longest x50 418 us: swap(): return lax.ppermute(v, 'dp', [(i, i ^ 1 << k) for i in range(n)])]
    psum x2 -> x0, blocking collectives: 117 us -> none  [the longest x1 75.1 us: local(): lax.psum((jnp.sum(qkv_grad.astype(jnp.float32), axis=0), jnp.sum(grad_ffn...]
    ppermute x0 -> x55, starting transfers between devices: none -> 55.3 us  [the longest x50 55.2 us: swap(): return lax.ppermute(v, 'dp', [(i, i ^ 1 << k) for i in range(n)])]
    another operation x5 -> x49, other arithmetic: 2.12 us -> 51.2 us  [the longest x42 34.1 us: ordered(): jnp.stack([jnp.where(b == 0, own, other), jnp.where(b == 0, other, own)],...]
    dot_general x0 -> x3, local copies, waits for them, and re-layouts: none -> 37.2 us  [mm(): return lax.dot_general(a, b, dims, preferred_element_type=F32)]
    add x1 -> x15, other arithmetic: 0.01 us -> 31.6 us  [the longest x2 16 us: scatter_tokens(): v = keep + swap_core(pick(v, 1 - core, 1).astype(BF16))]
  transfers between devices with their start and end apart: 14 -> 55, of which waited for: 9 -> 28; matrix products, arithmetic and copies ran while one was open for 9% -> 39% of each run, Pallas kernels for 0% -> 0%
where the time goes in v1:
time: 965 us; the launch traced here: 954 us
  waiting for transfers between devices  418 us (43%)
  matrix products  176 us (18%)
  local copies, waits for them, and re-layouts  168 us (17%)
  other arithmetic  135 us (14%)
  starting transfers between devices  55.3 us (6%)
    ppermute x50, waiting for transfers between devices, swap(): return lax.ppermute(v, 'dp', [(i, i ^ 1 << k) for i in range(n)])  418 us
    dot_general x12, matrix products, mm(): return lax.dot_general(a, b, dims, preferred_element_type=F32)  158 us
    ppermute x50, starting transfers between devices, swap(): return lax.ppermute(v, 'dp', [(i, i ^ 1 << k) for i in range(n)])  55.2 us
    dot_general x3, local copies, waits for them, and re-layouts, mm(): return lax.dot_general(a, b, dims, preferred_element_type=F32)  37.2 us
    another operation x42, other arithmetic, ordered(): jnp.stack([jnp.where(b == 0, own, other), jnp.where(b == 0, other, own)],...  34.1 us
    unnamed x179, local copies, waits for them, and re-layouts  22.1 us
  transfers between devices with their start and end apart: 55, of which 28 were waited for; matrix products, arithmetic and copies ran while one was open for 39% of the time, Pallas kernels for 0%

profile of v1, /device:TPU:0, one launch (start us, length us, event | category | flops | bytes accessed | tf_op | source)
XLA Modules:
  0.0 954.0 jit_solution(8268594650038495737)
XLA Ops:
  0.7 3.1 collective-permute-start
  11.5 3.1 constant_dynamic-slice_fusion.3
  51.0 2.8 collective-permute-done.10
  59.3 21.8 %collective-permute-done.11 = bf16[2,2,128,256]{3,2,1,0:T(8,128)(2,1)S(1)} collective-permute-done((bf16[2,2,128,256]{3,2,1,0:T(8,128)(2,1)S(1)}, bf16[2,2,128,256]{3,2,1,0:T(8,128)(2,1)S(1)}, u32[]{:S(2)}, u32[]{:S(2)}) %collective-permute-start.11) | collective-permute-done | bytes 262176 | tf_op jit(solution)/shard_map/ppermute | solution.py:81
  81.1 4.7 collective-permute-start.6
  91.2 4.7 collective-permute-done.6
  98.0 17.4 %collective-permute-done.18 = bf16[2,128,1024]{2,1,0:T(8,128)(2,1)S(1)} collective-permute-done((bf16[2,128,1024]{2,1,0:T(8,128)(2,1)S(1)}, bf16[2,128,1024]{2,1,0:T(8,128)(2,1)S(1)}, u32[]{:S(2)}, u32[]{:S(2)}) %collective-permute-start.18) | collective-permute-done | bytes 524320 | tf_op jit(solution)/shard_map/ppermute | solution.py:81
  115.6 5.5 collective-permute-done.14
  121.1 3.0 collective-permute-start.19
  124.6 9.0 collective-permute-done.3
  134.6 58.6 %collective-permute-done.7 = bf16[2,2,128,768]{3,2,1,0:T(8,128)(2,1)S(1)} collective-permute-done((bf16[2,2,128,768]{3,2,1,0:T(8,128)(2,1)S(1)}, bf16[2,2,128,768]{3,2,1,0:T(8,128)(2,1)S(1)}, u32[]{:S(2)}, u32[]{:S(2)}) %collective-permute-start.7) | collective-permute-done | bytes 786464 | tf_op jit(solution)/shard_map/ppermute | solution.py:81
  193.4 22.2 %collective-permute-done.19 = bf16[2,2,128,1024]{3,2,1,0:T(8,128)(2,1)S(1)} collective-permute-done((bf16[2,2,128,1024]{3,2,1,0:T(8,128)(2,1)S(1)}, bf16[2,2,128,1024]{3,2,1,0:T(8,128)(2,1)S(1)}, u32[]{:S(2)}, u32[]{:S(2)}) %collective-permute-start.19) | collective-permute-done | bytes 1048608 | tf_op jit(solution)/shard_map/ppermute | solution.py:81
  217.5 12.3 %collective-permute-done.15 = bf16[2,2,128,1024]{3,2,1,0:T(8,128)(2,1)S(1)} collective-permute-done((bf16[2,2,128,1024]{3,2,1,0:T(8,128)(2,1)S(1)}, bf16[2,2,128,1024]{3,2,1,0:T(8,128)(2,1)S(1)}, u32[]{:S(2)}, u32[]{:S(2)}) %collective-permute-start.15) | collective-permute-done | bytes 1048608 | tf_op jit(solution)/shard_map/ppermute | solution.py:81
  237.4 10.4 %collective-permute-done.8 = bf16[2,2,2,128,768]{4,3,2,1,0:T(8,128)(2,1)S(1)} collective-permute-done((bf16[2,2,2,128,768]{4,3,2,1,0:T(8,128)(2,1)S(1)}, bf16[2,2,2,128,768]{4,3,2,1,0:T(8,128)(2,1)S(1)}, u32[]{:S(2)}, u32[]{:S(2)}) %collective-permute-start.8) | collective-permute-done | bytes 1572896 | tf_op jit(solution)/shard_map/ppermute | solution.py:81
  250.3 42.5 %collective-permute-done.20 = bf16[2,2,2,128,1024]{4,3,2,1,0:T(8,128)(2,1)S(1)} collective-permute-done((bf16[2,2,2,128,1024]{4,3,2,1,0:T(8,128)(2,1)S(1)}, bf16[2,2,2,128,1024]{4,3,2,1,0:T(8,128)(2,1)S(1)}, u32[]{:S(2)}, u32[]{:S(2)}) %collective-permute-start.20) | collective-permute-done | bytes 2097184 | tf_op jit(solution)/shard_map/ppermute | solution.py:81
  296.0 30.0 %collective-permute-done.16 = bf16[2,2,2,128,1024]{4,3,2,1,0:T(8,128)(2,1)} collective-permute-done((bf16[2,2,2,128,1024]{4,3,2,1,0:T(8,128)(2,1)S(1)}, bf16[2,2,2,128,1024]{4,3,2,1,0:T(8,128)(2,1)}, u32[]{:S(2)}, u32[]{:S(2)}) %collective-permute-start.16) | collective-permute-done | bytes 2097184 | tf_op jit(solution)/shard_map/ppermute | solution.py:81
  335.4 7.4 add_convert_fusion.3
  342.8 8.5 broadcast_add_fusion
  351.3 10.9 %reshape.432 = f32[4,512,3,256]{3,2,1,0:T(4,128)} reshape(f32[2048,768]{1,0:T(8,128)} %broadcast_add_fusion) | data formatting | bytes 12582912 | tf_op jit(solution)/shard_map/reshape | solution.py:170
  362.1 6.9 slice.183
  369.0 11.8 %fusion.121 = (f32[4,512,1,256]{3,2,1,0:T(1,128)}, f32[4,512,1,256]{3,2,1,0:T(1,128)}) fusion(f32[4,512,3,256]{3,2,1,0:T(4,128)} %reshape.432), kind=kLoop, calls=%fused_computation.351 | loop fusion | bytes 8388608 | tf_op jit(solution)/shard_map/slice | solution.py:172
  389.6 5.2 select_bitcast_fusion.1
  394.8 7.6 pad_maximum_fusion.1
  402.4 8.5 copy.118
  410.9 6.9 convolution_convert_fusion
  417.8 6.1 fusion.52
  424.0 6.2 fusion.125
  430.2 5.0 convolution_convert_fusion.2
  450.7 7.0 fusion.46
  464.2 3.2 fusion.39
  468.0 2.8 copy.131
  470.9 12.4 %copy.136 = bf16[2048,2048]{1,0:T(8,128)(2,1)} copy(bf16[2048,2048]{0,1:T(8,128)(2,1)} %bitcast.465) | data formatting | bytes 16777216 | tf_op jit(solution)/shard_map/dot_general | solution.py:18
  483.2 6.0 fusion.129
  491.6 14.7 %multiply_convert_fusion = (bf16[2048,1024]{1,0:T(8,128)(2,1)}, f32[2048,1024]{1,0:T(8,128)}) fusion(f32[1024]{0:T(1024)S(1)} %copy-done.71, bf16[2048,2048]{1,0:T(8,128)(2,1)} %bitcast.482, bf16[2048,1024]{1,0:T(8,128)(2,1)S(1)} %bitcast.497), kind=kOutput, calls=%fused_computation.27 | convolution fusion | flops 8602517504 | bytes 25169920 | tf_op jit(solution)/shard_map/dot_general | solution.py:18
  506.3 14.4 %fusion.10 = f32[2,2,2,2,128,1024]{5,4,3,2,1,0:T(8,128)S(1)} fusion(bf16[2,2,2,2,128,2048]{5,4,3,2,1,0:T(8,128)(2,1)S(1)} %bitcast.488, bf16[2048,1024]{1,0:T(8,128)(2,1)} %get-tuple-element.135), kind=kOutput, calls=%fused_computation.40 | convolution fusion | flops 8589934592 | bytes 20971520 | tf_op jit(solution)/shard_map/dot_general | solution.py:18
  520.8 15.8 %fusion.126 = f32[2048,2048]{1,0:T(8,128)} fusion(bf16[2048,1024]{1,0:T(8,128)(2,1)} %get-tuple-element.135, bf16[2048,1024]{1,0:T(8,128)(2,1)S(1)} %bitcast.498), kind=kOutput, calls=%fused_computation.356 | convolution fusion | flops 8589934592 | bytes 25165824 | tf_op jit(solution)/shard_map/dot_general | solution.py:18
  536.6 15.5 %convert_reduce_fusion.1 = (f32[1024]{0:T(1024)S(1)}, bf16[2048,1024]{1,0:T(8,128)(2,1)}) fusion(f32[2048,1024]{1,0:T(8,128)} %get-tuple-element.136, f32[1024]{0:T(1024)S(1)} %copy-done.71, bf16[2048,2048]{1,0:T(8,128)(2,1)S(1)} %bitcast.468, bf16[2048,1024]{1,0:T(8,128)(2,1)S(1)} %bitcast.499), kind=kOutput, calls=%fused_computation.26 | convolution fusion | flops 8617196544 | bytes 25174016 | tf_op jit(solution)/shard_map/dot_general | solution.py:18
  555.9 8.6 convolution_add_fusion
  568.6 14.8 %fusion.127 = f32[2048,2048]{1,0:T(8,128)} fusion(bf16[2048,768]{1,0:T(8,128)(2,1)} %bitcast.504, bf16[2048,768]{1,0:T(8,128)(2,1)S(1)} %bitcast.503), kind=kOutput, calls=%fused_computation.357 | convolution fusion | flops 6442450944 | bytes 23068672 | tf_op jit(solution)/shard_map/dot_general | solution.py:18
  583.4 29.6 %fusion.119 = (f32[2048]{0:T(1024)S(1)}, f32[2048]{0:T(1024)S(1)}, f32[2048,2048]{1,0:T(8,128)}, f32[2048]{0:T(1024)}, f32[2048]{0:T(1024)}, /*index=5*/bf16[2048,2048]{1,0:T(8,128)(2,1)}, bf16[2048,2048]{1,0:T(8,128)(2,1)}) fusion(f32[2048]{0:T(1024)S(1)} %bitcast.522, f32[2048]{0:T(1024)S(1)} %bitcast.521, bf16[4,1,256,2048]{3,2,1,0:T(8,128)(2,1)} %copy-done.2, ...), kind=kOutput, calls=%fused_computation.349 | convolution fusion | flops 8669618176 | bytes 67190784 | tf_op jit(solution)/shard_map/dot_general | solution.py:18
  613.0 6.0 fusion.9
  619.0 12.3 %copy.157 = bf16[2048,2048]{1,0:T(8,128)(2,1)} copy(bf16[2048,2048]{0,1:T(8,128)(2,1)} %bitcast.484) | data formatting | bytes 16777216 | tf_op jit(solution)/shard_map/dot_general | solution.py:18
  631.4 14.4 %fusion.12 = f32[2,2,2,2,128,1024]{5,4,3,2,1,0:T(8,128)} fusion(bf16[2,2,2,2,128,2048]{5,4,3,2,1,0:T(8,128)(2,1)} %bitcast.490, bf16[2048,1024]{1,0:T(8,128)(2,1)} %get-tuple-element.138), kind=kOutput, calls=%fused_computation.42 | convolution fusion | flops 8589934592 | bytes 20971520 | tf_op jit(solution)/shard_map/dot_general | solution.py:18
  645.8 12.5 %copy.156 = bf16[2048,2048]{1,0:T(8,128)(2,1)} copy(bf16[2048,2048]{0,1:T(8,128)(2,1)} %bitcast.483) | data formatting | bytes 16777216 | tf_op jit(solution)/shard_map/dot_general | solution.py:18
  658.2 9.3 fusion.128
  667.6 6.2 fusion.26
  674.6 2.9 collective-permute-done.41
  683.1 12.1 %collective-permute-done.44 = bf16[2,2,128,256]{3,2,1,0:T(8,128)(2,1)S(1)} collective-permute-done((bf16[2,2,128,256]{3,2,1,0:T(8,128)(2,1)S(1)}, bf16[2,2,128,256]{3,2,1,0:T(8,128)(2,1)S(1)}, u32[]{:S(2)}, u32[]{:S(2)}) %collective-permute-start.44) | collective-permute-done | bytes 262176 | tf_op jit(solution)/shard_map/ppermute | solution.py:81
  697.3 3.5 collective-permute-done.45
  705.3 9.5 collective-permute-done.35
  724.4 3.5 bitcast_add_fusion.2
  731.6 43.6 %collective-permute-done.36 = bf16[2,2,128,768]{3,2,1,0:T(8,128)(2,1)} collective-permute-done((bf16[2,2,128,768]{3,2,1,0:T(8,128)(2,1)}, bf16[2,2,128,768]{3,2,1,0:T(8,128)(2,1)}, u32[]{:S(2)}, u32[]{:S(2)}) %collective-permute-start.36) | collective-permute-done | bytes 786464 | tf_op jit(solution)/shard_map/ppermute | solution.py:81
  776.9 3.5 bitcast_add_fusion.3
  781.5 3.4 collective-permute-start.48
  784.9 11.5 %collective-permute-done.37 = bf16[2,128,768]{2,1,0:T(8,128)(2,1)S(1)} collective-permute-done((bf16[2,128,768]{2,1,0:T(8,128)(2,1)S(1)}, bf16[2,128,768]{2,1,0:T(8,128)(2,1)S(1)}, u32[]{:S(2)}, u32[]{:S(2)}) %collective-permute-start.37) | collective-permute-done | bytes 393248 | tf_op jit(solution)/shard_map/ppermute | solution.py:81
  798.5 5.9 bitcast_add_fusion
  806.8 13.3 %collective-permute-done.52 = bf16[2,2,128,1024]{3,2,1,0:T(8,128)(2,1)} collective-permute-done((bf16[2,2,128,1024]{3,2,1,0:T(8,128)(2,1)}, bf16[2,2,128,1024]{3,2,1,0:T(8,128)(2,1)}, u32[]{:S(2)}, u32[]{:S(2)}) %collective-permute-start.52) | collective-permute-done | bytes 1048608 | tf_op jit(solution)/shard_map/ppermute | solution.py:81
  822.9 10.1 %bitcast_add_fusion.1 = f32[4,256,2048]{2,1,0:T(8,128)} fusion(bf16[4,256,2048]{2,1,0:T(8,128)(2,1)} %collective-permute-done.21, f32[4,2,256,2048]{3,2,1,0:T(8,128)} %bitcast.460, s32[]{:T(128)S(6)} %select_n.444), kind=kLoop, calls=%fused_computation.25 | loop fusion | flops 4194304 | bytes 20971524 | tf_op jit(solution)/shard_map/add | solution.py:106
  836.8 5.8 collective-permute-done.48
  846.3 7.5 collective-permute-done.53
  859.6 40.2 %collective-permute-done.22 = bf16[2,256,2048]{2,1,0:T(8,128)(2,1)} collective-permute-done((bf16[2,256,2048]{2,1,0:T(8,128)(2,1)S(1)}, bf16[2,256,2048]{2,1,0:T(8,128)(2,1)}, u32[]{:S(2)}, u32[]{:S(2)}) %collective-permute-start.22) | collective-permute-done | bytes 2097184 | tf_op jit(solution)/shard_map/ppermute | solution.py:81
  905.1 20.4 %collective-permute-done.23 = bf16[256,2048]{1,0:T(8,128)(2,1)S(1)} collective-permute-done((bf16[256,2048]{1,0:T(8,128)(2,1)S(1)}, bf16[256,2048]{1,0:T(8,128)(2,1)S(1)}, u32[]{:S(2)}, u32[]{:S(2)}) %collective-permute-start.23) | collective-permute-done | bytes 1048608 | tf_op jit(solution)/shard_map/ppermute | solution.py:81
  925.5 3.6 convert_reduce_fusion.4
  940.9 3.8 collective-permute-done.33
  (422 shorter events, 199.8 us)
Async XLA Ops:
  0.7 24.5 %collective-permute-start = (s32[512]{0:T(512)}, s32[512]{0:T(512)S(1)}, u32[]{:S(2)}, u32[]{:S(2)}) collective-permute-start(s32[512]{0:T(512)} %param.28), channel_id=1, source_target_pairs={{0,8},{2,10},{4,12},{6,14},{8,0},{10,2},{12,4},{14,6},{16,24},{18,... | collective-permute-start | bytes 6152 | tf_op jit(solution)/shard_map/ppermute | solution.py:81
  6.2 41.4 %collective-permute-start.9 = (bf16[128,2,256]{2,0,1:T(8,128)(2,1)}, bf16[128,2,256]{2,0,1:T(8,128)(2,1)}, u32[]{:S(2)}, u32[]{:S(2)}) collective-permute-start(bf16[128,2,256]{2,0,1:T(8,128)(2,1)} %bitcast.30), channel_id=1, source_target_pairs={{0,2},{2,0},{4,6},{6,4},{8,10},{10,8},{12,14},{14,12},{16,18},{18,... | collective-permute-start | bytes 393224 | tf_op jit(solution)/shard_map/ppermute | solution.py:81
  10.2 45.4 %collective-permute-start.5 = (bf16[128,2,768]{2,0,1:T(8,128)(2,1)}, bf16[128,2,768]{2,0,1:T(8,128)(2,1)}, u32[]{:S(2)}, u32[]{:S(2)}) collective-permute-start(bf16[128,2,768]{2,0,1:T(8,128)(2,1)} %bitcast.10), channel_id=1, source_target_pairs={{0,2},{2,0},{4,6},{6,4},{8,10},{10,8},{12,14},{14,12},{16,18},{18,... | collective-permute-start | bytes 1179656 | tf_op jit(solution)/shard_map/ppermute | solution.py:81
  15.7 73.8 %collective-permute-start.13 = (bf16[128,2,1024]{2,0,1:T(8,128)(2,1)}, bf16[128,2,1024]{2,0,1:T(8,128)(2,1)}, u32[]{:S(2)}, u32[]{:S(2)}) collective-permute-start(bf16[128,2,1024]{2,0,1:T(8,128)(2,1)} %bitcast.456), channel_id=1, source_target_pairs={{0,2},{2,0},{4,6},{6,4},{8,10},{10,8},{12,14},{14,12},{16,18},{18,... | collective-permute-start | bytes 1572872 | tf_op jit(solution)/shard_map/ppermute | solution.py:81
  17.2 68.7 %collective-permute-start.2 = (bf16[256,2048]{1,0:T(8,128)(2,1)S(1)}, bf16[256,2048]{1,0:T(8,128)(2,1)S(1)}, u32[]{:S(2)}, u32[]{:S(2)}) collective-permute-start(bf16[256,2048]{1,0:T(8,128)(2,1)S(1)} %copy-done.3), channel_id=1, source_target_pairs={{0,8},{2,10},{4,12},{6,14},{8,0},{10,2},{12,4},{14,6},{16,24},{18,... | collective-permute-start | bytes 3145736 | tf_op jit(solution)/shard_map/ppermute | solution.py:81
  17.7 36.1 %copy-start.6 = (bf16[256,2048]{1,0:T(8,128)(2,1)S(1)}, bf16[256,2048]{1,0:T(8,128)(2,1)}, u32[]{:S(2)}) copy-start(bf16[256,2048]{1,0:T(8,128)(2,1)} %param.29) | copy-start | bytes 3145732
  25.2 14.6 %collective-permute-start.1 = (s32[2,512]{1,0:T(2,128)S(1)}, s32[2,512]{1,0:T(2,128)}, u32[]{:S(2)}, u32[]{:S(2)}) collective-permute-start(s32[2,512]{1,0:T(2,128)S(1)} %pad_add_fusion.1), channel_id=1, source_target_pairs={{0,2},{2,0},{4,6},{6,4},{8,10},{10,8},{12,14},{14,12},{16,18},{18,... | collective-permute-start | bytes 12296 | tf_op jit(solution)/shard_map/ppermute | solution.py:81
  39.8 48.0 %collective-permute-start.17 = (bf16[128,2,1024]{2,0,1:T(8,128)(2,1)}, bf16[128,2,1024]{2,0,1:T(8,128)(2,1)}, u32[]{:S(2)}, u32[]{:S(2)}) collective-permute-start(bf16[128,2,1024]{2,0,1:T(8,128)(2,1)} %bitcast.510), channel_id=1, source_target_pairs={{0,2},{2,0},{4,6},{6,4},{8,10},{10,8},{12,14},{14,12},{16,18},{18,... | collective-permute-start | bytes 1572872 | tf_op jit(solution)/shard_map/ppermute | solution.py:81
  48.6 5.2 collective-permute-start.10
  53.8 70.5 %collective-permute-start.24 = (bf16[256,2048]{1,0:T(8,128)(2,1)S(1)}, bf16[256,2048]{1,0:T(8,128)(2,1)S(1)}, u32[]{:S(2)}, u32[]{:S(2)}) collective-permute-start(bf16[256,2048]{1,0:T(8,128)(2,1)S(1)} %copy-done.6), channel_id=1, source_target_pairs={{0,8},{2,10},{4,12},{6,14},{8,0},{10,2},{12,4},{14,6},{16,24},{18,... | collective-permute-start | bytes 3145736 | tf_op jit(solution)/shard_map/ppermute | solution.py:81
  55.5 32.8 %copy-start.41 = (bf16[128,2,1,1024]{3,0,1,2:T(8,128)(2,1)S(1)}, bf16[128,2,1,1024]{3,0,1,2:T(8,128)(2,1)}, u32[]{:S(2)}) copy-start(bf16[128,2,1,1024]{3,0,1,2:T(8,128)(2,1)} %copy.164) | copy-start | bytes 1572868
  55.5 25.6 %collective-permute-start.11 = (bf16[2,2,128,256]{3,2,1,0:T(8,128)(2,1)S(1)}, bf16[2,2,128,256]{3,2,1,0:T(8,128)(2,1)S(1)}, u32[]{:S(2)}, u32[]{:S(2)}) collective-permute-start(bf16[2,2,128,256]{3,2,1,0:T(8,128)(2,1)S(1)} %pad_maximum_fusion.20), channel_id=1, source_target_pairs={{0,16},{2,18},{4,20},{6,22},{8,24},{10,26},{12,28},{14,30},{16,0},... | collective-permute-start | bytes 786440 | tf_op jit(solution)/shard_map/ppermute | solution.py:81
  81.1 14.7 %collective-permute-start.6 = (bf16[2,128,768]{2,1,0:T(8,128)(2,1)S(1)}, bf16[2,128,768]{2,1,0:T(8,128)(2,1)S(1)}, u32[]{:S(2)}, u32[]{:S(2)}) collective-permute-start(bf16[2,128,768]{2,1,0:T(8,128)(2,1)S(1)} %fusion.93), channel_id=1, source_target_pairs={{0,8},{2,10},{4,12},{6,14},{8,0},{10,2},{12,4},{14,6},{16,24},{18,... | collective-permute-start | bytes 1179656 | tf_op jit(solution)/shard_map/ppermute | solution.py:81
  85.9 145.7 %collective-permute-start.12 = (bf16[2,2,2,128,256]{4,3,2,1,0:T(8,128)(2,1)S(1)}, bf16[2,2,2,128,256]{4,3,2,1,0:T(8,128)(2,1)S(1)}, u32[]{:S(2)}, u32[]{:S(2)}) collective-permute-start(bf16[2,2,2,128,256]{4,3,2,1,0:T(8,128)(2,1)S(1)} %pad_maximum_fusion.19), channel_id=1, source_target_pairs={{0,4},{2,6},{4,0},{6,2},{8,12},{10,14},{12,8},{14,10},{16,20},{18,... | collective-permute-start | bytes 1572872 | tf_op jit(solution)/shard_map/ppermute | solution.py:81
  87.7 45.9 %collective-permute-start.3 = (bf16[2,256,2048]{2,1,0:T(8,128)(2,1)S(1)}, bf16[2,256,2048]{2,1,0:T(8,128)(2,1)S(1)}, u32[]{:S(2)}, u32[]{:S(2)}) collective-permute-start(bf16[2,256,2048]{2,1,0:T(8,128)(2,1)S(1)} %pad_maximum_fusion.7), channel_id=1, source_target_pairs={{0,2},{2,0},{4,6},{6,4},{8,10},{10,8},{12,14},{14,12},{16,18},{18,... | collective-permute-start | bytes 6291464 | tf_op jit(solution)/shard_map/ppermute | solution.py:81
  89.6 25.8 %collective-permute-start.18 = (bf16[2,128,1024]{2,1,0:T(8,128)(2,1)S(1)}, bf16[2,128,1024]{2,1,0:T(8,128)(2,1)S(1)}, u32[]{:S(2)}, u32[]{:S(2)}) collective-permute-start(bf16[2,128,1024]{2,1,0:T(8,128)(2,1)S(1)} %fusion.69), channel_id=1, source_target_pairs={{0,8},{2,10},{4,12},{6,14},{8,0},{10,2},{12,4},{14,6},{16,24},{18,... | collective-permute-start | bytes 1572872 | tf_op jit(solution)/shard_map/ppermute | solution.py:81
  95.8 25.3 %collective-permute-start.14 = (bf16[2,128,1024]{2,1,0:T(8,128)(2,1)S(1)}, bf16[2,128,1024]{2,1,0:T(8,128)(2,1)S(1)}, u32[]{:S(2)}, u32[]{:S(2)}) collective-permute-start(bf16[2,128,1024]{2,1,0:T(8,128)(2,1)S(1)} %fusion.73), channel_id=1, source_target_pairs={{0,8},{2,10},{4,12},{6,14},{8,0},{10,2},{12,4},{14,6},{16,24},{18,... | collective-permute-start | bytes 1572872 | tf_op jit(solution)/shard_map/ppermute | solution.py:81
  115.4 77.8 %collective-permute-start.7 = (bf16[2,2,128,768]{3,2,1,0:T(8,128)(2,1)S(1)}, bf16[2,2,128,768]{3,2,1,0:T(8,128)(2,1)S(1)}, u32[]{:S(2)}, u32[]{:S(2)}) collective-permute-start(bf16[2,2,128,768]{3,2,1,0:T(8,128)(2,1)S(1)} %pad_maximum_fusion.18), channel_id=1, source_target_pairs={{0,16},{2,18},{4,20},{6,22},{8,24},{10,26},{12,28},{14,30},{16,0},... | collective-permute-start | bytes 2359304 | tf_op jit(solution)/shard_map/ppermute | solution.py:81
  121.1 94.5 %collective-permute-start.19 = (bf16[2,2,128,1024]{3,2,1,0:T(8,128)(2,1)S(1)}, bf16[2,2,128,1024]{3,2,1,0:T(8,128)(2,1)S(1)}, u32[]{:S(2)}, u32[]{:S(2)}) collective-permute-start(bf16[2,2,128,1024]{3,2,1,0:T(8,128)(2,1)S(1)} %pad_maximum_fusion.17), channel_id=1, source_target_pairs={{0,16},{2,18},{4,20},{6,22},{8,24},{10,26},{12,28},{14,30},{16,0},... | collective-permute-start | bytes 3145736 | tf_op jit(solution)/shard_map/ppermute | solution.py:81
  124.3 110.4 %copy-start.10 = (bf16[256,2048]{1,0:T(8,128)(2,1)}, bf16[256,2048]{1,0:T(8,128)(2,1)S(1)}, u32[]{:S(2)}) copy-start(bf16[256,2048]{1,0:T(8,128)(2,1)S(1)} %collective-permute-done.24) | copy-start | bytes 3145732
  124.4 105.4 %collective-permute-start.15 = (bf16[2,2,128,1024]{3,2,1,0:T(8,128)(2,1)S(1)}, bf16[2,2,128,1024]{3,2,1,0:T(8,128)(2,1)S(1)}, u32[]{:S(2)}, u32[]{:S(2)}) collective-permute-start(bf16[2,2,128,1024]{3,2,1,0:T(8,128)(2,1)S(1)} %pad_maximum_fusion.16), channel_id=1, source_target_pairs={{0,16},{2,18},{4,20},{6,22},{8,24},{10,26},{12,28},{14,30},{16,0},... | collective-permute-start | bytes 3145736 | tf_op jit(solution)/shard_map/ppermute | solution.py:81
  133.6 101.2 %collective-permute-start.25 = (bf16[2,256,2048]{2,1,0:T(8,128)(2,1)S(1)}, bf16[2,256,2048]{2,1,0:T(8,128)(2,1)S(1)}, u32[]{:S(2)}, u32[]{:S(2)}) collective-permute-start(bf16[2,256,2048]{2,1,0:T(8,128)(2,1)S(1)} %pad_maximum_fusion.10), channel_id=1, source_target_pairs={{0,2},{2,0},{4,6},{6,4},{8,10},{10,8},{12,14},{14,12},{16,18},{18,... | collective-permute-start | bytes 6291464 | tf_op jit(solution)/shard_map/ppermute | solution.py:81
  193.2 137.2 %collective-permute-start.4 = (bf16[4,256,2048]{2,1,0:T(8,128)(2,1)S(1)}, bf16[4,256,2048]{2,1,0:T(8,128)(2,1)S(1)}, u32[]{:S(2)}, u32[]{:S(2)}) collective-permute-start(bf16[4,256,2048]{2,1,0:T(8,128)(2,1)S(1)} %pad_maximum_fusion.2), channel_id=1, source_target_pairs={{0,1},{1,0},{2,3},{3,2},{4,5},{5,4},{6,7},{7,6},{8,9},{9,8},{10,11... | collective-permute-start | bytes 12582920 | tf_op jit(solution)/shard_map/ppermute | solution.py:84
  215.6 32.2 %collective-permute-start.8 = (bf16[2,2,2,128,768]{4,3,2,1,0:T(8,128)(2,1)S(1)}, bf16[2,2,2,128,768]{4,3,2,1,0:T(8,128)(2,1)S(1)}, u32[]{:S(2)}, u32[]{:S(2)}) collective-permute-start(bf16[2,2,2,128,768]{4,3,2,1,0:T(8,128)(2,1)S(1)} %pad_maximum_fusion.11), channel_id=1, source_target_pairs={{0,4},{2,6},{4,0},{6,2},{8,12},{10,14},{12,8},{14,10},{16,20},{18,... | collective-permute-start | bytes 4718600 | tf_op jit(solution)/shard_map/ppermute | solution.py:81
  229.8 63.0 %collective-permute-start.20 = (bf16[2,2,2,128,1024]{4,3,2,1,0:T(8,128)(2,1)S(1)}, bf16[2,2,2,128,1024]{4,3,2,1,0:T(8,128)(2,1)S(1)}, u32[]{:S(2)}, u32[]{:S(2)}) collective-permute-start(bf16[2,2,2,128,1024]{4,3,2,1,0:T(8,128)(2,1)S(1)} %pad_maximum_fusion.9), channel_id=1, source_target_pairs={{0,4},{2,6},{4,0},{6,2},{8,12},{10,14},{12,8},{14,10},{16,20},{18,... | collective-permute-start | bytes 6291464 | tf_op jit(solution)/shard_map/ppermute | solution.py:81
  231.7 94.4 %collective-permute-start.16 = (bf16[2,2,2,128,1024]{4,3,2,1,0:T(8,128)(2,1)S(1)}, bf16[2,2,2,128,1024]{4,3,2,1,0:T(8,128)(2,1)}, u32[]{:S(2)}, u32[]{:S(2)}) collective-permute-start(bf16[2,2,2,128,1024]{4,3,2,1,0:T(8,128)(2,1)S(1)} %pad_maximum_fusion.8), channel_id=1, source_target_pairs={{0,4},{2,6},{4,0},{6,2},{8,12},{10,14},{12,8},{14,10},{16,20},{18,... | collective-permute-start | bytes 6291464 | tf_op jit(solution)/shard_map/ppermute | solution.py:81
  237.4 152.1 %collective-permute-start.26 = (bf16[4,256,2048]{2,1,0:T(8,128)(2,1)}, bf16[4,256,2048]{2,1,0:T(8,128)(2,1)}, u32[]{:S(2)}, u32[]{:S(2)}) collective-permute-start(bf16[4,256,2048]{2,1,0:T(8,128)(2,1)} %pad_maximum_fusion.5), channel_id=1, source_target_pairs={{0,1},{1,0},{2,3},{3,2},{4,5},{5,4},{6,7},{7,6},{8,9},{9,8},{10,11... | collective-permute-start | bytes 12582920 | tf_op jit(solution)/shard_map/ppermute | solution.py:84
  490.1 188.6 %collective-permute-start.43 = (bf16[2,2,2,128,256]{4,3,2,1,0:T(8,128)(2,1)}, bf16[2,2,2,128,256]{4,3,2,1,0:T(8,128)(2,1)}, u32[]{:S(2)}, u32[]{:S(2)}) collective-permute-start(bf16[2,2,2,128,256]{4,3,2,1,0:T(8,128)(2,1)} %fusion.59), channel_id=1, source_target_pairs={{0,4},{2,6},{4,0},{6,2},{8,12},{10,14},{12,8},{14,10},{16,20},{18,... | collective-permute-start | bytes 1572872 | tf_op jit(solution)/shard_map/ppermute | solution.py:81
  506.3 30.3 %slice-start = ((s8[8388608]{0:T(1024)(128)(4,1)}), s8[4194304]{0:T(1024)(128)(4,1)S(1)}, s32[]{:S(2)}) async-start(s8[8388608]{0:T(1024)(128)(4,1)} %bitcast.466), calls=%async_computation | async-start | bytes 8388608
  520.8 32.6 %copy-start.15 = (f32[2,2,2,2,128,1024]{5,4,3,2,1,0:T(8,128)}, f32[2,2,2,2,128,1024]{5,4,3,2,1,0:T(8,128)S(1)}, u32[]{:S(2)}) copy-start(f32[2,2,2,2,128,1024]{5,4,3,2,1,0:T(8,128)S(1)} %fusion.10) | copy-start | bytes 25165828
  552.1 115.4 %collective-permute-start.39 = (f32[1792]{0:T(1024)S(1)}, f32[1792]{0:T(1024)S(1)}, u32[]{:S(2)}, u32[]{:S(2)}) collective-permute-start(f32[1792]{0:T(1024)S(1)} %pad_maximum_fusion.23), channel_id=1, source_target_pairs={{0,4},{2,6},{4,0},{6,2},{8,12},{10,14},{12,8},{14,10},{16,20},{18,... | collective-permute-start | bytes 21512 | tf_op jit(solution)/shard_map/ppermute | solution.py:81
  555.0 169.4 %collective-permute-start.51 = (bf16[2,2,2,128,1024]{4,3,2,1,0:T(8,128)(2,1)}, bf16[2,2,2,128,1024]{4,3,2,1,0:T(8,128)(2,1)}, u32[]{:S(2)}, u32[]{:S(2)}) collective-permute-start(bf16[2,2,2,128,1024]{4,3,2,1,0:T(8,128)(2,1)} %fusion.27), channel_id=1, source_target_pairs={{0,4},{2,6},{4,0},{6,2},{8,12},{10,14},{12,8},{14,10},{16,20},{18,... | collective-permute-start | bytes 6291464 | tf_op jit(solution)/shard_map/ppermute | solution.py:81
  567.3 255.6 %collective-permute-start.21 = (bf16[4,256,2048]{2,1,0:T(8,128)(2,1)}, bf16[4,256,2048]{2,1,0:T(8,128)(2,1)}, u32[]{:S(2)}, u32[]{:S(2)}) collective-permute-start(bf16[4,256,2048]{2,1,0:T(8,128)(2,1)} %fusion.8), channel_id=1, source_target_pairs={{0,1},{1,0},{2,3},{3,2},{4,5},{5,4},{6,7},{7,6},{8,9},{9,8},{10,11... | collective-permute-start | bytes 12582920 | tf_op jit(solution)/shard_map/ppermute | solution.py:84
  619.0 179.4 %collective-permute-start.27 = (bf16[4,256,2048]{2,1,0:T(8,128)(2,1)}, bf16[4,256,2048]{2,1,0:T(8,128)(2,1)}, u32[]{:S(2)}, u32[]{:S(2)}) collective-permute-start(bf16[4,256,2048]{2,1,0:T(8,128)(2,1)} %fusion.9), channel_id=1, source_target_pairs={{0,1},{1,0},{2,3},{3,2},{4,5},{5,4},{6,7},{7,6},{8,9},{9,8},{10,11... | collective-permute-start | bytes 12582920 | tf_op jit(solution)/shard_map/ppermute | solution.py:84
  667.6 6.3 collective-permute-start.40
  673.8 3.7 collective-permute-start.41
  677.5 37.3 %collective-permute-start.35 = (bf16[2,2,2,128,768]{4,3,2,1,0:T(8,128)(2,1)S(1)}, bf16[2,2,2,128,768]{4,3,2,1,0:T(8,128)(2,1)S(1)}, u32[]{:S(2)}, u32[]{:S(2)}) collective-permute-start(bf16[2,2,2,128,768]{4,3,2,1,0:T(8,128)(2,1)S(1)} %fusion.37), channel_id=1, source_target_pairs={{0,4},{2,6},{4,0},{6,2},{8,12},{10,14},{12,8},{14,10},{16,20},{18,... | collective-permute-start | bytes 4718600 | tf_op jit(solution)/shard_map/ppermute | solution.py:81
  678.7 3.8 collective-permute-start.42
  682.5 12.7 %collective-permute-start.44 = (bf16[2,2,128,256]{3,2,1,0:T(8,128)(2,1)S(1)}, bf16[2,2,128,256]{3,2,1,0:T(8,128)(2,1)S(1)}, u32[]{:S(2)}, u32[]{:S(2)}) collective-permute-start(bf16[2,2,128,256]{3,2,1,0:T(8,128)(2,1)S(1)} %fusion.100), channel_id=1, source_target_pairs={{0,16},{2,18},{4,20},{6,22},{8,24},{10,26},{12,28},{14,30},{16,0},... | collective-permute-start | bytes 786440 | tf_op jit(solution)/shard_map/ppermute | solution.py:81
  695.3 5.6 collective-permute-start.45
  700.8 76.0 %collective-permute-start.47 = (bf16[2,2,2,128,1024]{4,3,2,1,0:T(8,128)(2,1)}, bf16[2,2,2,128,1024]{4,3,2,1,0:T(8,128)(2,1)}, u32[]{:S(2)}, u32[]{:S(2)}) collective-permute-start(bf16[2,2,2,128,1024]{4,3,2,1,0:T(8,128)(2,1)} %fusion.26), channel_id=1, source_target_pairs={{0,4},{2,6},{4,0},{6,2},{8,12},{10,14},{12,8},{14,10},{16,20},{18,... | collective-permute-start | bytes 6291464 | tf_op jit(solution)/shard_map/ppermute | solution.py:81
  716.0 5.0 collective-permute-start.46
  720.9 54.2 %collective-permute-start.36 = (bf16[2,2,128,768]{3,2,1,0:T(8,128)(2,1)}, bf16[2,2,128,768]{3,2,1,0:T(8,128)(2,1)}, u32[]{:S(2)}, u32[]{:S(2)}) collective-permute-start(bf16[2,2,128,768]{3,2,1,0:T(8,128)(2,1)} %fusion.57), channel_id=1, source_target_pairs={{0,16},{2,18},{4,20},{6,22},{8,24},{10,26},{12,28},{14,30},{16,0},... | collective-permute-start | bytes 2359304 | tf_op jit(solution)/shard_map/ppermute | solution.py:81
  727.9 52.4 %copy-start.8 = (f32[2,2,2,128,1024]{4,3,2,1,0:T(8,128)}, f32[2,2,2,128,1024]{4,3,2,1,0:T(8,128)S(1)}, u32[]{:S(2)}) copy-start(f32[2,2,2,128,1024]{4,3,2,1,0:T(8,128)S(1)} %bitcast_add_fusion.2) | copy-start | bytes 12582916
  729.2 90.9 %collective-permute-start.52 = (bf16[2,2,128,1024]{3,2,1,0:T(8,128)(2,1)}, bf16[2,2,128,1024]{3,2,1,0:T(8,128)(2,1)}, u32[]{:S(2)}, u32[]{:S(2)}) collective-permute-start(bf16[2,2,128,1024]{3,2,1,0:T(8,128)(2,1)} %fusion.41), channel_id=1, source_target_pairs={{0,16},{2,18},{4,20},{6,22},{8,24},{10,26},{12,28},{14,30},{16,0},... | collective-permute-start | bytes 3145736 | tf_op jit(solution)/shard_map/ppermute | solution.py:81
  776.5 19.9 %collective-permute-start.37 = (bf16[2,128,768]{2,1,0:T(8,128)(2,1)S(1)}, bf16[2,128,768]{2,1,0:T(8,128)(2,1)S(1)}, u32[]{:S(2)}, u32[]{:S(2)}) collective-permute-start(bf16[2,128,768]{2,1,0:T(8,128)(2,1)S(1)} %dynamic-slice_bitcast_fusion.2), channel_id=1, source_target_pairs={{0,8},{2,10},{4,12},{6,14},{8,0},{10,2},{12,4},{14,6},{16,24},{18,... | collective-permute-start | bytes 1179656 | tf_op jit(solution)/shard_map/ppermute | solution.py:81
  781.5 61.1 %collective-permute-start.48 = (bf16[2,2,128,1024]{3,2,1,0:T(8,128)(2,1)}, bf16[2,2,128,1024]{3,2,1,0:T(8,128)(2,1)}, u32[]{:S(2)}, u32[]{:S(2)}) collective-permute-start(bf16[2,2,128,1024]{3,2,1,0:T(8,128)(2,1)} %fusion.40), channel_id=1, source_target_pairs={{0,16},{2,18},{4,20},{6,22},{8,24},{10,26},{12,28},{14,30},{16,0},... | collective-permute-start | bytes 3145736 | tf_op jit(solution)/shard_map/ppermute | solution.py:81
  797.2 47.1 %collective-permute-start.38 = (bf16[128,2,768]{2,0,1:T(8,128)(2,1)}, bf16[128,2,768]{2,0,1:T(8,128)(2,1)}, u32[]{:S(2)}, u32[]{:S(2)}) collective-permute-start(bf16[128,2,768]{2,0,1:T(8,128)(2,1)} %fusion.89), channel_id=1, source_target_pairs={{0,2},{2,0},{4,6},{6,4},{8,10},{10,8},{12,14},{14,12},{16,18},{18,... | collective-permute-start | bytes 1179656 | tf_op jit(solution)/shard_map/ppermute | solution.py:81
  806.0 51.2 %collective-permute-start.28 = (bf16[2,256,2048]{2,1,0:T(8,128)(2,1)}, bf16[2,256,2048]{2,1,0:T(8,128)(2,1)}, u32[]{:S(2)}, u32[]{:S(2)}) collective-permute-start(bf16[2,256,2048]{2,1,0:T(8,128)(2,1)} %slice.263), channel_id=1, source_target_pairs={{0,2},{2,0},{4,6},{6,4},{8,10},{10,8},{12,14},{14,12},{16,18},{18,... | collective-permute-start | bytes 6291464 | tf_op jit(solution)/shard_map/ppermute | solution.py:81
  822.5 31.3 %collective-permute-start.53 = (bf16[2,128,1024]{2,1,0:T(8,128)(2,1)}, bf16[2,128,1024]{2,1,0:T(8,128)(2,1)}, u32[]{:S(2)}, u32[]{:S(2)}) collective-permute-start(bf16[2,128,1024]{2,1,0:T(8,128)(2,1)} %dynamic-slice_bitcast_fusion), channel_id=1, source_target_pairs={{0,8},{2,10},{4,12},{6,14},{8,0},{10,2},{12,4},{14,6},{16,24},{18,... | collective-permute-start | bytes 1572872 | tf_op jit(solution)/shard_map/ppermute | solution.py:81
  835.5 64.4 %collective-permute-start.22 = (bf16[2,256,2048]{2,1,0:T(8,128)(2,1)S(1)}, bf16[2,256,2048]{2,1,0:T(8,128)(2,1)}, u32[]{:S(2)}, u32[]{:S(2)}) collective-permute-start(bf16[2,256,2048]{2,1,0:T(8,128)(2,1)S(1)} %slice.264), channel_id=1, source_target_pairs={{0,2},{2,0},{4,6},{6,4},{8,10},{10,8},{12,14},{14,12},{16,18},{18,... | collective-permute-start | bytes 6291464 | tf_op jit(solution)/shard_map/ppermute | solution.py:81
  844.2 58.4 %collective-permute-start.49 = (bf16[2,128,1024]{2,1,0:T(8,128)(2,1)S(1)}, bf16[2,128,1024]{2,1,0:T(8,128)(2,1)S(1)}, u32[]{:S(2)}, u32[]{:S(2)}) collective-permute-start(bf16[2,128,1024]{2,1,0:T(8,128)(2,1)S(1)} %dynamic-slice_bitcast_fusion.1), channel_id=1, source_target_pairs={{0,8},{2,10},{4,12},{6,14},{8,0},{10,2},{12,4},{14,6},{16,24},{18,... | collective-permute-start | bytes 1572872 | tf_op jit(solution)/shard_map/ppermute | solution.py:81
  853.8 46.0 %slice-start.2 = ((s8[8388608]{0:T(1024)(128)(4,1)}), s8[4194304]{0:T(1024)(128)(4,1)S(1)}, s32[]{:S(2)}) async-start(s8[8388608]{0:T(1024)(128)(4,1)} %bitcast.469), calls=%async_computation.2 | async-start | bytes 8388608
  855.9 43.9 %slice-start.3 = ((s8[8388608]{0:T(1024)(128)(4,1)}), s8[4194304]{0:T(1024)(128)(4,1)S(1)}, s32[]{:S(2)}) async-start(s8[8388608]{0:T(1024)(128)(4,1)} %bitcast.469), calls=%async_computation.3 | async-start | bytes 8388608
  856.0 77.1 %collective-permute-start.54 = (bf16[128,2,1024]{2,0,1:T(8,128)(2,1)}, bf16[128,2,1024]{2,0,1:T(8,128)(2,1)}, u32[]{:S(2)}, u32[]{:S(2)}) collective-permute-start(bf16[128,2,1024]{2,0,1:T(8,128)(2,1)} %fusion.61), channel_id=1, source_target_pairs={{0,2},{2,0},{4,6},{6,4},{8,10},{10,8},{12,14},{14,12},{16,18},{18,... | collective-permute-start | bytes 1572872 | tf_op jit(solution)/shard_map/ppermute | solution.py:81
  859.5 44.8 %collective-permute-start.29 = (bf16[256,2048]{1,0:T(8,128)(2,1)S(1)}, bf16[256,2048]{1,0:T(8,128)(2,1)S(1)}, u32[]{:S(2)}, u32[]{:S(2)}) collective-permute-start(bf16[256,2048]{1,0:T(8,128)(2,1)S(1)} %fusion.43), channel_id=1, source_target_pairs={{0,8},{2,10},{4,12},{6,14},{8,0},{10,2},{12,4},{14,6},{16,24},{18,... | collective-permute-start | bytes 3145736 | tf_op jit(solution)/shard_map/ppermute | solution.py:81
  902.5 23.0 %collective-permute-start.23 = (bf16[256,2048]{1,0:T(8,128)(2,1)S(1)}, bf16[256,2048]{1,0:T(8,128)(2,1)S(1)}, u32[]{:S(2)}, u32[]{:S(2)}) collective-permute-start(bf16[256,2048]{1,0:T(8,128)(2,1)S(1)} %fusion.42), channel_id=1, source_target_pairs={{0,8},{2,10},{4,12},{6,14},{8,0},{10,2},{12,4},{14,6},{16,24},{18,... | collective-permute-start | bytes 3145736 | tf_op jit(solution)/shard_map/ppermute | solution.py:81
  902.7 26.4 %copy-start.18 = (bf16[2,128,1,1024]{3,1,0,2:T(8,128)(2,1)}, bf16[2,128,1,1024]{3,1,0,2:T(8,128)(2,1)S(1)}, u32[]{:S(2)}) copy-start(bf16[2,128,1,1024]{3,1,0,2:T(8,128)(2,1)S(1)} %get-tuple-element.71) | copy-start | bytes 1572868
  903.6 33.8 %collective-permute-start.50 = (bf16[128,2,1024]{2,0,1:T(8,128)(2,1)}, bf16[128,2,1024]{2,0,1:T(8,128)(2,1)}, u32[]{:S(2)}, u32[]{:S(2)}) collective-permute-start(bf16[128,2,1024]{2,0,1:T(8,128)(2,1)} %fusion.65), channel_id=1, source_target_pairs={{0,2},{2,0},{4,6},{6,4},{8,10},{10,8},{12,14},{14,12},{16,18},{18,... | collective-permute-start | bytes 1572872 | tf_op jit(solution)/shard_map/ppermute | solution.py:81
  929.2 2.3 collective-permute-start.30
  931.5 4.5 collective-permute-start.31
  936.1 4.3 collective-permute-start.32
  940.4 4.3 collective-permute-start.33
  944.8 7.6 collective-permute-start.34
  (72 other events, 666.3 us)

commit v2 on v1

--- a/solution.py
+++ b/solution.py
@@ -1,14 +1,18 @@
+import functools
 import math
 
 import jax
 import jax.numpy as jnp
 from jax import lax
+from jax.experimental import pallas as pl
+from jax.experimental.pallas import tpu as pltpu
 from jax.sharding import PartitionSpec as P
 
 HEAD_DIM = 256
 ROT = 64
 BIT_X, BIT_Y, BIT_ZL, FIRST_ZH = 0, 1, 2, 3
 F32, BF16 = jnp.float32, jnp.bfloat16
+MESH = pl.DeviceIdType.MESH
 NN = (((1,), (0,)), ((), ()))
 NT = (((1,), (1,)), ((), ()))
 TN = (((0,), (0,)), ((), ()))
@@ -51,7 +55,7 @@
     return jnp.concatenate([rotated, rot_rest], axis=-1)
 
 
-def local(
+def local_pairs(
     layer_input,
     ln1_gain,
     ln1_bias,
@@ -258,7 +262,461 @@
     )
 
 
+NEAR = (1, 4, 8, 5, 9, 12, 13)
+
+
+def place():
+    return lax.axis_index("dp"), lax.axis_index("tensor")
+
+
+def feature_of(d):
+    return 2 * ((d >> BIT_ZL) & 1) + (d & 1)
+
+
+def greet(peers):
+    barrier = pltpu.get_barrier_semaphore()
+    for peer in peers:
+        pl.semaphore_signal(barrier, inc=1, device_id=peer, device_id_type=MESH)
+    pl.semaphore_wait(barrier, len(peers))
+
+
+class Copies:
+    def __init__(self, local_sems, send_sems, recv_sems):
+        self.sems = (local_sems, send_sems, recv_sems)
+        self.sent, self.kept = [], []
+
+    def remote(self, source, target, device):
+        k = len(self.sent)
+        copy = pltpu.make_async_remote_copy(
+            src_ref=source,
+            dst_ref=target,
+            send_sem=self.sems[1].at[k],
+            recv_sem=self.sems[2].at[k],
+            device_id=device,
+            device_id_type=MESH,
+        )
+        copy.start()
+        self.sent.append(copy)
+        return copy
+
+    def local(self, source, target):
+        copy = pltpu.make_async_copy(source, target, self.sems[0].at[len(self.kept)])
+        copy.start()
+        self.kept.append(copy)
+        return copy
+
+    def finish(self):
+        for copy in self.sent:
+            copy.wait_send()
+
+
+GATHER_SEQUENCE = "x0 s1 f1a x1 s2 x2 f1b x3 c0 sq sd f2 c1 c2 fq c3 fd x4 c4"
+
+
+def gather_kernel(
+    x_ref, c_ref, w1, w2, wq, wd, xg, cg, g1, g2, gq, gd, local_sems, send_sems, recv_sems
+):
+    me, core = place()
+    rows = w1.shape[0]
+    greet([(me ^ d, core) for d in NEAR] + [(me ^ 2, core), (me, 1 - core)])
+    copies = Copies(local_sems, send_sems, recv_sems)
+    weights = {"1": (w1, g1, 1), "2": (w2, g2, 0), "q": (wq, gq, 1), "d": (wd, gd, 0)}
+    tokens = {"x": (x_ref, xg), "c": (c_ref, cg)}
+
+    def block(w, dim, d):
+        size = w.shape[dim] // 4
+        cut = pl.ds(feature_of(d) * size, size)
+        return w.at[cut, :] if dim == 0 else w.at[:, cut]
+
+    def slot(g, dim, d):
+        cut = pl.ds(d * rows, rows)
+        return g.at[:, cut] if dim == 0 else g.at[cut, :]
+
+    state, last, kept = {}, [], []
+    for step in GATHER_SEQUENCE.split():
+        kind, name = step[0], step[1]
+        if kind == "s":
+            w, g, dim = weights[name]
+            kept.append(copies.local(block(w, dim, me), slot(g, dim, me)))
+            last.append(copies.remote(block(w, dim, me ^ 2), slot(g, dim, me), (me ^ 2, core)))
+            state[name] = [
+                copies.remote(block(w, dim, me ^ d), slot(g, dim, me), (me ^ d, core)) for d in NEAR
+            ]
+        elif kind == "f":
+            w, g, dim = weights[name]
+            part = {"a": (0, 3), "b": (3, 7)}.get(step[2:], (0, 7))
+            for k in range(*part):
+                state[name][k].wait_recv()
+                held = slot(g, dim, me ^ NEAR[k])
+                last.append(copies.remote(held, held, (me ^ 2, core)))
+        else:
+            source, g = tokens[kind]
+            if name == "0":
+                kept.append(copies.local(source, g.at[0, core]))
+                state[kind] = [
+                    copies.remote(source, g.at[2, core], (me ^ 4, core)),
+                    copies.remote(source, g.at[1, core], (me ^ 1, core)),
+                ]
+                last.append(copies.remote(source, g.at[0, core], (me, 1 - core)))
+            elif name == "1":
+                state[kind][0].wait_recv()
+                state[kind].append(copies.remote(g.at[2, core], g.at[3, core], (me ^ 1, core)))
+                last.append(copies.remote(g.at[2, core], g.at[2, core], (me, 1 - core)))
+            elif name == "2":
+                state[kind][1].wait_recv()
+                last.append(copies.remote(g.at[1, core], g.at[1, core], (me, 1 - core)))
+            elif name == "3":
+                state[kind][2].wait_recv()
+                last.append(copies.remote(g.at[3, core], g.at[3, core], (me, 1 - core)))
+    for copy in last:
+        copy.wait_recv()
+    for copy in kept:
+        copy.wait()
+    copies.finish()
+
+
+def in_hbm(count):
+    return [pl.BlockSpec(memory_space=pltpu.HBM)] * count
+
+
+def gather_all(x, c, w1, w2, wq, wd):
+    rows = w1.shape[0]
+    n = lax.axis_size("dp")
+    shapes = [(4, 2) + x.shape] * 2 + [
+        (rows * n, w1.shape[1] // 4),
+        (w2.shape[0] // 4, rows * n),
+        (rows * n, wq.shape[1] // 4),
+        (wd.shape[0] // 4, rows * n),
+    ]
+    return pl.pallas_call(
+        gather_kernel,
+        out_shape=[jax.ShapeDtypeStruct(s, BF16) for s in shapes],
+        in_specs=in_hbm(6),
+        out_specs=in_hbm(6),
+        scratch_shapes=[
+            pltpu.SemaphoreType.DMA((6,)),
+            pltpu.SemaphoreType.DMA((78,)),
+            pltpu.SemaphoreType.DMA((78,)),
+        ],
+        compiler_params=pltpu.CompilerParams(collective_id=1, has_side_effects=True),
+        name="gather_all",
+    )(x, c, w1, w2, wq, wd)
+
+
+def scatter_kernel(
+    g1, g2, gq, gd, p_out, p_in, vec,
+    f1, f2, fq, fd, out_keep, out_got, in_keep, in_got, vec_out,
+    r1, r2, rq, rd, s1, s2, sq, sd, a_out, a_in, c_out, c_in, x_out, x_in, vec_got,
+    local_sems, send_sems, recv_sems,
+):
+    me, core = place()
+    by, upper = (me >> 1) & 1, me >> 2
+    n = lax.axis_size("dp")
+    greet([(me ^ d, core) for d in NEAR] + [(me ^ 2, core), (me, 1 - core)])
+    copies = Copies(local_sems, send_sems, recv_sems)
+    grads = {
+        "1": (g1, f1, r1, s1, 0), "2": (g2, f2, r2, s2, 1), "q": (gq, fq, rq, sq, 0), "d": (gd, fd, rd, sd, 1)
+    }
+    rows = g1.shape[0] // n
+
+    def cut(ref, dim, start, size):
+        start = pl.multiple_of(start * size, size)
+        return ref.at[pl.ds(start, size), :] if dim == 0 else ref.at[:, pl.ds(start, size)]
+
+    token_sets = {"o": (p_out, out_keep, out_got, a_out, c_out, x_out), "i": (p_in, in_keep, in_got, a_in, c_in, x_in)}
+    state = {}
+    for name in "oi":
+        p, _, _, acc, got, _ = token_sets[name]
+        state[name] = (
+            [copies.remote(p.at[g, 1 - core], got.at[g], (me, 1 - core)) for g in range(4)],
+            [copies.local(p.at[g, core], acc.at[g]) for g in range(4)],
+        )
+    hops = [(me, 1 - core), (me ^ 2, core), (me ^ 1, core), (me ^ 4, core), (me ^ 8, core)]
+    vec_out[...] = vec[...]
+
+    def vector_hop(k):
+        copy = copies.remote(vec_out, vec_got.at[k], hops[k])
+        copies.sent.pop()
+        copies.sent.append(None)
+        copy.wait()
+        if k == 0:
+            vec_out[:8, :] += vec_got[0, :8, :]
+        else:
+            vec_out[...] += vec_got[k]
+
+    for name in "21qd":
+        g, f, r, s, dim = grads[name]
+        state[name] = [
+            copies.remote(
+                cut(g, dim, ((upper ^ u) * 2 + 1 - by), 2 * rows), cut(r, dim, u, 2 * rows), (me ^ 2, core)
+            )
+            for u in range(4)
+        ]
+    landed, kept = [], []
+
+    def forward(name):
+        g, f, r, s, dim = grads[name]
+        for u in (2, 3, 1, 0):
+            state[name][u].wait_recv()
+            mine = cut(g, dim, (upper ^ u) * 2 + by, 2 * rows)
+            total = mine[...].astype(F32) + cut(r, dim, u, 2 * rows)[...].astype(F32)
+            cut(s, dim, u, 2 * rows)[...] = total.astype(BF16)
+            for x in (1, 0):
+                piece = cut(s, dim, u * 2 + ((me & 1) ^ x), rows)
+                size = f.shape[2 - dim] // 4
+                start = feature_of(me) * size
+                target = f.at[me >> 3, :, pl.ds(start, size)] if dim == 0 else f.at[me >> 3, pl.ds(start, size), :]
+                if u == 0 and x == 0:
+                    kept.append(copies.local(piece, target))
+                else:
+                    landed.append(copies.remote(piece, target, (me ^ (4 * u + x), core)))
+
+    def tokens_core(name):
+        _, _, _, acc, got, over = token_sets[name]
+        sent, loaded = state[name]
+        for g in (1, 3, 0, 2):
+            sent[g].wait_recv()
+            loaded[g].wait()
+            acc[g] = (acc[g].astype(F32) + got[g].astype(F32)).astype(BF16)
+            if g & 1:
+                state[name + str(g)] = copies.remote(acc.at[g], over.at[g // 2], (me ^ 1, core))
+
+    def tokens_x(name):
+        _, keep, end, acc, got, over = token_sets[name]
+        state[name + "3"].wait_recv()
+        acc[2] = (acc[2].astype(F32) + over[1].astype(F32)).astype(BF16)
+        landed.append(copies.remote(acc.at[2], end, (me ^ 4, core)))
+        state[name + "1"].wait_recv()
+        acc[0] = (acc[0].astype(F32) + over[0].astype(F32)).astype(BF16)
+        kept.append(copies.local(acc.at[0], keep))
+
+    tokens_core("o")
+    vector_hop(0)
+    forward("2")
+    tokens_x("o")
+    vector_hop(1)
+    tokens_core("i")
+    forward("1")
+    tokens_x("i")
+    vector_hop(2)
+    forward("q")
+    vector_hop(3)
+    forward("d")
+    vector_hop(4)
+    for copy in landed:
+        copy.wait_recv()
+    for copy in kept:
+        copy.wait()
+    for copy in copies.sent:
+        if copy is not None:
+            copy.wait_send()
+
+
+def scatter_all(g1, g2, gq, gd, p_out, p_in, vec):
+    n = lax.axis_size("dp")
+    d_model = p_out.shape[-1]
+    rows, tok = d_model // n, p_out.shape[2]
+    shapes = [
+        (n // 8, rows, 4 * g1.shape[1]),
+        (n // 8, 4 * g2.shape[0], rows),
+        (n // 8, rows, 4 * gq.shape[1]),
+        (n // 8, 4 * gd.shape[0], rows),
+    ] + [(tok, d_model)] * 4
+    vmem = pl.BlockSpec(memory_space=pltpu.VMEM)
+    half = [
+        pltpu.VMEM((d_model // 2, g1.shape[1]), BF16),
+        pltpu.VMEM((g2.shape[0], d_model // 2), BF16),
+        pltpu.VMEM((d_model // 2, gq.shape[1]), BF16),
+        pltpu.VMEM((gd.shape[0], d_model // 2), BF16),
+    ]
+    return pl.pallas_call(
+        scatter_kernel,
+        out_shape=[jax.ShapeDtypeStruct(s, BF16) for s in shapes]
+        + [jax.ShapeDtypeStruct(vec.shape, F32)],
+        in_specs=[vmem] * 4 + in_hbm(2) + [vmem],
+        out_specs=in_hbm(8) + [vmem],
+        scratch_shapes=half
+        + half
+        + [pltpu.VMEM((4, tok, d_model), BF16)] * 4
+        + [pltpu.VMEM((2, tok, d_model), BF16)] * 2
+        + [
+            pltpu.VMEM((5,) + vec.shape, F32),
+            pltpu.SemaphoreType.DMA((20,)),
+            pltpu.SemaphoreType.DMA((64,)),
+            pltpu.SemaphoreType.DMA((64,)),
+        ],
+        compiler_params=pltpu.CompilerParams(
+            collective_id=2, has_side_effects=True, vmem_limit_bytes=60 << 20
+        ),
+        name="scatter_all",
+    )(g1, g2, gq, gd, p_out, p_in, vec)
+
+
+def local_fast(
+    layer_input,
+    ln1_gain,
+    ln1_bias,
+    ln2_gain,
+    ln2_bias,
+    qkv_weight,
+    qkv_bias,
+    dense_weight,
+    dense_bias,
+    fc1_weight,
+    fc1_bias,
+    fc2_weight,
+    fc2_bias,
+    seq_ids,
+    cotangent,
+):
+    me, core = place()
+    rows_here, d_model = layer_input.shape
+    feature = feature_of(me)
+
+    def swap(v, k):
+        return lax.ppermute(v, "dp", [(i, i ^ (1 << k)) for i in range(16)])
+
+    def take_block(v, parts):
+        return lax.dynamic_slice_in_dim(v, feature * (v.shape[0] // parts), v.shape[0] // parts, 0)
+
+    gains = [v.astype(F32) for v in (ln1_gain, ln1_bias, ln2_gain, ln2_bias)]
+    ids = jnp.stack([seq_ids, swap(seq_ids, BIT_X)], axis=0)
+    ids = jnp.concatenate([ids, swap(ids, BIT_ZL)], axis=0)
+    group_len = seq_ids.shape[0]
+    tokens = 4 * group_len
+
+    xg, cg, w_fc1, w_fc2, w_qkv, w_dense = gather_all(
+        layer_input, cotangent, fc1_weight, fc2_weight, qkv_weight, dense_weight
+    )
+    rows_in = xg.reshape(tokens, d_model)
+    cot = cg.reshape(tokens, d_model)
+
+    def normalize(v):
+        v = v.astype(F32)
+        center = v - jnp.mean(v, axis=-1, keepdims=True)
+        spread = jnp.mean(center * center, axis=-1, keepdims=True)
+        scale = lax.rsqrt(spread + 1e-05)
+        return center * scale, scale
+
+    xhat, _ = normalize(rows_in)
+    normed_attn = (xhat * gains[0] + gains[1]).astype(BF16)
+    normed_ffn = (xhat * gains[2] + gains[3]).astype(BF16)
+
+    ffn_input = mm(normed_ffn, w_fc1, NN) + take_block(fc1_bias, 4).astype(F32)
+    cdf = 0.5 * (1.0 + lax.erf(ffn_input * (1.0 / math.sqrt(2.0))))
+    density = jnp.exp(-0.5 * ffn_input * ffn_input) * (1.0 / math.sqrt(2.0 * math.pi))
+    hidden = (ffn_input * cdf).astype(BF16)
+    slope = cdf + ffn_input * density
+    grad_fc2 = mm(hidden, cot, TN).astype(BF16)
+    grad_ffn = (mm(cot, w_fc2, NT) * slope).astype(BF16)
+    grad_fc1 = mm(normed_ffn, grad_ffn, TN).astype(BF16)
+
+    qkv = mm(normed_attn, w_qkv, NN) + take_block(qkv_bias, 4).astype(F32)
+    qkv = qkv.reshape(4, group_len, 3 * HEAD_DIM)
+    cosines, sines = turn_angles(ids)
+    query = rotary(qkv[:, :, :HEAD_DIM], cosines, sines).astype(BF16)
+    keys = rotary(qkv[:, :, HEAD_DIM : 2 * HEAD_DIM], cosines, sines).astype(BF16)
+    values = qkv[:, :, 2 * HEAD_DIM :].astype(BF16)
+    places = jnp.arange(group_len, dtype=jnp.int32)
+    allowed = (ids[:, :, None] == ids[:, None, :]) & (places[None, None, :] <= places[None, :, None])
+    scores = jnp.einsum("gqd,gkd->gqk", query, keys, preferred_element_type=F32) * 0.0625
+    scores = jnp.where(allowed, scores, -1e30)
+    weights = jnp.exp(scores - jnp.max(scores, axis=-1, keepdims=True))
+    probability = weights / jnp.sum(weights, axis=-1, keepdims=True)
+    prob_low = probability.astype(BF16)
+    attended = jnp.einsum("gqk,gkd->gqd", prob_low, values, preferred_element_type=F32)
+    attended = attended.astype(BF16).reshape(tokens, HEAD_DIM)
+
+    partial_out = (mm(attended, w_dense, NN) + mm(hidden, w_fc2, NN)).astype(BF16)
+
+    grad_dense = mm(attended, cot, TN).astype(BF16)
+    grad_attended = mm(cot, w_dense, NT).astype(BF16).reshape(4, group_len, HEAD_DIM)
+    grad_prob = jnp.einsum("gqd,gkd->gqk", grad_attended, values, preferred_element_type=F32)
+    row_dot = jnp.sum(probability * grad_prob, axis=-1, keepdims=True)
+    grad_scores = (probability * (grad_prob - row_dot)).astype(BF16)
+    grad_query = jnp.einsum("gqk,gkd->gqd", grad_scores, keys, preferred_element_type=F32) * 0.0625
+    grad_keys = jnp.einsum("gqk,gqd->gkd", grad_scores, query, preferred_element_type=F32) * 0.0625
+    grad_values = jnp.einsum("gqk,gqd->gkd", prob_low, grad_attended, preferred_element_type=F32)
+    qkv_grad = jnp.concatenate(
+        [
+            rotary_back(grad_query, cosines, sines).astype(BF16),
+            rotary_back(grad_keys, cosines, sines).astype(BF16),
+            grad_values.astype(BF16),
+        ],
+        axis=-1,
+    ).reshape(tokens, 3 * HEAD_DIM)
+    grad_qkv = mm(normed_attn, qkv_grad, TN).astype(BF16)
+
+    attn_part = mm(qkv_grad, w_qkv, NT)
+    ffn_part = mm(grad_ffn, w_fc1, NT)
+    partial_in = (attn_part * gains[0] + ffn_part * gains[2]).astype(BF16)
+    cot_rows = cotangent.astype(F32)
+    small = jnp.stack(
+        [
+            jnp.sum(attn_part * xhat, axis=0),
+            jnp.sum(attn_part, axis=0),
+            jnp.sum(ffn_part * xhat, axis=0),
+            jnp.sum(ffn_part, axis=0),
+            jnp.sum(cot_rows, axis=0),
+        ]
+    )
+    columns = jnp.concatenate(
+        [jnp.sum(qkv_grad.astype(F32), axis=0), jnp.sum(grad_ffn.astype(F32), axis=0)]
+    )
+    columns = jnp.pad(columns, (0, d_model - columns.shape[0]))
+    ours = jnp.arange(8)[:, None] == feature
+    vec = jnp.concatenate(
+        [jnp.pad(small, ((0, 3), (0, 0))), jnp.where(ours, columns[None], 0.0)], axis=0
+    )
+
+    f1, f2, fq, fd, out_keep, out_got, in_keep, in_got, vec = scatter_all(
+        grad_fc1,
+        grad_fc2,
+        grad_qkv,
+        grad_dense,
+        partial_out.reshape(4, 2, rows_here, d_model),
+        partial_in.reshape(4, 2, rows_here, d_model),
+        vec,
+    )
+    out_fc1, out_fc2, out_qkv, out_dense = (
+        jnp.sum(v.astype(F32), axis=0) for v in (f1, f2, fq, fd)
+    )
+    layer_output = (
+        layer_input.astype(F32)
+        + (out_keep.astype(F32) + out_got.astype(F32))
+        + dense_bias.astype(F32)
+        + fc2_bias.astype(F32)
+    ).astype(BF16)
+    own_hat, own_scale = normalize(layer_input)
+    e_rows = in_keep.astype(F32) + in_got.astype(F32)
+    input_grad = cot_rows + own_scale * (
+        e_rows
+        - jnp.mean(e_rows, axis=-1, keepdims=True)
+        - own_hat * jnp.mean(e_rows * own_hat, axis=-1, keepdims=True)
+    )
+    blocks = vec[8:12]
+    out_qkv_bias = blocks[:, : 3 * HEAD_DIM].reshape(-1)
+    out_fc1_bias = blocks[:, 3 * HEAD_DIM : 3 * HEAD_DIM + w_fc1.shape[1]].reshape(-1)
+    return (
+        layer_output,
+        input_grad,
+        vec[0],
+        vec[1],
+        vec[2],
+        vec[3],
+        out_qkv,
+        out_qkv_bias,
+        out_dense,
+        vec[4],
+        out_fc1,
+        out_fc1_bias,
+        out_fc2,
+        vec[4],
+    )
+
+
 def solution(mesh):
+    local = local_fast if mesh.shape["dp"] == 16 else local_pairs
     in_specs = (
         P(("dp", "tensor"), None),
         P(),

time: 965 us -> 739 us (0.77)
  Pallas kernels: 0 us -> 462 us
  waiting for transfers between devices: 418 us -> 3.54 us
  local copies, waits for them, and re-layouts: 168 us -> 31.3 us
  other arithmetic: 135 us -> 72.9 us
  starting transfers between devices: 55.3 us -> 3.07 us
  matrix products: 176 us -> 158 us
    pallas_call x0 -> x2, Pallas kernels: none -> 462 us  [the longest x1 274 us: scatter_all(): pl.pallas_call(scatter_kernel, out_shape=[jax.ShapeDtypeStruct(s, BF16) f...]
    ppermute x55 -> x2, waiting for transfers between devices: 418 us -> 3.54 us  [swap(): return lax.ppermute(v, 'dp', [(i, i ^ 1 << k) for i in range(16)])]
    ppermute x55 -> x2, starting transfers between devices: 55.3 us -> 3.07 us  [swap(): return lax.ppermute(v, 'dp', [(i, i ^ 1 << k) for i in range(16)])]
    dot_general x3 -> x0, local copies, waits for them, and re-layouts: 37.2 us -> none  [mm(): return lax.dot_general(a, b, dims, preferred_element_type=F32)]
    another operation x49 -> x6, other arithmetic: 51.2 us -> 15.7 us  [the longest x42 34.1 us: ordered(): jnp.stack([jnp.where(b == 0, own, other), jnp.where(b == 0, other, own)],...]
    add x15 -> x1, other arithmetic: 31.6 us -> 3.17 us  [local_fast(): cot_rows + own_scale * (e_rows - jnp.mean(e_rows, axis=-1, keepdims=True)...]
    convert_element_type x14 -> x0, local copies, waits for them, and re-layouts: 23.7 us -> none  [the longest x4 8.85 us: scatter_grad(): pick(g, 1 - bit[BIT_Y], axis).astype(BF16)]
    slice x7 -> x3, local copies, waits for them, and re-layouts: 25 us -> 2.92 us  [the longest x1 1.81 us: local_fast(): vec[4]]
  transfers between devices with their start and end apart: 55 -> 2, of which waited for: 28 -> 1; matrix products, arithmetic and copies ran while one was open for 39% -> 16% of each run, Pallas kernels for 0% -> 26%
where the time goes in v2:
time: 739 us; the launch traced here: 732 us
  Pallas kernels  462 us (63%)
  matrix products  158 us (21%)
  other arithmetic  72.9 us (10%)
  local copies, waits for them, and re-layouts  31.3 us (4%)
    pallas_call x1, Pallas kernels, scatter_all(): pl.pallas_call(scatter_kernel, out_shape=[jax.ShapeDtypeStruct(s, BF16) f...  274 us
    pallas_call x1, Pallas kernels, gather_all(): pl.pallas_call(gather_kernel, out_shape=[jax.ShapeDtypeStruct(s, BF16) fo...  188 us
    dot_general x12, matrix products, mm(): return lax.dot_general(a, b, dims, preferred_element_type=F32)  140 us
    convert_element_type x2, other arithmetic, local_fast(): normed_attn = (xhat * gains[0] + gains[1]).astype(BF16)  17.1 us
    another operation x5, other arithmetic  15.7 us
  transfers between devices with their start and end apart: 2, of which 1 were waited for; matrix products, arithmetic and copies ran while one was open for 16% of the time, Pallas kernels for 26%

profile of v2, /device:TPU:0, one launch (start us, length us, event | category | flops | bytes accessed | tf_op | source)
XLA Modules:
  0.0 732.1 jit_solution(9300515923819855861)
XLA Ops:
  0.6 3.0 collective-permute-start
  3.7 1.4 convert_reduce_fusion.6
  5.2 1.6 fusion.16
  7.4 0.7 convert_element_type.154
  8.1 0.7 convert_element_type.155
  8.8 0.7 convert_element_type.146
  9.5 0.7 convert_element_type.147
  10.2 2.0 convert_reduce_fusion.7
  12.2 187.7 %gather_all.1 = (bf16[4,2,256,2048]{3,2,1,0:T(8,128)(2,1)}, bf16[4,2,256,2048]{3,2,1,0:T(8,128)(2,1)}, bf16[2048,1024]{1,0:T(8,128)(2,1)}, bf16[1024,2048]{1,0:T...) custom-call(bf16[256,2048]{1,0:T(8,128)(2,1)} %x_ref.1, bf16[256,2048]{1,0:T(8,128)(2,1)} %c_ref.1, ...), custom_call_target="tpu_custom_call" | custom-call | tf_op jit(solution)/shard_map/gather_all/pallas_call | solution.py:391
  199.9 4.7 convert_reduce_fusion
  204.6 1.0 copy-done
  205.6 2.4 multiply_reduce_fusion.2
  208.0 0.8 dynamic-slice_convert_fusion
  208.8 9.8 %add_convert_fusion.3 = bf16[4,2,256,2048]{3,2,1,0:T(8,128)(2,1)} fusion(bf16[4,2,256,2048]{3,2,1,0:T(8,128)(2,1)} %get-tuple-element.29, f32[2048]{0:T(1024)S(1)} %convert_element_type.155, f32[2048]{0:T(1024)S(1)} %convert_element_type.154, f32[4,2,256]{2,1,0:T(2,128)S(1)} %get-tuple-element.76, f32[4,2,256]{2,1,0:T(2,128)S(1)} %get-tuple-element.79), kind=kLoop, calls=%fused_computation.8 | loop fusion | flops 25165824 | bytes 16809984 | tf_op jit(solution)/shard_map/convert_element_type | solution.py:602
  218.7 7.3 add_convert_fusion.2
  225.9 6.9 broadcast_add_fusion
  233.2 2.4 copy-done.2
  235.6 1.7 copy-done.5
  237.3 2.4 fusion.51
  240.4 6.9 convolution_convert_fusion.4
  247.3 14.1 %multiply_convert_fusion = (bf16[2048,1024]{1,0:T(8,128)(2,1)S(1)}, f32[2048,1024]{1,0:T(8,128)}) fusion(f32[1024]{0:T(1024)S(1)} %dynamic-slice_convert_fusion.1, bf16[2048,2048]{1,0:T(8,128)(2,1)} %get-tuple-element.54, bf16[2048,1024]{1,0:T(8,128)(2,1)S(1)} %copy-done.39), kind=kOutput, calls=%fused_computation.20 | convolution fusion | flops 8602517504 | bytes 25169920 | tf_op jit(solution)/shard_map/dot_general | solution.py:22
  261.4 11.0 %convolution_convert_fusion.g2 = bf16[1024,2048]{1,0:T(8,128)(2,1)} fusion(bf16[2048,1024]{1,0:T(8,128)(2,1)S(1)} %get-tuple-element.80, bf16[2048,2048]{1,0:T(8,128)(2,1)S(1)} %bitcast.88), kind=kOutput, calls=%fused_computation.29 | convolution fusion | flops 8592031744 | bytes 16777216 | tf_op jit(solution)/shard_map/dot_general | solution.py:22
  272.4 11.7 %fusion.56 = f32[2048,2048]{1,0:T(8,128)} fusion(bf16[2048,1024]{1,0:T(8,128)(2,1)S(1)} %get-tuple-element.80, bf16[1024,2048]{1,0:T(8,128)(2,1)S(1)} %copy-done.40), kind=kOutput, calls=%fused_computation.143 | convolution fusion | flops 8589934592 | bytes 25165824 | tf_op jit(solution)/shard_map/dot_general | solution.py:22
  284.1 17.4 %convert_reduce_fusion.1 = (f32[1024]{0:T(1024)S(1)}, bf16[2048,1024]{1,0:T(8,128)(2,1)}) fusion(f32[2048,1024]{1,0:T(8,128)} %get-tuple-element.81, f32[1024]{0:T(1024)S(1)} %dynamic-slice_convert_fusion.1, bf16[2048,2048]{1,0:T(8,128)(2,1)S(1)} %bitcast.89, bf16[1024,2048]{1,0:T(8,128)(2,1)} %get-tuple-element.31), kind=kOutput, calls=%fused_computation.19 | convolution fusion | flops 8617196544 | bytes 25174016 | tf_op jit(solution)/shard_map/dot_general | solution.py:22
  301.6 12.5 %convolution_convert_fusion.1.g1 = bf16[2048,1024]{1,0:T(8,128)(2,1)} fusion(bf16[2048,2048]{1,0:T(8,128)(2,1)S(1)} %bitcast.95, bf16[2048,1024]{1,0:T(8,128)(2,1)} %get-tuple-element.87), kind=kOutput, calls=%fused_computation.30 | convolution fusion | flops 8592031744 | bytes 16777216 | tf_op jit(solution)/shard_map/dot_general | solution.py:22
  314.3 3.5 collective-permute-done.1
  318.0 1.2 reduce-window.6
  319.7 3.2 slice_negate_fusion.3
  322.9 7.0 fusion.34
  330.0 5.7 fusion.55
  335.7 4.5 convolution_convert_fusion.5
  340.2 2.1 multiply_reduce_fusion.3
  342.3 1.2 multiply_convert_fusion.1
  343.7 0.8 convolution_multiply_fusion
  345.0 1.2 convolution_multiply_fusion.1
  346.3 1.7 slice.190
  348.0 1.7 fusion.53
  349.6 1.4 slice.189
  351.0 1.7 fusion.52
  352.7 2.2 copy.51
  354.9 2.2 copy.53
  357.1 7.0 fusion.28
  364.1 1.2 copy.52
  365.3 1.9 copy.50
  367.3 1.0 constant_dynamic-update-slice_fusion.3
  368.2 1.2 constant_dynamic-update-slice_fusion.2
  369.4 1.2 constant_dynamic-update-slice_fusion
  370.6 3.2 fusion.26
  374.4 2.9 copy.54
  377.3 7.2 convolution_convert_fusion.3.gd
  384.5 9.6 %fusion.57 = f32[2048,2048]{1,0:T(8,128)} fusion(bf16[2048,768]{1,0:T(8,128)(2,1)S(1)} %bitcast.98, bf16[2048,768]{1,0:T(8,128)(2,1)S(1)} %copy-done.42), kind=kOutput, calls=%fused_computation.144 | convolution fusion | flops 6442450944 | bytes 23068672 | tf_op jit(solution)/shard_map/dot_general | solution.py:22
  394.1 8.5 %convolution_convert_fusion.2.gq = bf16[2048,768]{1,0:T(8,128)(2,1)} fusion(bf16[2048,2048]{1,0:T(8,128)(2,1)S(1)} %bitcast.93, bf16[2048,768]{1,0:T(8,128)(2,1)S(1)} %bitcast.99), kind=kOutput, calls=%fused_computation.31 | convolution fusion | flops 6444023808 | bytes 14680064 | tf_op jit(solution)/shard_map/dot_general | solution.py:22
  402.7 22.9 %fusion.49 = (f32[2048]{0:T(1024)S(1)}, f32[2048]{0:T(1024)S(1)}, bf16[2048,2048]{1,0:T(8,128)(2,1)}, f32[2048]{0:T(1024)S(1)}, f32[2048]{0:T(1024)S(1)}) fusion(f32[2048]{0:T(1024)S(1)} %bitcast.103, f32[2048]{0:T(1024)S(1)} %bitcast.101, bf16[4,2,256,2048]{3,2,1,0:T(8,128)(2,1)} %get-tuple-element.29, f32[2048]{0:T(1024)S(1)} %copy-done.26, ...), kind=kOutput, calls=%fused_computation.135 | convolution fusion | flops 8644452352 | bytes 42008576 | tf_op jit(solution)/shard_map/dot_general | solution.py:22
  425.6 11.3 %add_convert_fusion.1 = bf16[2048,2048]{1,0:T(8,128)(2,1)} fusion(f32[2048,2048]{1,0:T(8,128)} %fusion.56, bf16[2048,256]{1,0:T(8,128)(2,1)S(1)} %bitcast.97, bf16[256,2048]{1,0:T(8,128)(2,1)S(1)} %copy-done.22), kind=kOutput, calls=%fused_computation.6 | convolution fusion | flops 2155872256 | bytes 27262976 | tf_op jit(solution)/shard_map/dot_general | solution.py:22
  437.8 274.5 %scatter_all.1 = (bf16[2,128,4096]{2,1,0:T(8,128)(2,1)}, bf16[2,4096,128]{2,1,0:T(8,128)(2,1)}, bf16[2,128,3072]{2,1,0:T(8,128)(2,1)}, bf16[2,1024,128]{2,1,0:T(...) custom-call(bf16[2048,1024]{1,0:T(8,128)(2,1)} %convolution_convert_, ...), custom_call_target="tpu_custom_call" | custom-call | tf_op jit(solution)/shard_map/scatter_all/pallas_call | solution.py:532
  712.3 0.9 slice.132
  713.2 0.8 slice_bitcast_fusion
  713.9 1.8 fusion.54
  715.8 2.2 fusion.25
  719.2 2.1 convert_reduce_fusion.8
  721.3 3.0 convert_reduce_fusion.5
  724.4 1.7 convert_reduce_fusion.4
  726.1 1.7 convert_reduce_fusion.3
  728.1 3.2 convert_add_fusion.1
  (140 shorter events, 6.8 us)
Async XLA Ops:
  0.6 313.5 %collective-permute-start = (s32[512]{0:T(512)}, s32[512]{0:T(512)S(1)}, u32[]{:S(2)}, u32[]{:S(2)}) collective-permute-start(s32[512]{0:T(512)} %param.28), channel_id=1, source_target_pairs={{0,2},{2,0},{4,6},{6,4},{8,10},{10,8},{12,14},{14,12},{16,18},{18,... | collective-permute-start | bytes 6152 | tf_op jit(solution)/shard_map/ppermute | solution.py:577
  5.2 3.6 copy-start.33
  8.1 210.5 %copy-start.23 = (f32[2048]{0:T(1024)}, f32[2048]{0:T(1024)S(1)}, u32[]{:S(2)}) copy-start(f32[2048]{0:T(1024)S(1)} %convert_element_type.154) | copy-start | bytes 24580
  9.5 209.1 %copy-start.25 = (f32[2048]{0:T(1024)}, f32[2048]{0:T(1024)S(1)}, u32[]{:S(2)}) copy-start(f32[2048]{0:T(1024)S(1)} %convert_element_type.146) | copy-start | bytes 24580
  199.9 5.8 copy-start
  204.6 14.0 %copy-start.27 = (f32[4,2,2,128]{3,1,2,0:T(2,128)}, f32[4,2,2,128]{3,1,2,0:T(2,128)S(1)}, u32[]{:S(2)}) copy-start(f32[4,2,2,128]{3,1,2,0:T(2,128)S(1)} %copy.65) | copy-start | bytes 24580
  208.0 10.6 %copy-start.29 = (f32[4,2,2,128]{3,1,2,0:T(2,128)}, f32[4,2,2,128]{3,1,2,0:T(2,128)S(1)}, u32[]{:S(2)}) copy-start(f32[4,2,2,128]{3,1,2,0:T(2,128)S(1)} %copy.66) | copy-start | bytes 24580
  208.8 9.8 %slice-start = ((s8[8388608]{0:T(1024)(128)(4,1)}), s8[4194304]{0:T(1024)(128)(4,1)S(1)}, s32[]{:S(2)}) async-start(s8[8388608]{0:T(1024)(128)(4,1)} %bitcast.79), calls=%async_computation | async-start | bytes 8388608
  208.8 9.8 %slice-start.1 = ((s8[8388608]{0:T(1024)(128)(4,1)}), s8[4194304]{0:T(1024)(128)(4,1)S(1)}, s32[]{:S(2)}) async-start(s8[8388608]{0:T(1024)(128)(4,1)} %bitcast.79), calls=%async_computation.1 | async-start | bytes 8388608
  218.7 7.3 copy-start.41
  232.9 2.7 copy-start.2
  235.6 1.7 copy-start.5
  237.3 3.1 copy-start.21
  240.4 6.9 copy-start.39
  240.4 21.0 %slice-start.2 = ((s8[8388608]{0:T(1024)(128)(4,1)}), s8[4194304]{0:T(1024)(128)(4,1)S(1)}, s32[]{:S(2)}) async-start(s8[8388608]{0:T(1024)(128)(4,1)} %bitcast.86), calls=%async_computation.2 | async-start | bytes 8388608
  247.3 14.1 %slice-start.3 = ((s8[8388608]{0:T(1024)(128)(4,1)}), s8[4194304]{0:T(1024)(128)(4,1)S(1)}, s32[]{:S(2)}) async-start(s8[8388608]{0:T(1024)(128)(4,1)} %bitcast.86), calls=%async_computation.3 | async-start | bytes 8388608
  261.4 11.0 %copy-start.40 = (bf16[1024,2048]{1,0:T(8,128)(2,1)S(1)}, bf16[1024,2048]{1,0:T(8,128)(2,1)}, u32[]{:S(2)}) copy-start(bf16[1024,2048]{1,0:T(8,128)(2,1)} %get-tuple-element.31) | copy-start | bytes 12582916
  272.4 29.1 %slice-start.6 = ((s8[8388608]{0:T(1024)(128)(4,1)}), s8[4194304]{0:T(1024)(128)(4,1)S(1)}, s32[]{:S(2)}) async-start(s8[8388608]{0:T(1024)(128)(4,1)} %bitcast.94), calls=%async_computation.6 | async-start | bytes 8388608
  284.1 17.4 %slice-start.7 = ((s8[8388608]{0:T(1024)(128)(4,1)}), s8[4194304]{0:T(1024)(128)(4,1)S(1)}, s32[]{:S(2)}) async-start(s8[8388608]{0:T(1024)(128)(4,1)} %bitcast.94), calls=%async_computation.7 | async-start | bytes 8388608
  301.5 12.6 %copy-start.36 = (s32[512]{0:T(512)S(1)}, s32[512]{0:T(512)}, u32[]{:S(2)}) copy-start(s32[512]{0:T(512)} %param.28) | copy-start | bytes 6148
  301.6 12.7 %copy-start.37 = (bf16[2048]{0:T(1024)(128)(2,1)S(1)}, bf16[2048]{0:T(1024)(128)(2,1)}, u32[]{:S(2)}) copy-start(bf16[2048]{0:T(1024)(128)(2,1)} %param.23) | copy-start | bytes 12292
  301.6 12.7 %copy-start.38 = (bf16[2048]{0:T(1024)(128)(2,1)S(1)}, bf16[2048]{0:T(1024)(128)(2,1)}, u32[]{:S(2)}) copy-start(bf16[2048]{0:T(1024)(128)(2,1)} %param.27) | copy-start | bytes 12292
  314.2 3.7 collective-permute-start.1
  322.9 7.0 copy-start.10
  322.9 7.0 copy-start.12
  335.7 4.5 copy-start.7
  335.7 4.5 copy-start.43
  342.3 1.2 copy-start.13
  342.3 1.3 copy-start.18
  343.7 1.2 copy-start.11
  343.7 1.4 copy-start.17
  346.3 4.8 copy-start.3
  377.3 7.2 copy-start.14
  377.3 7.2 copy-start.42
  377.3 16.8 %slice-start.4 = ((s8[8388608]{0:T(1024)(128)(4,1)}), s8[4194304]{0:T(1024)(128)(4,1)S(1)}, s32[]{:S(2)}) async-start(s8[8388608]{0:T(1024)(128)(4,1)} %bitcast.91), calls=%async_computation.4 | async-start | bytes 8388608
  384.5 9.6 %slice-start.5 = ((s8[8388608]{0:T(1024)(128)(4,1)}), s8[4194304]{0:T(1024)(128)(4,1)S(1)}, s32[]{:S(2)}) async-start(s8[8388608]{0:T(1024)(128)(4,1)} %bitcast.91), calls=%async_computation.5 | async-start | bytes 8388608
  394.1 8.6 %copy-start.24 = (f32[2048]{0:T(1024)S(1)}, f32[2048]{0:T(1024)}, u32[]{:S(2)}) copy-start(f32[2048]{0:T(1024)} %copy-done.23) | copy-start | bytes 24580
  394.1 8.6 %copy-start.26 = (f32[2048]{0:T(1024)S(1)}, f32[2048]{0:T(1024)}, u32[]{:S(2)}) copy-start(f32[2048]{0:T(1024)} %copy-done.25) | copy-start | bytes 24580
  394.1 8.6 %copy-start.28 = (f32[4,2,2,128]{3,1,2,0:T(2,128)S(1)}, f32[4,2,2,128]{3,1,2,0:T(2,128)}, u32[]{:S(2)}) copy-start(f32[4,2,2,128]{3,1,2,0:T(2,128)} %copy-done.27) | copy-start | bytes 24580
  394.1 8.6 %copy-start.30 = (f32[4,2,2,128]{3,1,2,0:T(2,128)S(1)}, f32[4,2,2,128]{3,1,2,0:T(2,128)}, u32[]{:S(2)}) copy-start(f32[4,2,2,128]{3,1,2,0:T(2,128)} %copy-done.29) | copy-start | bytes 24580
  402.7 22.9 %copy-start.6 = (bf16[4,512,256]{2,1,0:T(8,128)(2,1)S(1)}, bf16[4,512,256]{2,1,0:T(8,128)(2,1)}, u32[]{:S(2)}) copy-start(bf16[4,512,256]{2,1,0:T(8,128)(2,1)} %convolution_convert_fusion.5) | copy-start | bytes 3145732
  402.7 22.9 %copy-start.22 = (bf16[256,2048]{1,0:T(8,128)(2,1)S(1)}, bf16[256,2048]{1,0:T(8,128)(2,1)}, u32[]{:S(2)}) copy-start(bf16[256,2048]{1,0:T(8,128)(2,1)} %get-tuple-element.34) | copy-start | bytes 3145732
  425.6 11.4 %copy-start.31 = (f32[2048]{0:T(1024)S(1)}, f32[2048]{0:T(1024)}, u32[]{:S(2)}) copy-start(f32[2048]{0:T(1024)} %convert_reduce_fusion.7) | copy-start | bytes 24580
  437.8 278.0 %copy-start.1 = (bf16[256,2048]{1,0:T(8,128)(2,1)S(1)}, bf16[256,2048]{1,0:T(8,128)(2,1)}, u32[]{:S(2)}) copy-start(bf16[256,2048]{1,0:T(8,128)(2,1)} %x_ref.1) | copy-start | bytes 3145732
  437.8 278.0 %copy-start.34 = (f32[256]{0:T(256)S(1)}, f32[256]{0:T(256)}, u32[]{:S(2)}) copy-start(f32[256]{0:T(256)} %copy-done.33) | copy-start | bytes 3076
  437.8 278.0 %copy-start.35 = (f32[256]{0:T(256)S(1)}, f32[256]{0:T(256)}, u32[]{:S(2)}) copy-start(f32[256]{0:T(256)} %add_rsqrt_fusion.1) | copy-start | bytes 3076
  712.3 12.1 %copy-start.16 = (bf16[2,128,4096]{2,1,0:T(8,128)(2,1)S(1)}, bf16[2,128,4096]{2,1,0:T(8,128)(2,1)}, u32[]{:S(2)}) copy-start(bf16[2,128,4096]{2,1,0:T(8,128)(2,1)} %get-tuple-element.42) | copy-start | bytes 6291460
  715.7 15.6 %copy-start.32 = (f32[1,2048]{1,0:T(1,128)}, f32[1,2048]{1,0:T(1,128)S(1)}, u32[]{:S(2)}) copy-start(f32[1,2048]{1,0:T(1,128)S(1)} %get-tuple-element.71) | copy-start | bytes 24580
  719.2 6.8 copy-start.15
  724.3 3.4 copy-start.4
  724.3 3.4 copy-start.8
  724.3 3.4 copy-start.9
  724.3 3.4 copy-start.19
  724.4 3.8 copy-start.20

commit v3 on v1

--- a/solution.py
+++ b/solution.py
@@ -2,13 +2,17 @@
 
 import jax
 import jax.numpy as jnp
+import numpy as np
 from jax import lax
+from jax.experimental import pallas as pl
+from jax.experimental.pallas import tpu as pltpu
 from jax.sharding import PartitionSpec as P
 
 HEAD_DIM = 256
 ROT = 64
 BIT_X, BIT_Y, BIT_ZL, FIRST_ZH = 0, 1, 2, 3
 F32, BF16 = jnp.float32, jnp.bfloat16
+MESH = pl.DeviceIdType.MESH
 NN = (((1,), (0,)), ((), ()))
 NT = (((1,), (1,)), ((), ()))
 TN = (((0,), (0,)), ((), ()))
@@ -51,7 +55,7 @@
     return jnp.concatenate([rotated, rot_rest], axis=-1)
 
 
-def local(
+def local_pairs(
     layer_input,
     ln1_gain,
     ln1_bias,
@@ -258,7 +262,596 @@
     )
 
 
+NEAR = (1, 4, 8, 5, 9, 12, 13)
+FAR_FIRST = (2, 3, 1, 0)
+TILE = 256
+ORDER = """
+g0 x0 s1 L0o f1a x1 x2 c0 s2 L2o L1o f1b x3 L3o L0p c1 c2 L2p L1p L3p W1 Pa f2a c3 Pb f2b sq sd C
+G2 W2 H fq G1 fd r2 A0 r1 A2 Gd Gq o0 rd rq o1 o2 i0 i1 i2 v
+"""
+
+
+def place():
+    return lax.axis_index("dp"), lax.axis_index("tensor")
+
+
+def feature_of(d):
+    return 2 * ((d >> BIT_ZL) & 1) + (d & 1)
+
+
+def greet(peers):
+    barrier = pltpu.get_barrier_semaphore()
+    for peer in peers:
+        pl.semaphore_signal(barrier, inc=1, device_id=peer, device_id_type=MESH)
+    pl.semaphore_wait(barrier, len(peers))
+
+
+class Copies:
+    def __init__(self, local_sems, send_sems, recv_sems):
+        self.sems = (local_sems, send_sems, recv_sems)
+        self.count, self.open, self.locals = 0, [], 0
+
+    def remote(self, source, target, device):
+        copy = pltpu.make_async_remote_copy(
+            src_ref=source,
+            dst_ref=target,
+            send_sem=self.sems[1].at[self.count],
+            recv_sem=self.sems[2].at[self.count],
+            device_id=device,
+            device_id_type=MESH,
+        )
+        copy.start()
+        self.count += 1
+        self.open.append(copy)
+        return copy
+
+    def local(self, source, target):
+        copy = pltpu.make_async_copy(source, target, self.sems[0].at[self.locals])
+        copy.start()
+        self.locals += 1
+        return copy
+
+    def now(self, *pairs):
+        for copy in [self.local(*pair) for pair in pairs]:
+            copy.wait()
+
+    def finish(self):
+        for copy in self.open:
+            copy.wait_send()
+
+
+def rows_at(start, size):
+    return pl.ds(pl.multiple_of(start * size, size), size)
+
+
+def fold(v):
+    return jnp.sum(v.reshape(v.shape[0] // 8, 8, v.shape[1]), axis=0)
+
+
+def rope(v, tables, sign):
+    first = v[:, :128]
+    turned = pltpu.roll(first, 96, 1) * tables[1] + pltpu.roll(first, 32, 1) * tables[2]
+    return jnp.concatenate([first * tables[0] + sign * turned, v[:, 128:]], axis=1)
+
+
+def layer_kernel(
+    x_ref, c_ref, w1, w2, wq, wd, flag, norms, turns,
+    f1, f2, fq, fd, out_keep, out_got, in_keep, in_got, vec,
+    xg, cg, g1, g2, gq, gd, na, r1, r2, rq, rd, co, ci, xo, xi, flags,
+    big1, big2, wa, wb, wqv, wdv, hid, gf, qkv, att, d1, d2, dq, dd, xt, st, stats, sums, cols, vec_got, fl,
+    local_sems, send_sems, recv_sems,
+):
+    me, core = place()
+    by, upper, mine = (me >> 1) & 1, me >> 2, feature_of(me)
+    rows = w1.shape[0]
+    d_model = x_ref.shape[1]
+    greet([(me ^ d, core) for d in NEAR] + [(me ^ 2, core), (me, 1 - core)])
+    copies = Copies(local_sems, send_sems, recv_sems)
+    weights = {"1": (w1, g1, 1), "2": (w2, g2, 0), "q": (wq, gq, 1), "d": (wd, gd, 0)}
+    tokens = {"x": (x_ref, xg), "c": (c_ref, cg)}
+    grads = {"1": (d1, f1, r1, 0), "2": (d2, f2, r2, 1), "q": (dq, fq, rq, 0), "d": (dd, fd, rd, 1)}
+    state, kept, landed = {}, [], []
+    pieces = {name: [] for name in weights}
+
+    def block(w, dim, d):
+        size = w.shape[dim] // 4
+        cut = pl.ds(feature_of(d) * size, size)
+        return w.at[cut, :] if dim == 0 else w.at[:, cut]
+
+    def slot(g, dim, d):
+        cut = pl.ds(d * rows, rows)
+        return g.at[:, cut] if dim == 0 else g.at[cut, :]
+
+    def send_flag():
+        kept.append(copies.local(flag, flags.at[0]))
+        state["flags"] = [copies.remote(flag, flags.at[k], (me ^ d, core)) for k, d in ((1, 1), (2, 4), (3, 5))]
+
+    def send_weight(name):
+        w, g, dim = weights[name]
+        pieces[name].append(copies.local(block(w, dim, me), slot(g, dim, me)))
+        pieces[name].append(copies.remote(block(w, dim, me ^ 2), slot(g, dim, me), (me ^ 2, core)))
+        state[name] = [copies.remote(block(w, dim, me ^ d), slot(g, dim, me), (me ^ d, core)) for d in NEAR]
+
+    def forward_weight(name, part):
+        w, g, dim = weights[name]
+        for k in range(*{"a": (0, 3), "b": (3, 7)}.get(part, (0, 7))):
+            state[name][k].wait_recv()
+            held = slot(g, dim, me ^ NEAR[k])
+            pieces[name].append(copies.remote(held, held, (me ^ 2, core)))
+
+    def weight_ready(name):
+        for copy in pieces[name]:
+            if copy is pieces[name][0]:
+                copy.wait()
+            else:
+                copy.wait_recv()
+
+    def token_step(kind, step):
+        source, g = tokens[kind]
+        if step == "0":
+            state[kind] = [
+                copies.remote(source, g.at[2, core], (me ^ 4, core)),
+                copies.remote(source, g.at[1, core], (me ^ 1, core)),
+            ]
+            state[kind + "p0"] = copies.remote(source, g.at[0, core], (me, 1 - core))
+        elif step == "1":
+            state[kind][0].wait_recv()
+            state[kind].append(copies.remote(g.at[2, core], g.at[3, core], (me ^ 1, core)))
+            state[kind + "p2"] = copies.remote(g.at[2, core], g.at[2, core], (me, 1 - core))
+        elif step == "2":
+            state[kind][1].wait_recv()
+            state[kind + "p1"] = copies.remote(g.at[1, core], g.at[1, core], (me, 1 - core))
+        elif step == "3":
+            state[kind][2].wait_recv()
+            state[kind + "p3"] = copies.remote(g.at[3, core], g.at[3, core], (me, 1 - core))
+
+    def normalize(rel, half):
+        if half == "o":
+            which = core
+            copies.now((x_ref if rel == 0 else xg.at[rel, core], xt.at[0]))
+        else:
+            which = 1 - core
+            state["xp%d" % rel].wait_recv()
+            copies.now((xg.at[rel, which], xt.at[0]))
+        tile = rel * 2 + which
+
+        @pl.loop(0, TILE // 32)
+        def _(k):
+            r = rows_at(k, 32)
+            here = rows_at(tile * (TILE // 32) + k, 32)
+            v = xt[0, r, :].astype(F32)
+            mean = jnp.mean(v, axis=-1, keepdims=True)
+            center = v - mean
+            scale = lax.rsqrt(jnp.mean(center * center, axis=-1, keepdims=True) + 1e-05)
+            xhat = center * scale
+            xt[1, r, :] = (xhat * norms[0:1, :] + norms[1:2, :]).astype(BF16)
+            big1[here, :] = (xhat * norms[2:3, :] + norms[3:4, :]).astype(BF16)
+            stats[here, 0:1] = mean
+            stats[here, 1:2] = scale
+
+        copies.now((xt.at[1], na.at[rows_at(tile, TILE), :]))
+
+    def up(lo, hi):
+        @pl.loop(lo, hi)
+        def _(i):
+            r = rows_at(i, TILE)
+            for j in range(0, wa.shape[1], 512):
+                c = slice(j, j + 512)
+                v = mm(big1[r, :], wa[:, c], NN) + norms[4:5, c]
+                cdf = 0.5 * (1.0 + lax.erf(v * (1.0 / math.sqrt(2.0))))
+                density = jnp.exp(-0.5 * v * v) * (1.0 / math.sqrt(2.0 * math.pi))
+                hid[r, c] = (v * cdf).astype(BF16)
+                gf[r, c] = (cdf + v * density).astype(BF16)
+
+    def load_cotangent():
+        for k in range(4):
+            state["cp%d" % k].wait_recv()
+        pairs = [(c_ref, big2.at[rows_at(core, TILE), :])]
+        pairs += [(cg.at[0, 1 - core], big2.at[rows_at(1 - core, TILE), :])]
+        pairs += [
+            (cg.at[k, h], big2.at[(k * 2 + h) * TILE : (k * 2 + h + 1) * TILE, :])
+            for k in (1, 2, 3)
+            for h in (0, 1)
+        ]
+        copies.now(*pairs)
+
+        @pl.loop(0, TILE // 32)
+        def _(k):
+            part = fold(big2[rows_at(core * (TILE // 32) + k, 32), :].astype(F32))
+            sums[4] = jnp.where(k == 0, part, sums[4] + part)
+
+    def cut(ref, dim, start, size):
+        start = pl.multiple_of(start * size, size)
+        return ref.at[pl.ds(start, size), :] if dim == 0 else ref.at[:, pl.ds(start, size)]
+
+    def send_grad(name):
+        d, f, r, dim = grads[name]
+
+        def product(pair):
+            c = rows_at(pair, 2 * rows)
+            if name == "1":
+                d[c, :] = mm(big1[:, c], gf[...], TN).astype(BF16)
+            elif name == "q":
+                d[c, :] = mm(big1[:, c], qkv[...], TN).astype(BF16)
+            elif name == "2":
+                for j in (0, 512):
+                    d[j : j + 512, c] = mm(hid[:, j : j + 512], big2[:, c], TN).astype(BF16)
+            else:
+                d[:, c] = mm(att[...], big2[:, c], TN).astype(BF16)
+
+        state["r" + name] = {}
+        for u in FAR_FIRST:
+            pair = (upper ^ u) * 2 + 1 - by
+            product(pair)
+            state["r" + name][u] = copies.remote(
+                cut(d, dim, pair, 2 * rows), cut(r, dim, u, 2 * rows), (me ^ 2, core)
+            )
+
+        @pl.loop(0, 4)
+        def _(u):
+            product(u * 2 + by)
+
+    def forward_grad(name):
+        d, f, r, dim = grads[name]
+        for u in FAR_FIRST:
+            state["r" + name][u].wait_recv()
+            own = cut(d, dim, (upper ^ u) * 2 + by, 2 * rows)
+            if name == "2":
+                stage = st
+            else:
+                stage = xt.at[0, :, pl.ds(0, d.shape[1] if dim == 0 else 2 * rows)]
+            copies.now((cut(r, dim, u, 2 * rows), stage))
+            own[...] = (own[...].astype(F32) + stage[...].astype(F32)).astype(BF16)
+            for x in (1, 0):
+                piece = cut(d, dim, (upper ^ u) * 4 + by * 2 + ((me & 1) ^ x), rows)
+                size = f.shape[2 - dim] // 4
+                c = pl.ds(mine * size, size)
+                target = f.at[me >> 3, :, c] if dim == 0 else f.at[me >> 3, c, :]
+                if u == 0 and x == 0:
+                    kept.append(copies.local(piece, target))
+                else:
+                    landed.append(copies.remote(piece, target, (me ^ (4 * u + x), core)))
+
+    def hidden_grad():
+        cols[...] = jnp.zeros_like(cols)
+
+        @pl.loop(0, 8)
+        def _(i):
+            r = rows_at(i, TILE)
+            for j in range(0, gf.shape[1], 512):
+                c = slice(j, j + 512)
+                g = (mm(big2[r, :], wb[c, :], NT) * gf[r, c].astype(F32)).astype(BF16)
+                gf[r, c] = g
+                at = slice(3 * HEAD_DIM + j, 3 * HEAD_DIM + j + 512)
+                cols[:, at] += fold(g.astype(F32))
+
+    def attention(lo, hi):
+        @pl.loop(lo, hi)
+        def _(number):
+            attend(number)
+
+    def attend(number):
+        size, half = 2 * TILE, TILE
+        quarter = size // 4
+
+        def at_rows(start, length):
+            return pl.ds(pl.multiple_of(number * size + start, TILE), length)
+
+        three = fl[number, 0:1, 0:1] > 0.5
+        tables = []
+        for k in range(3):
+            again = jnp.concatenate([turns[k, :quarter], turns[k, : 2 * quarter], turns[k, :quarter]], axis=0)
+            tables.append(jnp.where(three, again, turns[k]))
+        everything = at_rows(0, size)
+        full = mm(big1[everything, :], wqv[...], NN) + norms[5:6, : 3 * HEAD_DIM]
+        qkv[everything, :HEAD_DIM] = rope(full[:, :HEAD_DIM], tables, 1.0).astype(BF16)
+        qkv[everything, HEAD_DIM : 2 * HEAD_DIM] = rope(full[:, HEAD_DIM : 2 * HEAD_DIM], tables, 1.0).astype(BF16)
+        qkv[everything, 2 * HEAD_DIM :] = full[:, 2 * HEAD_DIM :].astype(BF16)
+        grad_q, grad_k, grad_v = {}, {}, {}
+        for i in (1, 0):
+            r = at_rows(i * half, half)
+            seen = (i + 1) * half
+            q = qkv[r, :HEAD_DIM]
+            k = qkv[at_rows(0, seen), HEAD_DIM : 2 * HEAD_DIM]
+            v = qkv[at_rows(0, seen), 2 * HEAD_DIM :]
+            ti = lax.broadcasted_iota(jnp.int32, (half, seen), 0) + i * half
+            tj = lax.broadcasted_iota(jnp.int32, (half, seen), 1)
+            part_i = (ti >= quarter).astype(jnp.int32) + (ti >= 3 * quarter).astype(jnp.int32)
+            part_j = (tj >= quarter).astype(jnp.int32) + (tj >= 3 * quarter).astype(jnp.int32)
+            s = mm(q, k, NT) * 0.0625
+            s = jnp.where(tj <= ti, s, -1e30)
+            s = jnp.where((part_i != part_j) & three, -1e30, s)
+            w = jnp.exp(s - jnp.max(s, axis=-1, keepdims=True))
+            p = w / jnp.sum(w, axis=-1, keepdims=True)
+            low = p.astype(BF16)
+            att[r, :] = mm(low, v, NN).astype(BF16)
+            ga = mm(big2[r, :], wdv[...], NT).astype(BF16)
+            gp = mm(ga, v, NT)
+            gs = (p * (gp - jnp.sum(p * gp, axis=-1, keepdims=True))).astype(BF16)
+            grad_q[i] = mm(gs, k, NN) * 0.0625
+            grad_k[i] = mm(gs, q, TN) * 0.0625
+            grad_v[i] = mm(low, ga, TN)
+
+        def put(k, total):
+            total = total.astype(BF16)
+            at = slice(k * HEAD_DIM, (k + 1) * HEAD_DIM)
+            qkv[everything, at] = total
+            cols[:, at] += fold(total.astype(F32))
+
+        def joined(one, two):
+            return jnp.concatenate([one + two[:half], two[half:]], axis=0)
+
+        put(0, rope(jnp.concatenate([grad_q[0], grad_q[1]], axis=0), tables, -1.0))
+        put(1, rope(joined(grad_k[0], grad_k[1]), tables, -1.0))
+        put(2, joined(grad_v[0], grad_v[1]))
+
+    sets = {"o": (out_keep, out_got, big1, co, xo), "i": (in_keep, in_got, big2, ci, xi)}
+
+    def token_product(name, rel, which, buffer, at, received):
+        tile = rel * 2 + which
+        r = rows_at(tile, TILE)
+        if name == "i":
+            copies.now((x_ref if rel == 0 and received else xg.at[rel, which], xt.at[0]))
+
+        @pl.loop(0, d_model // 512)
+        def _(j):
+            c = rows_at(j, 512)
+            if name == "o":
+                total = mm(att[r, :], wdv[:, c], NN) + mm(hid[r, :], wb[:, c], NN)
+            else:
+                a = mm(qkv[r, :], wqv[c, :], NT)
+                f = mm(gf[r, :], wa[c, :], NT)
+                xhat = (xt[0, :, c].astype(F32) - stats[r, 0:1]) * stats[r, 1:2]
+                sums[0, :, c] += fold(a * xhat)
+                sums[1, :, c] += fold(a)
+                sums[2, :, c] += fold(f * xhat)
+                sums[3, :, c] += fold(f)
+                total = a * norms[0:1, c] + f * norms[2:3, c]
+            if received:
+                total = total + xt[1, :, c].astype(F32)
+            buffer[at * TILE : (at + 1) * TILE, c] = total.astype(BF16)
+
+    def tile_of(buffer, at):
+        return buffer.at[at * TILE : (at + 1) * TILE, :]
+
+    def token_sum(name, step):
+        keep, end, buffer, got, over = sets[name]
+        if step == "0":
+            if name == "i":
+                sums[0:4] = jnp.zeros_like(sums[0:4])
+            state[name] = {}
+            for rel in (1, 3, 2, 0):
+                token_product(name, rel, 1 - core, buffer, rel, False)
+                state[name][rel] = copies.remote(tile_of(buffer, rel), got.at[rel], (me, 1 - core))
+        elif step == "1":
+            for rel in (3, 1, 2, 0):
+                state[name][rel].wait_recv()
+                copies.now((got.at[rel], xt.at[1]))
+                token_product(name, rel, core, buffer, 4 + rel, True)
+                if rel & 1:
+                    state[name + str(rel)] = copies.remote(
+                        tile_of(buffer, 4 + rel), over.at[rel // 2], (me ^ 1, core)
+                    )
+        else:
+            for rel in (2, 0):
+                state[name + str(rel + 1)].wait_recv()
+                copies.now((over.at[rel // 2], xt.at[1]))
+
+                @pl.loop(0, TILE // 32)
+                def _(k):
+                    r = rows_at((4 + rel) * (TILE // 32) + k, 32)
+                    buffer[r, :] = (
+                        buffer[r, :].astype(F32) + xt[1, rows_at(k, 32), :].astype(F32)
+                    ).astype(BF16)
+
+                if rel == 2:
+                    landed.append(copies.remote(tile_of(buffer, 6), end, (me ^ 4, core)))
+                else:
+                    kept.append(copies.local(tile_of(buffer, 4), keep))
+
+    def vectors():
+        vec[...] = jnp.zeros_like(vec)
+        for k in range(5):
+            vec[k : k + 1, :] = jnp.sum(sums[k], axis=0, keepdims=True)
+        for k in range(4):
+            ours = jnp.where(mine == k, 1.0, 0.0)
+            vec[8 + k : 9 + k, :] = jnp.sum(cols[...], axis=0, keepdims=True) * ours
+        hops = [(me, 1 - core), (me ^ 2, core), (me ^ 1, core), (me ^ 4, core), (me ^ 8, core)]
+        for k, device in enumerate(hops):
+            copy = copies.remote(vec, vec_got.at[k], device)
+            copies.open.pop()
+            copy.wait()
+            if k == 0:
+                vec[:8, :] += vec_got[0, :8, :]
+            else:
+                vec[...] += vec_got[k]
+
+    for op in ORDER.split():
+        kind, rest = op[0], op[1:]
+        if kind == "g":
+            send_flag()
+        elif kind in "xc":
+            token_step(kind, rest)
+        elif kind == "s":
+            send_weight(rest)
+        elif kind == "f":
+            forward_weight(rest[0], rest[1:])
+        elif kind == "L":
+            normalize(int(rest[0]), rest[1])
+        elif kind == "W":
+            weight_ready(rest)
+            copies.now((g1, wa) if rest == "1" else (g2, wb))
+        elif kind == "P":
+            up(*((0, 4) if rest == "a" else (4, 8)))
+        elif kind == "C":
+            load_cotangent()
+        elif kind == "G":
+            send_grad(rest)
+        elif kind == "H":
+            hidden_grad()
+        elif kind == "r":
+            forward_grad(rest)
+        elif kind == "A":
+            if rest == "0":
+                for name in "qd":
+                    weight_ready(name)
+                for copy in state["flags"]:
+                    copy.wait_recv()
+                kept.pop(0).wait()
+                copies.now((gq, wqv), (gd, wdv), (na, big1), (flags, fl))
+            attention(int(rest), int(rest) + 2)
+        elif kind in "oi":
+            token_sum(kind, rest)
+        else:
+            vectors()
+    for copy in landed:
+        copy.wait_recv()
+    for copy in kept:
+        copy.wait()
+    copies.finish()
+
+
+def turn_tables(group_len):
+    inverse = np.exp(
+        np.arange(ROT // 2, dtype=np.float32) * np.float32(-2.0 * math.log(10000.0) / ROT)
+    ).astype(np.float32)
+    angles = np.arange(group_len).astype(np.float32)[:, None] * inverse
+    tables = np.zeros((3, group_len, 128), np.float32)
+    tables[0] = 1.0
+    tables[0, :, : ROT // 2] = tables[0, :, ROT // 2 : ROT] = np.cos(angles)
+    tables[1, :, : ROT // 2] = -np.sin(angles)
+    tables[2, :, ROT // 2 : ROT] = np.sin(angles)
+    return tables
+
+
+def layer_call(x, c, w1, w2, wq, wd, flag, norms, turns):
+    n = lax.axis_size("dp")
+    tok, d = x.shape
+    rows, u1, uq, ud = w1.shape[0], w1.shape[1] // 4, wq.shape[1] // 4, wd.shape[0] // 4
+    many = 8 * tok
+    vmem = pl.BlockSpec(memory_space=pltpu.VMEM)
+    hbm = pl.BlockSpec(memory_space=pltpu.HBM)
+
+    def low(*shape):
+        return jax.ShapeDtypeStruct(shape, BF16)
+
+    results = [low(n // 8, rows, 4 * u1), low(n // 8, 4 * u1, rows), low(n // 8, rows, 4 * uq), low(n // 8, 4 * ud, rows)]
+    results += [low(tok, d)] * 4 + [jax.ShapeDtypeStruct((16, d), F32)]
+    spare = [low(4, 2, tok, d)] * 2 + [low(d, u1), low(u1, d), low(d, uq), low(ud, d), low(many, d)]
+    spare += [low(d // 2, u1), low(u1, d // 2), low(d // 2, uq), low(ud, d // 2)]
+    spare += [low(4, tok, d)] * 2 + [low(2, tok, d)] * 2 + [jax.ShapeDtypeStruct((4, 8, 128), F32)]
+    scratch = [
+        (many, d), (many, d), (d, u1), (u1, d), (d, uq), (ud, d), (many, u1), (many, u1), (many, uq), (many, ud),
+        (d, u1), (u1, d), (d, uq), (ud, d), (2, tok, d), (u1, 2 * rows),
+    ]
+    flops = 2 * 3 * many * d * (2 * u1 + uq + ud)
+    return pl.pallas_call(
+        layer_kernel,
+        out_shape=results + spare,
+        in_specs=[hbm] * 7 + [vmem] * 2,
+        out_specs=[hbm] * 8 + [vmem] + [hbm] * len(spare),
+        scratch_shapes=[pltpu.VMEM(s, BF16) for s in scratch]
+        + [
+            pltpu.VMEM((many, 2), F32),
+            pltpu.VMEM((5, 8, d), F32),
+            pltpu.VMEM((8, d), F32),
+            pltpu.VMEM((5, 16, d), F32),
+            pltpu.VMEM((4, 8, 128), F32),
+            pltpu.SemaphoreType.DMA((96,)),
+            pltpu.SemaphoreType.DMA((144,)),
+            pltpu.SemaphoreType.DMA((144,)),
+        ],
+        compiler_params=pltpu.CompilerParams(
+            collective_id=1, has_side_effects=True, vmem_limit_bytes=65000 << 10
+        ),
+        cost_estimate=pl.CostEstimate(flops=flops, bytes_accessed=200 << 20, transcendentals=0),
+        name="layer",
+    )(x, c, w1, w2, wq, wd, flag, norms, turns)[:9]
+
+
+def local_fast(
+    layer_input,
+    ln1_gain,
+    ln1_bias,
+    ln2_gain,
+    ln2_bias,
+    qkv_weight,
+    qkv_bias,
+    dense_weight,
+    dense_bias,
+    fc1_weight,
+    fc1_bias,
+    fc2_weight,
+    fc2_bias,
+    seq_ids,
+    cotangent,
+):
+    me, core = place()
+    rows_here, d_model = layer_input.shape
+    feature = feature_of(me)
+    units, width = fc1_weight.shape[1] // 4, 3 * HEAD_DIM
+
+    def take_block(v, size):
+        return jnp.pad(lax.dynamic_slice_in_dim(v, feature * size, size, 0), (0, d_model - size))
+
+    zero = jnp.zeros_like(ln1_gain)
+    norms = jnp.stack(
+        [ln1_gain, ln1_bias, ln2_gain, ln2_bias, take_block(fc1_bias, units), take_block(qkv_bias, width), zero, zero]
+    ).astype(F32)
+    flag = jnp.broadcast_to(jnp.max(seq_ids) > 0, (8, 128)).astype(F32)
+    f1, f2, fq, fd, out_keep, out_got, in_keep, in_got, vec = layer_call(
+        layer_input,
+        cotangent,
+        fc1_weight,
+        fc2_weight,
+        qkv_weight,
+        dense_weight,
+        flag,
+        norms,
+        turn_tables(seq_ids.shape[0]),
+    )
+    out_fc1, out_fc2, out_qkv, out_dense = (
+        jnp.sum(v.astype(F32), axis=0) for v in (f1, f2, fq, fd)
+    )
+    own = layer_input.astype(F32)
+    layer_output = (
+        own
+        + (out_keep.astype(F32) + out_got.astype(F32))
+        + dense_bias.astype(F32)
+        + fc2_bias.astype(F32)
+    ).astype(BF16)
+    center = own - jnp.mean(own, axis=-1, keepdims=True)
+    scale = lax.rsqrt(jnp.mean(center * center, axis=-1, keepdims=True) + 1e-05)
+    xhat = center * scale
+    e_rows = in_keep.astype(F32) + in_got.astype(F32)
+    input_grad = cotangent.astype(F32) + scale * (
+        e_rows
+        - jnp.mean(e_rows, axis=-1, keepdims=True)
+        - xhat * jnp.mean(e_rows * xhat, axis=-1, keepdims=True)
+    )
+    blocks = vec[8:12]
+    out_qkv_bias = blocks[:, :width].reshape(-1)
+    out_fc1_bias = blocks[:, width : width + units].reshape(-1)
+    return (
+        layer_output,
+        input_grad,
+        vec[0],
+        vec[1],
+        vec[2],
+        vec[3],
+        out_qkv,
+        out_qkv_bias,
+        out_dense,
+        vec[4],
+        out_fc1,
+        out_fc1_bias,
+        out_fc2,
+        vec[4],
+    )
+
+
 def solution(mesh):
+    local = local_fast if mesh.shape["dp"] == 16 else local_pairs
     in_specs = (
         P(("dp", "tensor"), None),
         P(),

time: 965 us -> 586 us (0.61)
  Pallas kernels: 0 us -> 547 us
  waiting for transfers between devices: 418 us -> 0 us
  matrix products: 176 us -> 0 us
  local copies, waits for them, and re-layouts: 168 us -> 8.03 us
  other arithmetic: 135 us -> 17.6 us
  starting transfers between devices: 55.3 us -> 0 us
    pallas_call x0 -> x1, Pallas kernels: none -> 547 us  [layer_call(): pl.pallas_call(layer_kernel, out_shape=results + spare, in_specs=[hbm] *...]
    ppermute x55 -> x0, waiting for transfers between devices: 418 us -> none  [the longest x50 418 us: swap(): return lax.ppermute(v, 'dp', [(i, i ^ 1 << k) for i in range(n)])]
    dot_general x17 -> x0, matrix products: 170 us -> none  [the longest x12 158 us: mm(): return lax.dot_general(a, b, dims, preferred_element_type=F32)]
    ppermute x55 -> x0, starting transfers between devices: 55.3 us -> none  [the longest x50 55.2 us: swap(): return lax.ppermute(v, 'dp', [(i, i ^ 1 << k) for i in range(n)])]
    another operation x49 -> x0, other arithmetic: 51.2 us -> none  [the longest x42 34.1 us: ordered(): jnp.stack([jnp.where(b == 0, own, other), jnp.where(b == 0, other, own)],...]
    dot_general x3 -> x0, local copies, waits for them, and re-layouts: 37.2 us -> none  [mm(): return lax.dot_general(a, b, dims, preferred_element_type=F32)]
    slice x13 -> x2, local copies, waits for them, and re-layouts: 35.1 us -> 0.64 us  [the longest x1 0.63 us: local_fast(): vec[4]]
    add x15 -> x1, other arithmetic: 31.6 us -> 4.55 us  [local_fast(): cotangent.astype(F32)]
  transfers between devices with their start and end apart: 55 -> 0, of which waited for: 28 -> 0; matrix products, arithmetic and copies ran while one was open for 39% -> 0% of each run, Pallas kernels for 0% -> 0%
where the time goes in v3:
time: 586 us; the launch traced here: 575 us
  Pallas kernels  547 us (93%)
  other arithmetic  17.6 us (3%)
  local copies, waits for them, and re-layouts  8.03 us (1%)
    pallas_call x1, Pallas kernels, layer_call(): pl.pallas_call(layer_kernel, out_shape=results + spare, in_specs=[hbm] *...  547 us

profile of v3, /device:TPU:0, one launch (start us, length us, event | category | flops | bytes accessed | tf_op | source)
XLA Modules:
  0.0 574.7 jit_solution(3396176649590003308)
XLA Ops:
  0.7 0.7 dynamic_slice.6
  1.4 0.8 dynamic_slice.7
  2.1 0.7 stack.24
  2.8 0.7 stack.25
  3.5 0.7 stack.26
  4.2 0.7 stack.27
  4.9 0.1 stack.31
  5.0 0.6 convert_element_type.51.norms
  5.7 1.3 reduce_max.9
  7.6 0.6 broadcast_in_dim.2.flag
  8.2 547.1 %layer.1 = (bf16[2,128,4096]{2,1,0:T(8,128)(2,1)}, bf16[2,4096,128]{2,1,0:T(8,128)(2,1)}, bf16[2,128,3072]{2,1,0:T(8,128)(2,1)}, bf16[2,1024,128]{2,1,0:T(8,128)...) custom-call(bf16[256,2048]{1,0:T(8,128)(2,1)} %x_ref.1, ...), custom_call_target="tpu_custom_call" | custom-call | flops 77309411328 | bytes 209715200 | tf_op jit(solution)/shard_map/layer/pallas_call | solution.py:748
  555.4 0.0 copy-start
  555.4 0.0 copy-start.1
  555.4 1.6 convert_reduce_fusion.3
  557.0 0.0 copy-start.11
  557.0 0.0 copy-start.12
  557.0 0.0 copy-start.2
  557.0 0.0 copy-start.6
  557.0 0.0 copy-start.7
  557.1 1.8 fusion.8
  558.9 0.0 copy-done
  558.9 0.0 copy-done.1
  558.9 2.0 fusion.12
  560.8 0.0 copy-done.11
  560.9 0.0 copy-done.12
  560.9 0.0 copy-done.2
  560.9 0.0 copy-done.6
  560.9 0.0 copy-done.7
  560.9 0.0 copy-start.9
  560.9 0.0 copy-start.4
  560.9 4.5 fusion.7
  565.5 0.0 copy-done.9
  565.5 0.6 fusion.13
  566.1 0.0 copy-start.10
  566.1 0.6 copy.32
  566.7 0.6 reshape.56
  567.3 0.0 copy-done.4
  567.4 0.0 copy-start.3
  567.4 1.7 convert_reduce_fusion
  569.0 0.6 copy-done.3
  569.6 0.0 copy-start.5
  569.6 1.7 convert_reduce_fusion.1
  571.3 0.0 copy-start.8
  571.3 0.0 copy-done.5
  571.3 1.5 convert_reduce_fusion.2
  572.8 0.0 copy-done.8
  572.8 0.9 convert_reduce_fusion.4
  573.6 0.0 copy-done.10
  573.6 0.6 copy.34
  (12 shorter events, 0.1 us)
Async XLA Ops:
  555.4 3.5 copy-start
  555.4 3.5 copy-start.1
  557.0 3.8 copy-start.11
  557.0 3.9 copy-start.12
  557.0 3.9 copy-start.2
  557.0 3.9 copy-start.6
  557.0 3.9 copy-start.7
  560.9 4.6 copy-start.9
  560.9 6.4 %copy-start.4 = (bf16[2,4096,128]{2,1,0:T(8,128)(2,1)S(1)}, bf16[2,4096,128]{2,1,0:T(8,128)(2,1)}, u32[]{:S(2)}) copy-start(bf16[2,4096,128]{2,1,0:T(8,128)(2,1)} %get-tuple-element.31) | copy-start | bytes 6291460
  566.1 7.5 %copy-start.10 = (f32[1,2048]{1,0:T(1,128)}, f32[1,2048]{1,0:T(1,128)S(1)}, u32[]{:S(2)}) copy-start(f32[1,2048]{1,0:T(1,128)S(1)} %get-tuple-element.36) | copy-start | bytes 24580
  567.4 2.2 copy-start.3
  569.6 1.7 copy-start.5
  571.3 1.5 copy-start.8

commit v4 on v3

--- a/solution.py
+++ b/solution.py
@@ -262,12 +262,13 @@
     )
 
 
-NEAR = (1, 4, 8, 5, 9, 12, 13)
-FAR_FIRST = (2, 3, 1, 0)
 TILE = 256
 ORDER = """
-g0 x0 s1 L0o f1a x1 x2 c0 s2 L2o L1o f1b x3 L3o L0p c1 c2 L2p L1p L3p W1 Pa f2a c3 Pb f2b sq sd C
-G2 W2 H fq G1 fd r2 A0 r1 A2 Gd Gq o0 rd rq o1 o2 i0 i1 i2 v
+g0 sd5 s14 s20 sq4 s113 s11 sq5 s19 s21 sd9 s18 s112 x0 s29 sd4 f18 s24 fd5 fq4 sq8 c0 sq1 f14 f11 f112 f113
+f19 sd12 x1 s15 fd4 f24 x2 s28 c2 f29 sd8 sd0 sq12 fd12 fq5 x3 s10 fq1 fd9 sq0 c1 s212 sd1 f21 L f15 s213 s25
+sq9 f28 c3 sq13 f212 fd8 W1 fq12 fd1 fq8 C f213 f25 P sd13 fq9 fq13 G2 W2 Wq H r23 A r22 r21 fd13 G1 Wd o0 r13
+r20 t21 Gd N r12 B o1 rd2 Gq rd3 r11 t11 rq3 i0 rq2 t20 oa i1 v0 rq1 r10 rq0 tq1 ia rd0 tq0 t10 v1 ob rd1 v2
+ib td0 td1
 """
 
 
@@ -291,17 +292,23 @@
         self.sems = (local_sems, send_sems, recv_sems)
         self.count, self.open, self.locals = 0, [], 0
 
-    def remote(self, source, target, device):
-        copy = pltpu.make_async_remote_copy(
+    def reserve(self, count):
+        self.count += count
+        return self.count - count
+
+    def at(self, number, source, target, device):
+        return pltpu.make_async_remote_copy(
             src_ref=source,
             dst_ref=target,
-            send_sem=self.sems[1].at[self.count],
-            recv_sem=self.sems[2].at[self.count],
+            send_sem=self.sems[1].at[number],
+            recv_sem=self.sems[2].at[number],
             device_id=device,
             device_id_type=MESH,
         )
+
+    def remote(self, source, target, device):
+        copy = self.at(self.reserve(1), source, target, device)
         copy.start()
-        self.count += 1
         self.open.append(copy)
         return copy
 
@@ -337,19 +344,19 @@
 def layer_kernel(
     x_ref, c_ref, w1, w2, wq, wd, flag, norms, turns,
     f1, f2, fq, fd, out_keep, out_got, in_keep, in_got, vec,
-    xg, cg, g1, g2, gq, gd, na, r1, r2, rq, rd, co, ci, xo, xi, flags,
-    big1, big2, wa, wb, wqv, wdv, hid, gf, qkv, att, d1, d2, dq, dd, xt, st, stats, sums, cols, vec_got, fl,
+    xg, cg, g1, g2, gq, gd, na, r1, r2, rq, rd, z1, z2, zq, zd, co, ci, xo, xi, ob, flags,
+    big1, big2, wa, wb, wqv, wdv, hid, gf, qkv, att, d1, d2, dq, dd, xt, st, stats, sums, cols, vec_own, vec_got, vec_sum, vec_core, fl,
     local_sems, send_sems, recv_sems,
 ):
     me, core = place()
     by, upper, mine = (me >> 1) & 1, me >> 2, feature_of(me)
     rows = w1.shape[0]
     d_model = x_ref.shape[1]
-    greet([(me ^ d, core) for d in NEAR] + [(me ^ 2, core), (me, 1 - core)])
+    greet([(me ^ d, core) for d in range(1, 16)] + [(me, 1 - core)])
     copies = Copies(local_sems, send_sems, recv_sems)
     weights = {"1": (w1, g1, 1), "2": (w2, g2, 0), "q": (wq, gq, 1), "d": (wd, gd, 0)}
     tokens = {"x": (x_ref, xg), "c": (c_ref, cg)}
-    grads = {"1": (d1, f1, r1, 0), "2": (d2, f2, r2, 1), "q": (dq, fq, rq, 0), "d": (dd, fd, rd, 1)}
+    grads = {"1": (d1, f1, r1, z1, 0), "2": (d2, f2, r2, z2, 1), "q": (dq, fq, rq, zq, 0), "d": (dd, fd, rd, zd, 1)}
     state, kept, landed = {}, [], []
     pieces = {name: [] for name in weights}
 
@@ -363,73 +370,106 @@
         return g.at[:, cut] if dim == 0 else g.at[cut, :]
 
     def send_flag():
+        cols[...] = jnp.zeros_like(cols)
         kept.append(copies.local(flag, flags.at[0]))
         state["flags"] = [copies.remote(flag, flags.at[k], (me ^ d, core)) for k, d in ((1, 1), (2, 4), (3, 5))]
 
-    def send_weight(name):
+    def send_weight(name, d):
         w, g, dim = weights[name]
-        pieces[name].append(copies.local(block(w, dim, me), slot(g, dim, me)))
-        pieces[name].append(copies.remote(block(w, dim, me ^ 2), slot(g, dim, me), (me ^ 2, core)))
-        state[name] = [copies.remote(block(w, dim, me ^ d), slot(g, dim, me), (me ^ d, core)) for d in NEAR]
-
-    def forward_weight(name, part):
+        if d == 0:
+            state[name, 0] = copies.local(block(w, dim, me), slot(g, dim, me))
+            pieces[name].append(copies.remote(block(w, dim, me ^ 2), slot(g, dim, me), (me ^ 2, core)))
+        else:
+            state[name, d] = copies.remote(block(w, dim, me ^ d), slot(g, dim, me), (me ^ d, core))
+
+    def forward_weight(name, d):
         w, g, dim = weights[name]
-        for k in range(*{"a": (0, 3), "b": (3, 7)}.get(part, (0, 7))):
-            state[name][k].wait_recv()
-            held = slot(g, dim, me ^ NEAR[k])
-            pieces[name].append(copies.remote(held, held, (me ^ 2, core)))
+        state[name, d].wait_recv()
+        held = slot(g, dim, me ^ d)
+        pieces[name].append(copies.remote(held, held, (me ^ 2, core)))
 
     def weight_ready(name):
+        state[name, 0].wait()
         for copy in pieces[name]:
-            if copy is pieces[name][0]:
-                copy.wait()
-            else:
-                copy.wait_recv()
+            copy.wait_recv()
+
+    def tile_at(ref, rel, half):
+        return ref.at[rows_at(rel * 2 + half, TILE), :]
 
     def token_step(kind, step):
         source, g = tokens[kind]
         if step == "0":
             state[kind] = [
-                copies.remote(source, g.at[2, core], (me ^ 4, core)),
-                copies.remote(source, g.at[1, core], (me ^ 1, core)),
+                copies.remote(source, tile_at(g, 2, core), (me ^ 4, core)),
+                copies.remote(source, tile_at(g, 1, core), (me ^ 1, core)),
             ]
-            state[kind + "p0"] = copies.remote(source, g.at[0, core], (me, 1 - core))
+            state[kind + "p0"] = copies.remote(source, tile_at(g, 0, core), (me, 1 - core))
         elif step == "1":
             state[kind][0].wait_recv()
-            state[kind].append(copies.remote(g.at[2, core], g.at[3, core], (me ^ 1, core)))
-            state[kind + "p2"] = copies.remote(g.at[2, core], g.at[2, core], (me, 1 - core))
+            state[kind].append(copies.remote(tile_at(g, 2, core), tile_at(g, 3, core), (me ^ 1, core)))
+            state[kind + "p2"] = copies.remote(tile_at(g, 2, core), tile_at(g, 2, core), (me, 1 - core))
         elif step == "2":
             state[kind][1].wait_recv()
-            state[kind + "p1"] = copies.remote(g.at[1, core], g.at[1, core], (me, 1 - core))
+            state[kind + "p1"] = copies.remote(tile_at(g, 1, core), tile_at(g, 1, core), (me, 1 - core))
         elif step == "3":
             state[kind][2].wait_recv()
-            state[kind + "p3"] = copies.remote(g.at[3, core], g.at[3, core], (me, 1 - core))
-
-    def normalize(rel, half):
-        if half == "o":
-            which = core
-            copies.now((x_ref if rel == 0 else xg.at[rel, core], xt.at[0]))
-        else:
-            which = 1 - core
+            state[kind + "p3"] = copies.remote(tile_at(g, 3, core), tile_at(g, 3, core), (me, 1 - core))
+
+    def normalize():
+        for rel in range(4):
             state["xp%d" % rel].wait_recv()
-            copies.now((xg.at[rel, which], xt.at[0]))
-        tile = rel * 2 + which
-
-        @pl.loop(0, TILE // 32)
+        keep = copies.locals
+        copies.locals += 4
+
+        def load(k, source):
+            return pltpu.make_async_copy(source, xt.at[k & 1], local_sems.at[keep + (k & 1)])
+
+        def store(k):
+            return pltpu.make_async_copy(
+                big2.at[rows_at(k & 1, TILE), :], na.at[rows_at(k, TILE), :], local_sems.at[keep + 2 + (k & 1)]
+            )
+
+        def start(k):
+            @pl.when(k == core)
+            def _():
+                load(k, x_ref).start()
+
+            @pl.when(k != core)
+            def _():
+                load(k, xg.at[rows_at(k, TILE), :]).start()
+
+        start(0)
+
+        @pl.loop(0, 8)
         def _(k):
-            r = rows_at(k, 32)
-            here = rows_at(tile * (TILE // 32) + k, 32)
-            v = xt[0, r, :].astype(F32)
-            mean = jnp.mean(v, axis=-1, keepdims=True)
-            center = v - mean
-            scale = lax.rsqrt(jnp.mean(center * center, axis=-1, keepdims=True) + 1e-05)
-            xhat = center * scale
-            xt[1, r, :] = (xhat * norms[0:1, :] + norms[1:2, :]).astype(BF16)
-            big1[here, :] = (xhat * norms[2:3, :] + norms[3:4, :]).astype(BF16)
-            stats[here, 0:1] = mean
-            stats[here, 1:2] = scale
-
-        copies.now((xt.at[1], na.at[rows_at(tile, TILE), :]))
+            @pl.when(k < 7)
+            def _():
+                start(k + 1)
+
+            load(k, x_ref).wait()
+
+            @pl.when(k > 1)
+            def _():
+                store(k).wait()
+
+            @pl.loop(0, TILE // 32)
+            def _(j):
+                r = rows_at(j, 32)
+                here = rows_at(k * (TILE // 32) + j, 32)
+                v = xt[k & 1, r, :].astype(F32)
+                mean = jnp.mean(v, axis=-1, keepdims=True)
+                center = v - mean
+                scale = lax.rsqrt(jnp.mean(center * center, axis=-1, keepdims=True) + 1e-05)
+                xhat = center * scale
+                big2[rows_at((k & 1) * (TILE // 32) + j, 32), :] = (xhat * norms[0:1, :] + norms[1:2, :]).astype(BF16)
+                big1[here, :] = (xhat * norms[2:3, :] + norms[3:4, :]).astype(BF16)
+                stats[here, 0:1] = mean
+                stats[here, 1:2] = scale
+
+            store(k).start()
+
+        store(0).wait()
+        store(1).wait()
 
     def up(lo, hi):
         @pl.loop(lo, hi)
@@ -446,12 +486,10 @@
     def load_cotangent():
         for k in range(4):
             state["cp%d" % k].wait_recv()
-        pairs = [(c_ref, big2.at[rows_at(core, TILE), :])]
-        pairs += [(cg.at[0, 1 - core], big2.at[rows_at(1 - core, TILE), :])]
-        pairs += [
-            (cg.at[k, h], big2.at[(k * 2 + h) * TILE : (k * 2 + h + 1) * TILE, :])
-            for k in (1, 2, 3)
-            for h in (0, 1)
+        pairs = [
+            (c_ref, tile_at(big2, 0, core)),
+            (tile_at(cg, 0, 1 - core), tile_at(big2, 0, 1 - core)),
+            (cg.at[pl.ds(2 * TILE, 6 * TILE), :], big2.at[pl.ds(2 * TILE, 6 * TILE), :]),
         ]
         copies.now(*pairs)
 
@@ -464,10 +502,19 @@
         start = pl.multiple_of(start * size, size)
         return ref.at[pl.ds(start, size), :] if dim == 0 else ref.at[:, pl.ds(start, size)]
 
-    def send_grad(name):
-        d, f, r, dim = grads[name]
-
-        def product(pair):
+    def make_grad(name):
+        d, _, r, _, dim = grads[name]
+        base = copies.reserve(4)
+
+        def send(k):
+            pair = (upper ^ (3 - k)) * 2 + 1 - by
+            return copies.at(
+                base + k, cut(d, dim, pair, 2 * rows), cut(r, dim, 3 - k, 2 * rows), (me ^ 2, core)
+            )
+
+        @pl.loop(0, 8)
+        def _(k):
+            pair = (upper ^ (3 - (k & 3))) * 2 + (by ^ 1 ^ (k >> 2))
             c = rows_at(pair, 2 * rows)
             if name == "1":
                 d[c, :] = mm(big1[:, c], gf[...], TN).astype(BF16)
@@ -479,42 +526,48 @@
             else:
                 d[:, c] = mm(att[...], big2[:, c], TN).astype(BF16)
 
-        state["r" + name] = {}
-        for u in FAR_FIRST:
-            pair = (upper ^ u) * 2 + 1 - by
-            product(pair)
-            state["r" + name][u] = copies.remote(
-                cut(d, dim, pair, 2 * rows), cut(r, dim, u, 2 * rows), (me ^ 2, core)
-            )
-
-        @pl.loop(0, 4)
-        def _(u):
-            product(u * 2 + by)
-
-    def forward_grad(name):
-        d, f, r, dim = grads[name]
-        for u in FAR_FIRST:
-            state["r" + name][u].wait_recv()
-            own = cut(d, dim, (upper ^ u) * 2 + by, 2 * rows)
-            if name == "2":
-                stage = st
+            @pl.when(k < 4)
+            def _():
+                send(k).start()
+
+        for k in range(4):
+            state["r" + name, 3 - k] = send(k)
+            copies.open.append(send(k))
+
+    def add_slab(name, dim, got, k, own):
+        d = grads[name][0]
+        stage = st if name == "2" else xt.at[0, :, pl.ds(0, d.shape[1] if dim == 0 else 2 * rows)]
+        copies.now((cut(got, dim, k, 2 * rows), stage))
+        some = 32 if dim == 0 else 128
+
+        @pl.loop(0, stage.shape[0] // some)
+        def _(j):
+            c = rows_at(j, some)
+            own[c, :] = (own[c, :].astype(F32) + stage[c, :].astype(F32)).astype(BF16)
+
+    def forward_grad(name, u):
+        d, f, r, z, dim = grads[name]
+        state["r" + name, u].wait_recv()
+        own = cut(d, dim, (upper ^ u) * 2 + by, 2 * rows)
+        add_slab(name, dim, r, u, own)
+        if u & 2:
+            state["z" + name, u & 1] = copies.remote(own, cut(z, dim, u & 1, 2 * rows), (me ^ 8, core))
+
+    def deliver_grad(name, u):
+        d, f, r, z, dim = grads[name]
+        state["z" + name, u].wait_recv()
+        add_slab(name, dim, z, u, cut(d, dim, (upper ^ u) * 2 + by, 2 * rows))
+        for x in (1, 0):
+            piece = cut(d, dim, (upper ^ u) * 4 + by * 2 + ((me & 1) ^ x), rows)
+            width = f.shape[1 - dim] // 4
+            c = pl.ds(mine * width, width)
+            target = f.at[:, c] if dim == 0 else f.at[c, :]
+            if u == 0 and x == 0:
+                kept.append(copies.local(piece, target))
             else:
-                stage = xt.at[0, :, pl.ds(0, d.shape[1] if dim == 0 else 2 * rows)]
-            copies.now((cut(r, dim, u, 2 * rows), stage))
-            own[...] = (own[...].astype(F32) + stage[...].astype(F32)).astype(BF16)
-            for x in (1, 0):
-                piece = cut(d, dim, (upper ^ u) * 4 + by * 2 + ((me & 1) ^ x), rows)
-                size = f.shape[2 - dim] // 4
-                c = pl.ds(mine * size, size)
-                target = f.at[me >> 3, :, c] if dim == 0 else f.at[me >> 3, c, :]
-                if u == 0 and x == 0:
-                    kept.append(copies.local(piece, target))
-                else:
-                    landed.append(copies.remote(piece, target, (me ^ (4 * u + x), core)))
+                landed.append(copies.remote(piece, target, (me ^ (4 * u + x), core)))
 
     def hidden_grad():
-        cols[...] = jnp.zeros_like(cols)
-
         @pl.loop(0, 8)
         def _(i):
             r = rows_at(i, TILE)
@@ -525,80 +578,207 @@
                 at = slice(3 * HEAD_DIM + j, 3 * HEAD_DIM + j + 512)
                 cols[:, at] += fold(g.astype(F32))
 
-    def attention(lo, hi):
-        @pl.loop(lo, hi)
-        def _(number):
-            attend(number)
-
-    def attend(number):
-        size, half = 2 * TILE, TILE
-        quarter = size // 4
-
-        def at_rows(start, length):
-            return pl.ds(pl.multiple_of(number * size + start, TILE), length)
-
+    size, half, quarter = 2 * TILE, TILE, TILE // 2
+
+    def group_rows(number, start, length):
+        return pl.ds(pl.multiple_of(number * size + start, TILE), length)
+
+    def group_tables(number):
         three = fl[number, 0:1, 0:1] > 0.5
         tables = []
         for k in range(3):
             again = jnp.concatenate([turns[k, :quarter], turns[k, : 2 * quarter], turns[k, :quarter]], axis=0)
             tables.append(jnp.where(three, again, turns[k]))
-        everything = at_rows(0, size)
-        full = mm(big1[everything, :], wqv[...], NN) + norms[5:6, : 3 * HEAD_DIM]
-        qkv[everything, :HEAD_DIM] = rope(full[:, :HEAD_DIM], tables, 1.0).astype(BF16)
-        qkv[everything, HEAD_DIM : 2 * HEAD_DIM] = rope(full[:, HEAD_DIM : 2 * HEAD_DIM], tables, 1.0).astype(BF16)
-        qkv[everything, 2 * HEAD_DIM :] = full[:, 2 * HEAD_DIM :].astype(BF16)
-        grad_q, grad_k, grad_v = {}, {}, {}
-        for i in (1, 0):
-            r = at_rows(i * half, half)
-            seen = (i + 1) * half
-            q = qkv[r, :HEAD_DIM]
-            k = qkv[at_rows(0, seen), HEAD_DIM : 2 * HEAD_DIM]
-            v = qkv[at_rows(0, seen), 2 * HEAD_DIM :]
-            ti = lax.broadcasted_iota(jnp.int32, (half, seen), 0) + i * half
-            tj = lax.broadcasted_iota(jnp.int32, (half, seen), 1)
-            part_i = (ti >= quarter).astype(jnp.int32) + (ti >= 3 * quarter).astype(jnp.int32)
-            part_j = (tj >= quarter).astype(jnp.int32) + (tj >= 3 * quarter).astype(jnp.int32)
-            s = mm(q, k, NT) * 0.0625
-            s = jnp.where(tj <= ti, s, -1e30)
-            s = jnp.where((part_i != part_j) & three, -1e30, s)
-            w = jnp.exp(s - jnp.max(s, axis=-1, keepdims=True))
-            p = w / jnp.sum(w, axis=-1, keepdims=True)
-            low = p.astype(BF16)
-            att[r, :] = mm(low, v, NN).astype(BF16)
-            ga = mm(big2[r, :], wdv[...], NT).astype(BF16)
-            gp = mm(ga, v, NT)
-            gs = (p * (gp - jnp.sum(p * gp, axis=-1, keepdims=True))).astype(BF16)
-            grad_q[i] = mm(gs, k, NN) * 0.0625
-            grad_k[i] = mm(gs, q, TN) * 0.0625
-            grad_v[i] = mm(low, ga, TN)
-
-        def put(k, total):
-            total = total.astype(BF16)
-            at = slice(k * HEAD_DIM, (k + 1) * HEAD_DIM)
-            qkv[everything, at] = total
-            cols[:, at] += fold(total.astype(F32))
-
-        def joined(one, two):
-            return jnp.concatenate([one + two[:half], two[half:]], axis=0)
-
-        put(0, rope(jnp.concatenate([grad_q[0], grad_q[1]], axis=0), tables, -1.0))
-        put(1, rope(joined(grad_k[0], grad_k[1]), tables, -1.0))
-        put(2, joined(grad_v[0], grad_v[1]))
-
-    sets = {"o": (out_keep, out_got, big1, co, xo), "i": (in_keep, in_got, big2, ci, xi)}
-
-    def token_product(name, rel, which, buffer, at, received):
-        tile = rel * 2 + which
-        r = rows_at(tile, TILE)
-        if name == "i":
-            copies.now((x_ref if rel == 0 and received else xg.at[rel, which], xt.at[0]))
-
-        @pl.loop(0, d_model // 512)
-        def _(j):
-            c = rows_at(j, 512)
-            if name == "o":
+        return tables
+
+    def probabilities(number, i):
+        seen = (i + 1) * half
+        q = qkv[group_rows(number, i * half, half), :HEAD_DIM]
+        k = qkv[group_rows(number, 0, seen), HEAD_DIM : 2 * HEAD_DIM]
+        v = qkv[group_rows(number, 0, seen), 2 * HEAD_DIM :]
+        ti = lax.broadcasted_iota(jnp.int32, (half, seen), 0) + i * half
+        tj = lax.broadcasted_iota(jnp.int32, (half, seen), 1)
+        part_i = (ti >= quarter).astype(jnp.int32) + (ti >= 3 * quarter).astype(jnp.int32)
+        part_j = (tj >= quarter).astype(jnp.int32) + (tj >= 3 * quarter).astype(jnp.int32)
+        three = fl[number, 0:1, 0:1] > 0.5
+        s = mm(q, k, NT) * 0.0625
+        s = jnp.where(tj <= ti, s, -1e30)
+        s = jnp.where((part_i != part_j) & three, -1e30, s)
+        w = jnp.exp(s - jnp.max(s, axis=-1, keepdims=True))
+        return q, k, v, w / jnp.sum(w, axis=-1, keepdims=True)
+
+    def attend(lo, hi):
+        @pl.loop(lo, hi)
+        def _(number):
+            tables = group_tables(number)
+            for h in (0, 1):
+                copies.now((na.at[group_rows(number, h * half, half), :], xt.at[h]))
+            for h in (0, 1):
+                r = group_rows(number, h * half, half)
+                here = [t[h * half : (h + 1) * half] for t in tables]
+                for k in range(3):
+                    at = slice(k * HEAD_DIM, (k + 1) * HEAD_DIM)
+                    full = mm(xt[h], wqv[:, at], NN) + norms[5:6, at]
+                    qkv[r, at] = (rope(full, here, 1.0) if k < 2 else full).astype(BF16)
+            for i in (0, 1):
+                _, _, v, p = probabilities(number, i)
+                att[group_rows(number, i * half, half), :] = mm(p.astype(BF16), v, NN).astype(BF16)
+
+    def attend_back(lo, hi):
+        @pl.loop(lo, hi)
+        def _(number):
+            grad_q, grad_k, grad_v = {}, {}, {}
+            tables = group_tables(number)
+            for i in (1, 0):
+                q, k, v, p = probabilities(number, i)
+                low = p.astype(BF16)
+                ga = mm(big2[group_rows(number, i * half, half), :], wdv[...], NT).astype(BF16)
+                gp = mm(ga, v, NT)
+                gs = (p * (gp - jnp.sum(p * gp, axis=-1, keepdims=True))).astype(BF16)
+                grad_q[i] = mm(gs, k, NN) * 0.0625
+                grad_k[i] = mm(gs, q, TN) * 0.0625
+                grad_v[i] = mm(low, ga, TN)
+
+            def put(k, total):
+                total = total.astype(BF16)
+                at = slice(k * HEAD_DIM, (k + 1) * HEAD_DIM)
+                qkv[group_rows(number, 0, size), at] = total
+                cols[:, at] += fold(total.astype(F32))
+
+            def joined(one, two):
+                return jnp.concatenate([one + two[:half], two[half:]], axis=0)
+
+            put(0, rope(jnp.concatenate([grad_q[0], grad_q[1]], axis=0), tables, -1.0))
+            put(1, rope(joined(grad_k[0], grad_k[1]), tables, -1.0))
+            put(2, joined(grad_v[0], grad_v[1]))
+
+    def add_tiles(one, other, out):
+        @pl.loop(0, TILE // 32)
+        def _(k):
+            r = rows_at(k, 32)
+            out[r, :] = (one[r, :].astype(F32) + other[r, :].astype(F32)).astype(BF16)
+
+    def rel_of(k):
+        return 3 - 2 * (k & 1) - (k >> 1)
+
+    def out_sum(received):
+        base = copies.reserve(4) if not received else state["o"]
+        over = copies.reserve(2) if received else 0
+
+        def to_core(k):
+            part = ob.at[rows_at(k, TILE), :]
+            return copies.at(base + k, part, co.at[rows_at(k, TILE), :], (me, 1 - core))
+
+        def to_x(k):
+            part = ob.at[rows_at(4 + k, TILE), :]
+            return copies.at(over + k, part, xo.at[rows_at(k, TILE), :], (me ^ 1, core))
+
+        spare = copies.locals
+        copies.locals += 3
+
+        def load(k, slot):
+            return pltpu.make_async_copy(
+                co.at[rows_at(k, TILE), :], xt.at[slot], local_sems.at[spare + slot]
+            )
+
+        def store(k):
+            target = ob.at[rows_at(4 * received + k, TILE), :]
+            return pltpu.make_async_copy(xt.at[1], target, local_sems.at[spare + 2])
+
+        if received:
+            for k in range(4):
+                to_core(k).wait_recv()
+
+        @pl.loop(0, 4)
+        def _(k):
+            r = rows_at(rel_of(k) * 2 + (core if received else 1 - core), TILE)
+            if received:
+                load(k, 0).start()
+                load(k, 0).wait()
+
+            @pl.loop(0, d_model // 512)
+            def _(j):
+                c = rows_at(j, 512)
                 total = mm(att[r, :], wdv[:, c], NN) + mm(hid[r, :], wb[:, c], NN)
+                if received:
+                    total = total + xt[0, :, c].astype(F32)
+                xt[1, :, c] = total.astype(BF16)
+
+            store(k).start()
+            store(k).wait()
+            if received:
+
+                @pl.when(k < 2)
+                def _():
+                    to_x(k).start()
+
             else:
+                to_core(k).start()
+
+        if received:
+            state["ox"] = [to_x(k) for k in range(2)]
+            copies.open.extend(state["ox"])
+        else:
+            state["o"] = base
+            copies.open.extend(to_core(k) for k in range(4))
+
+    def out_end(k):
+        state["ox"][k].wait_recv()
+        copies.now((ob.at[rows_at(6 + k, TILE), :], xt.at[0]), (xo.at[rows_at(k, TILE), :], xt.at[1]))
+        add_tiles(xt.at[0], xt.at[1], xt.at[0])
+        if k == 0:
+            copies.now((xt.at[0], ob.at[rows_at(6, TILE), :]))
+            landed.append(copies.remote(ob.at[rows_at(6, TILE), :], out_got, (me ^ 4, core)))
+        else:
+            copies.now((xt.at[0], out_keep))
+
+    def in_sum(received):
+        base = copies.reserve(4) if not received else state["i"]
+        over = copies.reserve(2) if received else 0
+
+        def to_core(k):
+            part = big2.at[rows_at(k, TILE), :]
+            return copies.at(base + k, part, ci.at[rows_at(k, TILE), :], (me, 1 - core))
+
+        def to_x(k):
+            part = big2.at[rows_at(4 + k, TILE), :]
+            return copies.at(over + k, part, xi.at[rows_at(k, TILE), :], (me ^ 1, core))
+
+        spare = copies.locals
+        copies.locals += 2
+
+        def load(source, slot):
+            return pltpu.make_async_copy(source, xt.at[slot], local_sems.at[spare + slot])
+
+        if received:
+            for k in range(4):
+                to_core(k).wait_recv()
+        else:
+            sums[0:4] = jnp.zeros_like(sums[0:4])
+
+        @pl.loop(0, 4)
+        def _(k):
+            tile = rel_of(k) * 2 + (core if received else 1 - core)
+            r = rows_at(tile, TILE)
+            if received:
+                load(ci.at[rows_at(k, TILE), :], 1).start()
+
+                @pl.when(k < 3)
+                def _():
+                    load(xg.at[r, :], 0).start()
+
+                @pl.when(k == 3)
+                def _():
+                    load(x_ref, 0).start()
+
+                load(x_ref, 1).wait()
+            else:
+                load(xg.at[r, :], 0).start()
+            load(x_ref, 0).wait()
+
+            @pl.loop(0, d_model // 512)
+            def _(j):
+                c = rows_at(j, 512)
                 a = mm(qkv[r, :], wqv[c, :], NT)
                 f = mm(gf[r, :], wa[c, :], NT)
                 xhat = (xt[0, :, c].astype(F32) - stats[r, 0:1]) * stats[r, 1:2]
@@ -607,103 +787,119 @@
                 sums[2, :, c] += fold(f * xhat)
                 sums[3, :, c] += fold(f)
                 total = a * norms[0:1, c] + f * norms[2:3, c]
+                if received:
+                    total = total + xt[1, :, c].astype(F32)
+                big2[rows_at(4 * received + k, TILE), c] = total.astype(BF16)
+
             if received:
-                total = total + xt[1, :, c].astype(F32)
-            buffer[at * TILE : (at + 1) * TILE, c] = total.astype(BF16)
-
-    def tile_of(buffer, at):
-        return buffer.at[at * TILE : (at + 1) * TILE, :]
-
-    def token_sum(name, step):
-        keep, end, buffer, got, over = sets[name]
+
+                @pl.when(k < 2)
+                def _():
+                    to_x(k).start()
+
+            else:
+                to_core(k).start()
+
+        if received:
+            state["ix"] = [to_x(k) for k in range(2)]
+            copies.open.extend(state["ix"])
+        else:
+            state["i"] = base
+            copies.open.extend(to_core(k) for k in range(4))
+
+    def in_end(k):
+        state["ix"][k].wait_recv()
+        copies.now((xi.at[rows_at(k, TILE), :], xt.at[1]))
+        acc = big2.at[rows_at(6 + k, TILE), :]
+        add_tiles(acc, xt.at[1], acc)
+        if k == 0:
+            landed.append(copies.remote(acc, in_got, (me ^ 4, core)))
+        else:
+            copies.now((acc, in_keep))
+
+    def vector_step(step):
+        def piece(ref, d):
+            return ref.at[:, rows_at(d, vec_got.shape[-1])]
+
         if step == "0":
-            if name == "i":
-                sums[0:4] = jnp.zeros_like(sums[0:4])
-            state[name] = {}
-            for rel in (1, 3, 2, 0):
-                token_product(name, rel, 1 - core, buffer, rel, False)
-                state[name][rel] = copies.remote(tile_of(buffer, rel), got.at[rel], (me, 1 - core))
+            vec_own[...] = jnp.zeros_like(vec_own)
+            for j in range(5):
+                vec_own[j : j + 1, :] = jnp.sum(sums[j], axis=0, keepdims=True)
+            for j in range(4):
+                ours = jnp.where(mine == j, 1.0, 0.0)
+                vec_own[8 + j : 9 + j, :] = jnp.sum(cols[...], axis=0, keepdims=True) * ours
+            state["v"] = [
+                copies.remote(piece(vec_own, me ^ d), vec_got.at[d], (me ^ d, core)) for d in range(1, 16)
+            ]
         elif step == "1":
-            for rel in (3, 1, 2, 0):
-                state[name][rel].wait_recv()
-                copies.now((got.at[rel], xt.at[1]))
-                token_product(name, rel, core, buffer, 4 + rel, True)
-                if rel & 1:
-                    state[name + str(rel)] = copies.remote(
-                        tile_of(buffer, 4 + rel), over.at[rel // 2], (me ^ 1, core)
-                    )
-        else:
-            for rel in (2, 0):
-                state[name + str(rel + 1)].wait_recv()
-                copies.now((over.at[rel // 2], xt.at[1]))
-
-                @pl.loop(0, TILE // 32)
-                def _(k):
-                    r = rows_at((4 + rel) * (TILE // 32) + k, 32)
-                    buffer[r, :] = (
-                        buffer[r, :].astype(F32) + xt[1, rows_at(k, 32), :].astype(F32)
-                    ).astype(BF16)
-
-                if rel == 2:
-                    landed.append(copies.remote(tile_of(buffer, 6), end, (me ^ 4, core)))
-                else:
-                    kept.append(copies.local(tile_of(buffer, 4), keep))
-
-    def vectors():
-        vec[...] = jnp.zeros_like(vec)
-        for k in range(5):
-            vec[k : k + 1, :] = jnp.sum(sums[k], axis=0, keepdims=True)
-        for k in range(4):
-            ours = jnp.where(mine == k, 1.0, 0.0)
-            vec[8 + k : 9 + k, :] = jnp.sum(cols[...], axis=0, keepdims=True) * ours
-        hops = [(me, 1 - core), (me ^ 2, core), (me ^ 1, core), (me ^ 4, core), (me ^ 8, core)]
-        for k, device in enumerate(hops):
-            copy = copies.remote(vec, vec_got.at[k], device)
-            copies.open.pop()
-            copy.wait()
-            if k == 0:
-                vec[:8, :] += vec_got[0, :8, :]
-            else:
-                vec[...] += vec_got[k]
-
-    for op in ORDER.split():
+            total = vec_own[:, rows_at(me, vec_got.shape[-1])]
+            for d, copy in enumerate(state["v"]):
+                copy.wait_recv()
+                total = total + vec_got[d + 1]
+            vec_sum[...] = total
+            state["v"] = copies.remote(vec_sum, vec_core, (me, 1 - core))
+        elif step == "2":
+            state["v"].wait_recv()
+            here = rows_at(me, vec_got.shape[-1])
+            vec[8:, here] = vec_sum[8:, :]
+            vec[:8, here] = vec_sum[:8, :] + vec_core[:8, :]
+            for d in range(1, 16):
+                landed.append(copies.remote(piece(vec, me), piece(vec, me), (me ^ d, core)))
+
+    def run(op):
         kind, rest = op[0], op[1:]
         if kind == "g":
             send_flag()
         elif kind in "xc":
             token_step(kind, rest)
         elif kind == "s":
-            send_weight(rest)
+            send_weight(rest[0], int(rest[1:]))
         elif kind == "f":
-            forward_weight(rest[0], rest[1:])
+            forward_weight(rest[0], int(rest[1:]))
         elif kind == "L":
-            normalize(int(rest[0]), rest[1])
+            normalize()
         elif kind == "W":
             weight_ready(rest)
-            copies.now((g1, wa) if rest == "1" else (g2, wb))
+            copies.now({"1": (g1, wa), "2": (g2, wb), "q": (gq, wqv), "d": (gd, wdv)}[rest])
+            if rest == "q":
+                for copy in state["flags"]:
+                    copy.wait_recv()
+                kept.pop(0).wait()
+                copies.now((flags, fl))
         elif kind == "P":
-            up(*((0, 4) if rest == "a" else (4, 8)))
+            up(*{"a": (0, 4), "b": (4, 8)}.get(rest, (0, 8)))
         elif kind == "C":
             load_cotangent()
         elif kind == "G":
-            send_grad(rest)
+            make_grad(rest)
         elif kind == "H":
             hidden_grad()
         elif kind == "r":
-            forward_grad(rest)
+            forward_grad(rest[0], int(rest[1]))
+        elif kind == "t":
+            deliver_grad(rest[0], int(rest[1]))
         elif kind == "A":
-            if rest == "0":
-                for name in "qd":
-                    weight_ready(name)
-                for copy in state["flags"]:
-                    copy.wait_recv()
-                kept.pop(0).wait()
-                copies.now((gq, wqv), (gd, wdv), (na, big1), (flags, fl))
-            attention(int(rest), int(rest) + 2)
-        elif kind in "oi":
-            token_sum(kind, rest)
+            attend(*{"0": (0, 2), "2": (2, 4)}.get(rest, (0, 4)))
+        elif kind == "B":
+            attend_back(*{"0": (0, 2), "2": (2, 4)}.get(rest, (0, 4)))
+        elif kind == "N":
+            copies.now((na, big1))
+        elif kind == "o":
+            if rest in "01":
+                out_sum(int(rest))
+            else:
+                out_end(0 if rest == "a" else 1)
+        elif kind == "i":
+            if rest in "01":
+                in_sum(int(rest))
+            else:
+                in_end(0 if rest == "a" else 1)
         else:
-            vectors()
+            vector_step(rest)
+
+    for op in ORDER.split():
+        with jax.named_scope("step_" + op):
+            run(op)
     for copy in landed:
         copy.wait_recv()
     for copy in kept:
@@ -735,11 +931,12 @@
     def low(*shape):
         return jax.ShapeDtypeStruct(shape, BF16)
 
-    results = [low(n // 8, rows, 4 * u1), low(n // 8, 4 * u1, rows), low(n // 8, rows, 4 * uq), low(n // 8, 4 * ud, rows)]
+    results = [low(rows, 4 * u1), low(4 * u1, rows), low(rows, 4 * uq), low(4 * ud, rows)]
     results += [low(tok, d)] * 4 + [jax.ShapeDtypeStruct((16, d), F32)]
-    spare = [low(4, 2, tok, d)] * 2 + [low(d, u1), low(u1, d), low(d, uq), low(ud, d), low(many, d)]
-    spare += [low(d // 2, u1), low(u1, d // 2), low(d // 2, uq), low(ud, d // 2)]
-    spare += [low(4, tok, d)] * 2 + [low(2, tok, d)] * 2 + [jax.ShapeDtypeStruct((4, 8, 128), F32)]
+    spare = [low(many, d)] * 2 + [low(d, u1), low(u1, d), low(d, uq), low(ud, d), low(many, d)]
+    for part in (2, 4):
+        spare += [low(d // part, u1), low(u1, d // part), low(d // part, uq), low(ud, d // part)]
+    spare += [low(4 * tok, d)] * 2 + [low(2 * tok, d)] * 2 + [low(many, d)] + [jax.ShapeDtypeStruct((4, 8, 128), F32)]
     scratch = [
         (many, d), (many, d), (d, u1), (u1, d), (d, uq), (ud, d), (many, u1), (many, u1), (many, uq), (many, ud),
         (d, u1), (u1, d), (d, uq), (ud, d), (2, tok, d), (u1, 2 * rows),
@@ -755,11 +952,14 @@
             pltpu.VMEM((many, 2), F32),
             pltpu.VMEM((5, 8, d), F32),
             pltpu.VMEM((8, d), F32),
-            pltpu.VMEM((5, 16, d), F32),
+            pltpu.VMEM((16, d), F32),
+            pltpu.VMEM((n, 16, d // n), F32),
+            pltpu.VMEM((16, d // n), F32),
+            pltpu.VMEM((16, d // n), F32),
             pltpu.VMEM((4, 8, 128), F32),
-            pltpu.SemaphoreType.DMA((96,)),
-            pltpu.SemaphoreType.DMA((144,)),
-            pltpu.SemaphoreType.DMA((144,)),
+            pltpu.SemaphoreType.DMA((128,)),
+            pltpu.SemaphoreType.DMA((176,)),
+            pltpu.SemaphoreType.DMA((176,)),
         ],
         compiler_params=pltpu.CompilerParams(
             collective_id=1, has_side_effects=True, vmem_limit_bytes=65000 << 10
@@ -810,9 +1010,7 @@
         norms,
         turn_tables(seq_ids.shape[0]),
     )
-    out_fc1, out_fc2, out_qkv, out_dense = (
-        jnp.sum(v.astype(F32), axis=0) for v in (f1, f2, fq, fd)
-    )
+    out_fc1, out_fc2, out_qkv, out_dense = (v.astype(F32) for v in (f1, f2, fq, fd))
     own = layer_input.astype(F32)
     layer_output = (
         own

time: 586 us -> 444 us (0.76); the launches traced: 575 us -> 441 us
  Pallas kernels: 547 us -> 415 us
    pallas_call x1, Pallas kernels: 547 us -> 415 us  [layer_call(): pl.pallas_call(layer_kernel, out_shape=results + spare, in_specs=[hbm] *...]
where the time goes in v4:
time: 444 us; the launch traced here: 441 us
  Pallas kernels  415 us (93%)
  other arithmetic  16.9 us (4%)
  local copies, waits for them, and re-layouts  7.48 us (2%)
    pallas_call x1, Pallas kernels, layer_call(): pl.pallas_call(layer_kernel, out_shape=results + spare, in_specs=[hbm] *...  415 us

profile of v4, /device:TPU:0, one launch (start us, length us, event | category | flops | bytes accessed | tf_op | source)
XLA Modules:
  0.0 441.2 jit_solution(10456126669502493493)
XLA Ops:
  0.7 0.7 dynamic_slice.6
  1.4 0.8 dynamic_slice.7
  2.1 0.7 stack.24
  2.8 0.7 stack.25
  3.5 0.7 stack.26
  4.2 0.7 stack.27
  4.9 0.1 stack.31
  5.0 0.6 convert_element_type.51.norms
  5.7 1.3 reduce_max.9
  7.6 0.6 broadcast_in_dim.2.flag
  8.2 415.3 %layer.1 = (bf16[128,4096]{1,0:T(8,128)(2,1)}, bf16[4096,128]{1,0:T(8,128)(2,1)}, bf16[128,3072]{1,0:T(8,128)(2,1)}, bf16[1024,128]{1,0:T(8,128)(2,1)}, bf16[256...) custom-call(bf16[256,2048]{1,0:T(8,128)(2,1)} %x_ref.1, ...), custom_call_target="tpu_custom_call" | custom-call | flops 77309411328 | bytes 209715200 | tf_op jit(solution)/shard_map/layer/pallas_call | solution.py:945
  423.6 0.0 copy-start
  423.6 0.0 copy-start.1
  423.6 1.6 convert_reduce_fusion
  425.2 0.0 copy-start.11
  425.2 0.0 copy-start.12
  425.2 0.0 copy-start.2
  425.2 0.0 copy-start.3
  425.2 0.0 copy-start.6
  425.2 1.8 fusion.8
  427.0 0.0 copy-done
  427.1 0.0 copy-done.1
  427.1 2.0 fusion.12
  429.0 0.0 copy-done.11
  429.0 0.0 copy-done.12
  429.1 0.0 copy-done.2
  429.1 0.0 copy-done.3
  429.1 0.0 copy-done.6
  429.1 0.0 copy-start.9
  429.1 0.0 copy-start.5
  429.1 4.5 %fusion.7 = (f32[256,2048]{1,0:T(8,128)}, bf16[256,2048]{1,0:T(8,128)(2,1)}) fusion(bf16[256,2048]{1,0:T(8,128)(2,1)S(1)} %copy-done, bf16[256,2048]{1,0:T(8,128)(2,1)S(1)} %copy-done.3, bf16[256,2048]{1,0:T(8,128)(2,1)S(1)} %copy-done.2, bf16[256,2048]{1,0:T(8,128)(2,1)S(1)} %copy-done.1, f32[256]{0:T(256)S(1)} %get-tuple-element.41, ...), kind=kLoop, calls=%fused_computation.10 | loop fusion | flops 9961472 | bytes 9457664 | tf_op jit(solution)/shard_map/add | solution.py:1025
  433.6 0.0 copy-start.4
  433.6 0.0 copy-done.9
  433.6 0.6 fusion.13
  434.2 0.0 copy-start.10
  434.2 0.6 copy.32
  434.9 0.6 reshape.56
  435.5 0.0 copy-done.5
  435.5 1.5 convert_element_type.62
  437.0 0.0 copy-start.7
  437.0 0.0 copy-done.4
  437.0 0.0 copy-start.8
  437.0 1.5 convert_element_type.63
  438.5 0.0 copy-done.7
  438.5 1.3 convert_element_type.60
  439.8 0.0 copy-done.8
  439.8 0.8 convert_element_type.61
  440.6 0.0 copy-done.10
  440.6 0.6 copy.34
  (12 shorter events, 0.1 us)
Async XLA Ops:
  423.6 3.5 copy-start
  423.6 3.5 copy-start.1
  425.2 3.8 copy-start.11
  425.2 3.9 copy-start.12
  425.2 3.9 copy-start.2
  425.2 3.9 copy-start.3
  425.2 3.9 copy-start.6
  429.1 4.5 %copy-start.9 = (f32[16,2048]{1,0:T(8,128)S(1)}, f32[16,2048]{1,0:T(8,128)}, u32[]{:S(2)}) copy-start(f32[16,2048]{1,0:T(8,128)} %get-tuple-element.27) | copy-start | bytes 393220
  429.1 6.4 %copy-start.5 = (bf16[128,4096]{1,0:T(8,128)(2,1)S(1)}, bf16[128,4096]{1,0:T(8,128)(2,1)}, u32[]{:S(2)}) copy-start(bf16[128,4096]{1,0:T(8,128)(2,1)} %get-tuple-element.30) | copy-start | bytes 3145732
  433.6 3.4 copy-start.4
  434.2 6.4 %copy-start.10 = (f32[1,2048]{1,0:T(1,128)}, f32[1,2048]{1,0:T(1,128)S(1)}, u32[]{:S(2)}) copy-start(f32[1,2048]{1,0:T(1,128)S(1)} %get-tuple-element.36) | copy-start | bytes 24580
  437.0 1.5 copy-start.7
  437.0 2.8 copy-start.8

commit v5 on v4

--- a/solution.py
+++ b/solution.py
@@ -264,11 +264,11 @@
 
 TILE = 256
 ORDER = """
-g0 sd5 s14 s20 sq4 s113 s11 sq5 s19 s21 sd9 s18 s112 x0 s29 sd4 f18 s24 fd5 fq4 sq8 c0 sq1 f14 f11 f112 f113
-f19 sd12 x1 s15 fd4 f24 x2 s28 c2 f29 sd8 sd0 sq12 fd12 fq5 x3 s10 fq1 fd9 sq0 c1 s212 sd1 f21 L f15 s213 s25
-sq9 f28 c3 sq13 f212 fd8 W1 fq12 fd1 fq8 C f213 f25 P sd13 fq9 fq13 G2 W2 Wq H r23 A r22 r21 fd13 G1 Wd o0 r13
-r20 t21 Gd N r12 B o1 rd2 Gq rd3 r11 t11 rq3 i0 rq2 t20 oa i1 v0 rq1 r10 rq0 tq1 ia rd0 tq0 t10 v1 ob rd1 v2
-ib td0 td1
+g0 sq5 sq13 sd13 sd1 sd5 s18 sq9 x0 s15 sq8 sd9 sd0 s113 fq13 sq4 fd1 f18 s112 s20 s10 s19 sq12 fq5 sd8 s11
+sq1 x1 s25 s21 sd4 c0 s14 f15 sq0 fq1 s29 f11 f113 fq4 s212 fq8 sd12 x2 s28 f19 s213 x3 fq12 fq9 L fd9 fd8 s24
+f112 f21 f14 f212 c1 Wq fd5 fd13 f25 A W1 f24 fd12 f29 c2 P f28 fd4 c3 f213 C G2 W2 Wd r23 o0 H r22 r21 t21 G1
+o1 r13 B N r20 r12 oa Gd Gq X i0 t20 r11 rd2 rq3 t11 i1 rq1 rq2 tq1 rd3 v0 rq0 rd0 ia rd1 tq0 r10 t10 v1 v2
+td1 td0 ib ob
 """
 
 
@@ -342,10 +342,10 @@
 
 
 def layer_kernel(
-    x_ref, c_ref, w1, w2, wq, wd, flag, norms, turns,
-    f1, f2, fq, fd, out_keep, out_got, in_keep, in_got, vec,
+    x_ref, c_ref, w1, w2, wq, wd, ids, turns, p0, p1, p2, p3, p4, p5, p6, p7,
+    f1, f2, fq, fd, out_keep, out_got, in_keep, in_got, vec, norms,
     xg, cg, g1, g2, gq, gd, na, r1, r2, rq, rd, z1, z2, zq, zd, co, ci, xo, xi, ob, flags,
-    big1, big2, wa, wb, wqv, wdv, hid, gf, qkv, att, d1, d2, dq, dd, xt, st, stats, sums, cols, vec_own, vec_got, vec_sum, vec_core, fl,
+    big1, big2, wa, wb, wqv, wdv, hid, gf, qkv, att, d1, d2, dq, dd, xt, st, stats, sums, cols, vec_own, vec_got, vec_sum, vec_core, fl, flag, vectors,
     local_sems, send_sems, recv_sems,
 ):
     me, core = place()
@@ -360,6 +360,25 @@
     state, kept, landed = {}, [], []
     pieces = {name: [] for name in weights}
 
+    def spread():
+        lanes = vectors.shape[1]
+        norms[...] = jnp.zeros_like(norms)
+        wide = d_model // lanes
+        start = 0
+        for part in (p0, p1, p2, p3, p4, p5, p6, p7):
+            vectors[start : start + part.shape[0], :] = part[...].astype(F32)
+            start += part.shape[0]
+        units, width = wa.shape[1] // lanes, wqv.shape[1] // lanes
+        places = [(row, row * wide, wide) for row in range(4)]
+        places.append((4, 6 * wide + mine * units, units))
+        places.append((5, 6 * wide + 4 * units + mine * width, width))
+        for row, start, count in places:
+            for k in range(count):
+                norms[row : row + 1, k * lanes : (k + 1) * lanes] = vectors[pl.ds(start + k, 1), :]
+        for k in range(wide):
+            both = vectors[pl.ds(4 * wide + k, 1), :] + vectors[pl.ds(5 * wide + k, 1), :]
+            norms[6:7, k * lanes : (k + 1) * lanes] = both
+
     def block(w, dim, d):
         size = w.shape[dim] // 4
         cut = pl.ds(feature_of(d) * size, size)
@@ -371,6 +390,7 @@
 
     def send_flag():
         cols[...] = jnp.zeros_like(cols)
+        flag[...] = jnp.full(flag.shape, ids[ids.shape[0] - 1], jnp.int32).astype(F32)
         kept.append(copies.local(flag, flags.at[0]))
         state["flags"] = [copies.remote(flag, flags.at[k], (me ^ d, core)) for k, d in ((1, 1), (2, 4), (3, 5))]
 
@@ -483,15 +503,18 @@
                 hid[r, c] = (v * cdf).astype(BF16)
                 gf[r, c] = (cdf + v * density).astype(BF16)
 
+    def group_tiles(own, gathered, target):
+        after = pl.ds(2 * TILE, 6 * TILE)
+        return [
+            (own, tile_at(target, 0, core)),
+            (tile_at(gathered, 0, 1 - core), tile_at(target, 0, 1 - core)),
+            (gathered.at[after, :], target.at[after, :]),
+        ]
+
     def load_cotangent():
         for k in range(4):
             state["cp%d" % k].wait_recv()
-        pairs = [
-            (c_ref, tile_at(big2, 0, core)),
-            (tile_at(cg, 0, 1 - core), tile_at(big2, 0, 1 - core)),
-            (cg.at[pl.ds(2 * TILE, 6 * TILE), :], big2.at[pl.ds(2 * TILE, 6 * TILE), :]),
-        ]
-        copies.now(*pairs)
+        copies.now(*group_tiles(c_ref, cg, big2))
 
         @pl.loop(0, TILE // 32)
         def _(k):
@@ -608,17 +631,32 @@
         return q, k, v, w / jnp.sum(w, axis=-1, keepdims=True)
 
     def attend(lo, hi):
+        spare = copies.locals
+        copies.locals += 4
+
+        def load(number, h):
+            at = 2 * (number & 1) + h
+            source = na.at[group_rows(number, h * half, half), :]
+            return pltpu.make_async_copy(source, xt.at[at], local_sems.at[spare + at])
+
+        for h in (0, 1):
+            load(lo, h).start()
+
         @pl.loop(lo, hi)
         def _(number):
+            @pl.when(number + 1 < hi)
+            def _():
+                for h in (0, 1):
+                    load(number + 1, h).start()
+
             tables = group_tables(number)
             for h in (0, 1):
-                copies.now((na.at[group_rows(number, h * half, half), :], xt.at[h]))
-            for h in (0, 1):
+                load(number, h).wait()
                 r = group_rows(number, h * half, half)
                 here = [t[h * half : (h + 1) * half] for t in tables]
                 for k in range(3):
                     at = slice(k * HEAD_DIM, (k + 1) * HEAD_DIM)
-                    full = mm(xt[h], wqv[:, at], NN) + norms[5:6, at]
+                    full = mm(xt[2 * (number & 1) + h], wqv[:, at], NN) + norms[5:6, at]
                     qkv[r, at] = (rope(full, here, 1.0) if k < 2 else full).astype(BF16)
             for i in (0, 1):
                 _, _, v, p = probabilities(number, i)
@@ -674,47 +712,61 @@
             return copies.at(over + k, part, xo.at[rows_at(k, TILE), :], (me ^ 1, core))
 
         spare = copies.locals
-        copies.locals += 3
-
-        def load(k, slot):
-            return pltpu.make_async_copy(
-                co.at[rows_at(k, TILE), :], xt.at[slot], local_sems.at[spare + slot]
-            )
+        copies.locals += 4
+
+        def load(k):
+            at = k & 1
+            return pltpu.make_async_copy(co.at[rows_at(k, TILE), :], xt.at[at], local_sems.at[spare + at])
 
         def store(k):
+            at = 2 + (k & 1)
             target = ob.at[rows_at(4 * received + k, TILE), :]
-            return pltpu.make_async_copy(xt.at[1], target, local_sems.at[spare + 2])
+            return pltpu.make_async_copy(xt.at[at], target, local_sems.at[spare + at])
+
+        def send(k):
+            store(k).wait()
+            if received:
+
+                @pl.when(k < 2)
+                def _():
+                    to_x(k).start()
+
+            else:
+                to_core(k).start()
 
         if received:
             for k in range(4):
                 to_core(k).wait_recv()
+            for k in range(2):
+                load(k).start()
 
         @pl.loop(0, 4)
         def _(k):
             r = rows_at(rel_of(k) * 2 + (core if received else 1 - core), TILE)
             if received:
-                load(k, 0).start()
-                load(k, 0).wait()
-
-            @pl.loop(0, d_model // 512)
-            def _(j):
-                c = rows_at(j, 512)
-                total = mm(att[r, :], wdv[:, c], NN) + mm(hid[r, :], wb[:, c], NN)
-                if received:
-                    total = total + xt[0, :, c].astype(F32)
-                xt[1, :, c] = total.astype(BF16)
+                load(k).wait()
+
+            @pl.loop(0, d_model // 1024)
+            def _(jj):
+                for j in range(2):
+                    c = rows_at(2 * jj + j, 512)
+                    total = mm(att[r, :], wdv[:, c], NN) + mm(hid[r, :], wb[:, c], NN)
+                    if received:
+                        total = total + xt[k & 1, :, c].astype(F32)
+                    xt[2 + (k & 1), :, c] = total.astype(BF16)
 
             store(k).start()
-            store(k).wait()
             if received:
 
                 @pl.when(k < 2)
                 def _():
-                    to_x(k).start()
-
-            else:
-                to_core(k).start()
-
+                    load(k + 2).start()
+
+            @pl.when(k > 0)
+            def _():
+                send(k - 1)
+
+        send(3)
         if received:
             state["ox"] = [to_x(k) for k in range(2)]
             copies.open.extend(state["ox"])
@@ -747,54 +799,47 @@
         spare = copies.locals
         copies.locals += 2
 
-        def load(source, slot):
-            return pltpu.make_async_copy(source, xt.at[slot], local_sems.at[spare + slot])
+        def load(k):
+            at = k & 1
+            return pltpu.make_async_copy(ci.at[rows_at(k, TILE), :], xt.at[at], local_sems.at[spare + at])
 
         if received:
             for k in range(4):
                 to_core(k).wait_recv()
+            for k in range(2):
+                load(k).start()
         else:
             sums[0:4] = jnp.zeros_like(sums[0:4])
+            for copy in state["X"]:
+                copy.wait()
 
         @pl.loop(0, 4)
         def _(k):
-            tile = rel_of(k) * 2 + (core if received else 1 - core)
-            r = rows_at(tile, TILE)
+            r = rows_at(rel_of(k) * 2 + (core if received else 1 - core), TILE)
             if received:
-                load(ci.at[rows_at(k, TILE), :], 1).start()
-
-                @pl.when(k < 3)
-                def _():
-                    load(xg.at[r, :], 0).start()
-
-                @pl.when(k == 3)
-                def _():
-                    load(x_ref, 0).start()
-
-                load(x_ref, 1).wait()
-            else:
-                load(xg.at[r, :], 0).start()
-            load(x_ref, 0).wait()
-
-            @pl.loop(0, d_model // 512)
-            def _(j):
-                c = rows_at(j, 512)
-                a = mm(qkv[r, :], wqv[c, :], NT)
-                f = mm(gf[r, :], wa[c, :], NT)
-                xhat = (xt[0, :, c].astype(F32) - stats[r, 0:1]) * stats[r, 1:2]
-                sums[0, :, c] += fold(a * xhat)
-                sums[1, :, c] += fold(a)
-                sums[2, :, c] += fold(f * xhat)
-                sums[3, :, c] += fold(f)
-                total = a * norms[0:1, c] + f * norms[2:3, c]
-                if received:
-                    total = total + xt[1, :, c].astype(F32)
-                big2[rows_at(4 * received + k, TILE), c] = total.astype(BF16)
+                load(k).wait()
+
+            @pl.loop(0, d_model // 1024)
+            def _(jj):
+                for j in range(2):
+                    c = rows_at(2 * jj + j, 512)
+                    a = mm(qkv[r, :], wqv[c, :], NT)
+                    f = mm(gf[r, :], wa[c, :], NT)
+                    xhat = (big1[r, c].astype(F32) - stats[r, 0:1]) * stats[r, 1:2]
+                    sums[0, :, c] += fold(a * xhat)
+                    sums[1, :, c] += fold(a)
+                    sums[2, :, c] += fold(f * xhat)
+                    sums[3, :, c] += fold(f)
+                    total = a * norms[0:1, c] + f * norms[2:3, c]
+                    if received:
+                        total = total + xt[k & 1, :, c].astype(F32)
+                    big2[rows_at(4 * received + k, TILE), c] = total.astype(BF16)
 
             if received:
 
                 @pl.when(k < 2)
                 def _():
+                    load(k + 2).start()
                     to_x(k).start()
 
             else:
@@ -850,6 +895,7 @@
         kind, rest = op[0], op[1:]
         if kind == "g":
             send_flag()
+            spread()
         elif kind in "xc":
             token_step(kind, rest)
         elif kind == "s":
@@ -884,6 +930,8 @@
             attend_back(*{"0": (0, 2), "2": (2, 4)}.get(rest, (0, 4)))
         elif kind == "N":
             copies.now((na, big1))
+        elif kind == "X":
+            state["X"] = [copies.local(*pair) for pair in group_tiles(x_ref, xg, big1)]
         elif kind == "o":
             if rest in "01":
                 out_sum(int(rest))
@@ -920,7 +968,7 @@
     return tables
 
 
-def layer_call(x, c, w1, w2, wq, wd, flag, norms, turns):
+def layer_call(x, c, w1, w2, wq, wd, ids, turns, *parts):
     n = lax.axis_size("dp")
     tok, d = x.shape
     rows, u1, uq, ud = w1.shape[0], w1.shape[1] // 4, wq.shape[1] // 4, wd.shape[0] // 4
@@ -932,21 +980,21 @@
         return jax.ShapeDtypeStruct(shape, BF16)
 
     results = [low(rows, 4 * u1), low(4 * u1, rows), low(rows, 4 * uq), low(4 * ud, rows)]
-    results += [low(tok, d)] * 4 + [jax.ShapeDtypeStruct((16, d), F32)]
+    results += [low(tok, d)] * 4 + [jax.ShapeDtypeStruct((16, d), F32), jax.ShapeDtypeStruct((8, d), F32)]
     spare = [low(many, d)] * 2 + [low(d, u1), low(u1, d), low(d, uq), low(ud, d), low(many, d)]
     for part in (2, 4):
         spare += [low(d // part, u1), low(u1, d // part), low(d // part, uq), low(ud, d // part)]
     spare += [low(4 * tok, d)] * 2 + [low(2 * tok, d)] * 2 + [low(many, d)] + [jax.ShapeDtypeStruct((4, 8, 128), F32)]
     scratch = [
         (many, d), (many, d), (d, u1), (u1, d), (d, uq), (ud, d), (many, u1), (many, u1), (many, uq), (many, ud),
-        (d, u1), (u1, d), (d, uq), (ud, d), (2, tok, d), (u1, 2 * rows),
+        (d, u1), (u1, d), (d, uq), (ud, d), (4, tok, d), (u1, 2 * rows),
     ]
     flops = 2 * 3 * many * d * (2 * u1 + uq + ud)
     return pl.pallas_call(
         layer_kernel,
         out_shape=results + spare,
-        in_specs=[hbm] * 7 + [vmem] * 2,
-        out_specs=[hbm] * 8 + [vmem] + [hbm] * len(spare),
+        in_specs=[hbm] * 6 + [pl.BlockSpec(memory_space=pltpu.SMEM)] + [vmem] * (1 + len(parts)),
+        out_specs=[hbm] * 8 + [vmem] * 2 + [hbm] * len(spare),
         scratch_shapes=[pltpu.VMEM(s, BF16) for s in scratch]
         + [
             pltpu.VMEM((many, 2), F32),
@@ -957,6 +1005,8 @@
             pltpu.VMEM((16, d // n), F32),
             pltpu.VMEM((16, d // n), F32),
             pltpu.VMEM((4, 8, 128), F32),
+            pltpu.VMEM((8, 128), F32),
+            pltpu.VMEM((sum(p.shape[0] for p in parts), 128), F32),
             pltpu.SemaphoreType.DMA((128,)),
             pltpu.SemaphoreType.DMA((176,)),
             pltpu.SemaphoreType.DMA((176,)),
@@ -966,7 +1016,67 @@
         ),
         cost_estimate=pl.CostEstimate(flops=flops, bytes_accessed=200 << 20, transcendentals=0),
         name="layer",
-    )(x, c, w1, w2, wq, wd, flag, norms, turns)[:9]
+    )(x, c, w1, w2, wq, wd, ids, turns, *parts)[:10]
+
+
+def finish_kernel(
+    x, c, out_keep, out_got, in_keep, in_got, norms, vec, f1, f2, fq, fd,
+    layer_output, input_grad, o1, o2, oq, od, v0, v1, v2, v3, v4, v5, bias_1, bias_q,
+):
+    own = x[...].astype(F32)
+    branch = out_keep[...].astype(F32) + out_got[...].astype(F32)
+    layer_output[...] = (own + branch + norms[6:7, :]).astype(BF16)
+    center = own - jnp.mean(own, axis=-1, keepdims=True)
+    scale = lax.rsqrt(jnp.mean(center * center, axis=-1, keepdims=True) + 1e-05)
+    xhat = center * scale
+    e = in_keep[...].astype(F32) + in_got[...].astype(F32)
+    input_grad[...] = c[...].astype(F32) + scale * (
+        e - jnp.mean(e, axis=-1, keepdims=True) - xhat * jnp.mean(e * xhat, axis=-1, keepdims=True)
+    )
+    for source, target in ((f1, o1), (f2, o2), (fq, oq), (fd, od)):
+        target[...] = source[...].astype(F32)
+
+    @pl.when(pl.program_id(0) == 0)
+    def _():
+        for target, row in ((v0, 0), (v1, 1), (v2, 2), (v3, 3), (v4, 4), (v5, 4)):
+            for k in range(target.shape[0]):
+                target[k : k + 1, :] = vec[row : row + 1, k * 128 : (k + 1) * 128]
+        width = bias_q.shape[0] // 4
+        for target, first in ((bias_q, 0), (bias_1, width)):
+            count = target.shape[0] // 4
+            for block in range(4):
+                for k in range(count):
+                    at = (first + k) * 128
+                    target[block * count + k : block * count + k + 1, :] = vec[8 + block : 9 + block, at : at + 128]
+
+
+def finish_call(x, c, out_keep, out_got, in_keep, in_got, norms, vec, f1, f2, fq, fd, units, width):
+    steps = 8
+
+    def rows_of(v):
+        return pl.BlockSpec((v.shape[0] // steps, v.shape[1]), lambda i: (i, 0))
+
+    tokens = [x, c, out_keep, out_got, in_keep, in_got]
+    sums = [f1, f2, fq, fd]
+    outs = [jax.ShapeDtypeStruct(x.shape, BF16)]
+    outs += [jax.ShapeDtypeStruct(v.shape, F32) for v in [x] + sums]
+    rows = [x.shape[1] // 128] * 6 + [4 * units // 128, 4 * width // 128]
+    vectors = [jax.ShapeDtypeStruct((count, 128), F32) for count in rows]
+
+    def whole(v):
+        return pl.BlockSpec(v.shape, lambda i: (0, 0))
+
+    return pl.pallas_call(
+        finish_kernel,
+        grid=(steps,),
+        out_shape=outs + vectors,
+        in_specs=[rows_of(v) for v in tokens]
+        + [whole(norms), whole(vec)]
+        + [rows_of(v) for v in sums],
+        out_specs=[rows_of(v) for v in outs] + [whole(v) for v in vectors],
+        compiler_params=pltpu.CompilerParams(vmem_limit_bytes=64000 << 10),
+        name="finish",
+    )(*tokens, norms, vec, *sums)
 
 
 def local_fast(
@@ -986,65 +1096,38 @@
     seq_ids,
     cotangent,
 ):
-    me, core = place()
-    rows_here, d_model = layer_input.shape
-    feature = feature_of(me)
     units, width = fc1_weight.shape[1] // 4, 3 * HEAD_DIM
-
-    def take_block(v, size):
-        return jnp.pad(lax.dynamic_slice_in_dim(v, feature * size, size, 0), (0, d_model - size))
-
-    zero = jnp.zeros_like(ln1_gain)
-    norms = jnp.stack(
-        [ln1_gain, ln1_bias, ln2_gain, ln2_bias, take_block(fc1_bias, units), take_block(qkv_bias, width), zero, zero]
-    ).astype(F32)
-    flag = jnp.broadcast_to(jnp.max(seq_ids) > 0, (8, 128)).astype(F32)
-    f1, f2, fq, fd, out_keep, out_got, in_keep, in_got, vec = layer_call(
+    parts = (ln1_gain, ln1_bias, ln2_gain, ln2_bias, dense_bias, fc2_bias, fc1_bias, qkv_bias)
+    f1, f2, fq, fd, out_keep, out_got, in_keep, in_got, vec, norms = layer_call(
         layer_input,
         cotangent,
         fc1_weight,
         fc2_weight,
         qkv_weight,
         dense_weight,
-        flag,
-        norms,
+        seq_ids,
         turn_tables(seq_ids.shape[0]),
+        *(v.reshape(-1, 128) for v in parts),
     )
-    out_fc1, out_fc2, out_qkv, out_dense = (v.astype(F32) for v in (f1, f2, fq, fd))
-    own = layer_input.astype(F32)
-    layer_output = (
-        own
-        + (out_keep.astype(F32) + out_got.astype(F32))
-        + dense_bias.astype(F32)
-        + fc2_bias.astype(F32)
-    ).astype(BF16)
-    center = own - jnp.mean(own, axis=-1, keepdims=True)
-    scale = lax.rsqrt(jnp.mean(center * center, axis=-1, keepdims=True) + 1e-05)
-    xhat = center * scale
-    e_rows = in_keep.astype(F32) + in_got.astype(F32)
-    input_grad = cotangent.astype(F32) + scale * (
-        e_rows
-        - jnp.mean(e_rows, axis=-1, keepdims=True)
-        - xhat * jnp.mean(e_rows * xhat, axis=-1, keepdims=True)
+    layer_output, input_grad, out_fc1, out_fc2, out_qkv, out_dense, *rest = finish_call(
+        layer_input, cotangent, out_keep, out_got, in_keep, in_got, norms, vec, f1, f2, fq, fd, units, width
     )
-    blocks = vec[8:12]
-    out_qkv_bias = blocks[:, :width].reshape(-1)
-    out_fc1_bias = blocks[:, width : width + units].reshape(-1)
+    gain_1, shift_1, gain_2, shift_2, bias_d, bias_2, bias_1, bias_q = (v.reshape(-1) for v in rest)
     return (
         layer_output,
         input_grad,
-        vec[0],
-        vec[1],
-        vec[2],
-        vec[3],
+        gain_1,
+        shift_1,
+        gain_2,
+        shift_2,
         out_qkv,
-        out_qkv_bias,
+        bias_q,
         out_dense,
-        vec[4],
+        bias_d,
         out_fc1,
-        out_fc1_bias,
+        bias_1,
         out_fc2,
-        vec[4],
+        bias_2,
     )
 
 

time: 444 us -> 402 us (0.905)
  other arithmetic: 16.9 us -> 0 us
  Pallas kernels: 415 us -> 399 us
  local copies, waits for them, and re-layouts: 7.48 us -> 0 us
    pallas_call x1, Pallas kernels: 415 us -> 388 us  [layer_call(): pl.pallas_call(layer_kernel, out_shape=results + spare, in_specs=[hbm] *...]
    pallas_call x0 -> x1, Pallas kernels: none -> 11.5 us  [finish_call(): pl.pallas_call(finish_kernel, grid=(steps,), out_shape=outs + vectors, in...]
    convert_element_type x7 -> x0, other arithmetic: 5.75 us -> none  [the longest x4 5.11 us: local_fast(): v.astype(F32)]
    reduce_sum x3 -> x0, other arithmetic: 5.33 us -> none  [the longest x1 1.95 us: local_fast(): jnp.mean(e_rows, axis=-1, keepdims=True)]
    add x1 -> x0, other arithmetic: 4.49 us -> none  [local_fast(): cotangent.astype(F32)]
where the time goes in v5:
time: 402 us; the launch traced here: 400 us
  Pallas kernels  399 us (99%)
    pallas_call x1, Pallas kernels, layer_call(): pl.pallas_call(layer_kernel, out_shape=results + spare, in_specs=[hbm] *...  388 us
    pallas_call x1, Pallas kernels, finish_call(): pl.pallas_call(finish_kernel, grid=(steps,), out_shape=outs + vectors, in...  11.5 us

profile of v5, /device:TPU:0, one launch (start us, length us, event | category | flops | bytes accessed | tf_op | source)
XLA Modules:
  0.0 399.9 jit_solution(9700683527385401622)
XLA Ops:
  0.7 387.6 %layer.1 = (bf16[128,4096]{1,0:T(8,128)(2,1)}, bf16[4096,128]{1,0:T(8,128)(2,1)}, bf16[128,3072]{1,0:T(8,128)(2,1)}, bf16[1024,128]{1,0:T(8,128)(2,1)}, bf16[256...) custom-call(bf16[256,2048]{1,0:T(8,128)(2,1)} %x.1, ...), custom_call_target="tpu_custom_call" | custom-call | flops 77309411328 | bytes 209715200 | tf_op jit(solution)/shard_map/layer/pallas_call | solution.py:993
  388.3 11.5 %finish.1 = (bf16[256,2048]{1,0:T(8,128)(2,1)}, f32[256,2048]{1,0:T(8,128)}, f32[128,4096]{1,0:T(8,128)}, f32[4096,128]{1,0:T(8,128)}, f32[128,3072]{1,0:T(8,128...) custom-call(bf16[256,2048]{1,0:T(8,128)(2,1)} %x.1, ...), custom_call_target="tpu_custom_call" | custom-call | tf_op jit(solution)/shard_map/finish/pallas_call | solution.py:1069

commit v6 on v5

--- a/solution.py
+++ b/solution.py
@@ -264,11 +264,11 @@
 
 TILE = 256
 ORDER = """
-g0 sq5 sq13 sd13 sd1 sd5 s18 sq9 x0 s15 sq8 sd9 sd0 s113 fq13 sq4 fd1 f18 s112 s20 s10 s19 sq12 fq5 sd8 s11
-sq1 x1 s25 s21 sd4 c0 s14 f15 sq0 fq1 s29 f11 f113 fq4 s212 fq8 sd12 x2 s28 f19 s213 x3 fq12 fq9 L fd9 fd8 s24
-f112 f21 f14 f212 c1 Wq fd5 fd13 f25 A W1 f24 fd12 f29 c2 P f28 fd4 c3 f213 C G2 W2 Wd r23 o0 H r22 r21 t21 G1
-o1 r13 B N r20 r12 oa Gd Gq X i0 t20 r11 rd2 rq3 t11 i1 rq1 rq2 tq1 rd3 v0 rq0 rd0 ia rd1 tq0 r10 t10 v1 v2
-td1 td0 ib ob
+g0 sq1 sd5 sd1 sq9 sq0 s14 s11 sd4 s112 s113 x0 sq4 sd9 fd1 sq12 sd12 s19 sq13 sq8 s15 f11 s20 s21 s10 sd0 s18
+sd8 fd4 f14 f113 x1 f112 sd13 fd9 x2 fq13 f21 fq12 sq5 c0 fq8 s212 fq4 fq1 fd8 s29 x3 fq9 fq5 fd13 L f19 s28
+f18 Wq c1 f15 fd5 fd12 s24 A s213 c2 s25 f212 f24 f29 W1 P f28 c3 Wd f25 C f213 G2 W2 o0 r23 H o1 r22 Gd G1
+rd3 oa N B r21 r13 t21 Gq X i0 r11 rd1 r12 t11 i1 rq2 td1 r20 v0 rd2 rd0 rq3 ia rq1 r10 t20 td0 rq0 ib tq0 v1
+ob v2 tq1 t10
 """
 
 
@@ -1051,7 +1051,7 @@
 
 
 def finish_call(x, c, out_keep, out_got, in_keep, in_got, norms, vec, f1, f2, fq, fd, units, width):
-    steps = 8
+    steps = 4
 
     def rows_of(v):
         return pl.BlockSpec((v.shape[0] // steps, v.shape[1]), lambda i: (i, 0))

time: 402 us -> 393 us (0.978)
  Pallas kernels: 399 us -> 391 us
    pallas_call x1, Pallas kernels: 388 us -> 381 us  [layer_call(): pl.pallas_call(layer_kernel, out_shape=results + spare, in_specs=[hbm] *...]
where the time goes in v6:
time: 393 us; the launch traced here: 391 us
  Pallas kernels  391 us (99%)
    pallas_call x1, Pallas kernels, layer_call(): pl.pallas_call(layer_kernel, out_shape=results + spare, in_specs=[hbm] *...  381 us
    pallas_call x1, Pallas kernels, finish_call(): pl.pallas_call(finish_kernel, grid=(steps,), out_shape=outs + vectors, in...  9.12 us

profile of v6, /device:TPU:0, one launch (start us, length us, event | category | flops | bytes accessed | tf_op | source)
XLA Modules:
  0.0 391.4 jit_solution(15862472804885244910)
XLA Ops:
  0.7 381.5 %layer.1 = (bf16[128,4096]{1,0:T(8,128)(2,1)}, bf16[4096,128]{1,0:T(8,128)(2,1)}, bf16[128,3072]{1,0:T(8,128)(2,1)}, bf16[1024,128]{1,0:T(8,128)(2,1)}, bf16[256...) custom-call(bf16[256,2048]{1,0:T(8,128)(2,1)} %x.1, ...), custom_call_target="tpu_custom_call" | custom-call | flops 77309411328 | bytes 209715200 | tf_op jit(solution)/shard_map/layer/pallas_call | solution.py:993
  382.1 9.1 %finish.1 = (bf16[256,2048]{1,0:T(8,128)(2,1)}, f32[256,2048]{1,0:T(8,128)}, f32[128,4096]{1,0:T(8,128)}, f32[4096,128]{1,0:T(8,128)}, f32[128,3072]{1,0:T(8,128...) custom-call(bf16[256,2048]{1,0:T(8,128)(2,1)} %x.1, ...), custom_call_target="tpu_custom_call" | custom-call | tf_op jit(solution)/shard_map/finish/pallas_call | solution.py:1069
